TPU v7x, 512 devices: a whole 4x4x16 slice. The times are simulated.
512 devices in a mesh: group: 16 (over z_hi, y), tensor: 32 (over x, z_lo, core).
Axes of the slice: x: 4, y: 4, z: 16 (z_hi: 4, z_lo: 4; z = z_hi * 4 + z_lo), core: 2. Of those that a mesh axis runs over, the one named last changes fastest.
Arguments:
- step_inputs: bfloat16 [4, 512, 4096], P(None, 'group', 'tensor'), may hold values from -6 to 6
- qkv_weight: bfloat16 [4096, 3, 4096], P(None, None, 'tensor'), may hold values from -0.09375 to 0.09375
- out_weight: bfloat16 [4096, 4096], P('tensor'), may hold values from -0.09375 to 0.09375
- head_gain: float32 [4096], P('tensor'), may hold values from 0.1 to 1.9
- head_decay: float32 [32], P('tensor'), may hold values from 0.3 to 0.98
- states_in: float32 [512, 32, 128, 128], P('group', 'tensor'), may hold values from -3 to 3
- remaining_steps: int32 [512], replicated, may hold values from 0 to 8, as said below
- migration_plan: int32 [512], replicated, may hold values from 0 to 511, as said below
Outputs:
- step_outputs: bfloat16 [4, 512, 4096], P(None, 'group', 'tensor')
Inputs may be any that keep to these rules, and one draw needn't show every extreme that they name: A permutation: row j after the move holds the sequence that row migration_plan[j] held. In each group exactly 13 rows receive a sequence from another group and exactly 13 rows send one to another group, at most 2 between any two groups, and 2 from one of them; all other rows keep their own sequence. `remaining_steps`: A sequence that the plan moves to another group has 4 or more steps left.
All inputs are finite; a program needn't handle non-finite values.
Results may differ from a plain program's by a relative error of at most 0.0065.
Values may be sent and summed in bfloat16 or wider, within the bound.
No kernel may reach another device: no remote copies, remote signals or barrier semaphores. Data moves between devices by JAX's collectives and lax.ppermute only.
A program may use at most 128 MiB of HBM per device.

v0:
```python
import jax
import jax.numpy as jnp
from jax import lax
from jax.sharding import PartitionSpec as P

STEPS = 4


def advance(
    states, features, steps_left, step_index, proj_weight, decay_rates, gain_rows, out_weight
):
    row_count = states.shape[0]
    local_heads = states.shape[1]
    head_size = states.shape[2]
    projected = jnp.dot(features, proj_weight, preferred_element_type=jnp.float32)
    projected = projected.reshape(row_count, 3, local_heads, head_size)
    query_vec = jax.nn.silu(projected[:, 0])
    key_vec = jax.nn.silu(projected[:, 1])
    value_vec = projected[:, 2]
    active = steps_left > step_index
    updated = (
        decay_rates[None, :, None, None] * states
        + key_vec[:, :, :, None] * value_vec[:, :, None, :]
    )
    states = jnp.where(active[:, None, None, None], updated, states)
    readout = jnp.einsum("bhd,bhde->bhe", query_vec, states, precision=lax.Precision.HIGHEST)
    scale_inv = lax.rsqrt(jnp.mean(readout * readout, axis=-1, keepdims=True) + 1e-05)
    normed = readout * scale_inv * gain_rows[None]
    normed = jnp.where(active[:, None, None], normed, jnp.zeros_like(normed))
    normed = normed.astype(jnp.bfloat16).reshape(row_count, local_heads * head_size)
    partial_value = jnp.dot(normed, out_weight, preferred_element_type=jnp.float32)
    return (states, partial_value)


def body(
    step_inputs,
    qkv_weight,
    out_weight,
    head_gain,
    head_decay,
    states_in,
    remaining_steps,
    migration_plan,
):
    batch_rows = states_in.shape[0]
    local_heads = states_in.shape[1]
    head_size = states_in.shape[2]
    groups = lax.axis_size("group")
    move_count = (4 * groups + 4) // 5
    own_group = lax.axis_index("group")
    own_plan = lax.dynamic_slice_in_dim(migration_plan, own_group * batch_rows, batch_rows)
    source_group = own_plan // batch_rows
    source_slot = own_plan % batch_rows
    incoming = source_group != own_group
    kept_states = jnp.take(states_in, source_slot, axis=0)
    all_rows = jnp.arange(groups * batch_rows)
    leaving = (migration_plan // batch_rows == own_group) & (all_rows // batch_rows != own_group)
    order_out = jnp.cumsum(leaving.astype(jnp.int32)) - 1
    slot_ids = jnp.arange(move_count)
    slot_hits = leaving[None, :] & (order_out[None, :] == slot_ids[:, None])
    chosen = jnp.sum(jnp.where(slot_hits, (migration_plan % batch_rows)[None, :], 0), axis=1)
    outgoing = jnp.take(states_in, chosen, axis=0)
    own_rows = own_group * batch_rows + jnp.arange(batch_rows)
    before = all_rows[None, :] < own_rows[:, None]
    leaves_source = (migration_plan[None, :] // batch_rows == source_group[:, None]) & (
        all_rows[None, :] // batch_rows != source_group[:, None]
    )
    arrival = jnp.sum((before & leaves_source).astype(jnp.int32), axis=1)
    arrival_index = source_group * move_count + arrival
    shard_rows = lax.all_gather(outgoing.astype(jnp.bfloat16), "group", axis=0, tiled=True).astype(
        jnp.float32
    )
    count_rows = shard_rows.shape[0]
    inside = incoming & (arrival_index >= 0) & (arrival_index < count_rows)
    picked = jnp.take(shard_rows, jnp.clip(arrival_index, 0, count_rows - 1), axis=0)
    states = jnp.where(inside[:, None, None, None], picked, kept_states)
    steps_left = jnp.take(remaining_steps, own_plan, axis=0)
    proj_weight = qkv_weight.reshape(qkv_weight.shape[0], 3 * local_heads * head_size)
    gain_rows = head_gain.reshape(local_heads, head_size)
    outputs = []
    for step_index in range(STEPS):
        features = lax.all_gather(step_inputs[step_index], "tensor", axis=1, tiled=True)
        states, partial_value = advance(
            states, features, steps_left, step_index, proj_weight, head_decay, gain_rows, out_weight
        )
        outputs.append(
            lax.psum_scatter(partial_value, "tensor", scatter_dimension=1, tiled=True).astype(
                jnp.bfloat16
            )
        )
    return jnp.stack(outputs)


def solution(mesh):
    placed = (
        P(None, "group", "tensor"),
        P(None, None, "tensor"),
        P("tensor", None),
        P("tensor"),
        P("tensor"),
        P("group", "tensor", None, None),
        P(),
        P(),
    )
    return jax.shard_map(
        body, mesh=mesh, in_specs=placed, out_specs=P(None, "group", "tensor"), check_vma=False
    )
```

profile of v0, /device:TPU:24, one launch (start us, length us, event | category | flops | bytes accessed | tf_op | source)
XLA Modules:
  0.0 888.1 jit_solution(7645875741480741204)
XLA Ops:
  6.5 0.8 add_select_fusion.6
  7.4 0.7 convert_bitcast_fusion.4
  8.1 0.3 reduce-window.9
  8.4 0.1 slice.57
  8.5 0.1 slice_reduce_fusion
  8.7 0.1 select_reduce_fusion
  8.9 0.6 gather_fusion.1
  9.5 0.9 fusion.45
  10.5 0.1 compare_and_fusion
  10.6 2.0 gather_fusion.3
  12.6 4.7 copy.14
  18.0 0.1 compare_select_fusion.7
  18.1 0.7 gather_fusion
  18.8 0.2 convert_reduce_fusion
  19.0 56.8 %all-gather = bf16[1,32,4096]{2,1,0:T(8,128)(2,1)S(1)} all-gather(bf16[1,32,128]{2,1,0:T(8,128)(2,1)S(1)} %get-tuple-element.22), channel_id=2, replica_groups=mesh['group'=16,'tensor'=32] {'tensor'}, dimensions={2}, use_global_device_ids=true | all-gather | bytes 270336 | tf_op jit(solution)/shard_map/all_gather | solution.py:82
  75.9 58.6 %all-gather.1 = bf16[1,32,4096]{2,1,0:T(8,128)(2,1)S(1)} all-gather(bf16[1,32,128]{2,1,0:T(8,128)(2,1)S(1)} %get-tuple-element.21), channel_id=3, replica_groups=mesh['group'=16,'tensor'=32] {'tensor'}, dimensions={2}, use_global_device_ids=true | all-gather | bytes 270336 | tf_op jit(solution)/shard_map/all_gather | solution.py:82
  134.5 51.7 %all-gather.2 = bf16[1,32,4096]{2,1,0:T(8,128)(2,1)S(1)} all-gather(bf16[1,32,128]{2,1,0:T(8,128)(2,1)S(1)} %get-tuple-element.24), channel_id=4, replica_groups=mesh['group'=16,'tensor'=32] {'tensor'}, dimensions={2}, use_global_device_ids=true | all-gather | bytes 270336 | tf_op jit(solution)/shard_map/all_gather | solution.py:82
  186.2 54.4 %all-gather.3 = bf16[1,32,4096]{2,1,0:T(8,128)(2,1)S(1)} all-gather(bf16[1,32,128]{2,1,0:T(8,128)(2,1)S(1)} %get-tuple-element.23), channel_id=5, replica_groups=mesh['group'=16,'tensor'=32] {'tensor'}, dimensions={2}, use_global_device_ids=true | all-gather | bytes 270336 | tf_op jit(solution)/shard_map/all_gather | solution.py:82
  240.6 2.9 fusion.6
  243.6 1.0 fusion.14
  244.7 1.0 fusion.17
  245.7 1.0 fusion.20
  246.8 9.5 %bitcast_convert_fusion = f32[208,128,128]{2,1,0:T(8,128)} fusion(bf16[208,1,128,128]{3,2,1,0:T(8,128)(2,1)} %all-gather.6.cloned.1.call-done), kind=kLoop, calls=%fused_computation.4 | loop fusion | flops 3407872 | bytes 20447232 | tf_op jit(solution)/shard_map/convert_element_type | solution.py:70
  256.3 6.8 gather_fusion.2
  263.2 2.9 add_select_fusion.2
  266.1 1.3 copy-done.4
  267.4 1.9 fusion.82
  269.3 0.1 multiply_reduce_fusion.3
  269.4 1.1 fusion.52
  270.6 0.2 reduce-scatter.7.cloned.1.call-start
  270.8 3.7 fusion.13
  274.5 0.1 multiply_reduce_fusion.2
  274.6 1.2 fusion.53
  275.9 4.1 fusion.23
  280.0 0.1 multiply_reduce_fusion.1
  280.1 1.1 fusion.54
  281.3 4.7 fusion.8
  286.0 0.1 multiply_reduce_fusion
  286.2 1.1 fusion.55
  287.3 147.4 %reduce-scatter.5.cloned.1.call-done = f32[32,128]{1,0:T(8,128)} async-done(((f32[32,4096]{1,0:T(8,128)}), f32[32,128]{1,0:T(8,128)}) %reduce-scatter.5.cloned.1.call-update) | async-done | bytes 16400 | tf_op jit(solution)/shard_map/reduce_scatter | solution.py:87
  434.8 0.7 convert_bitcast_fusion.3
  435.5 147.9 %reduce-scatter.7.cloned.1.call-done = f32[32,128]{1,0:T(8,128)} async-done(((f32[32,4096]{1,0:T(8,128)}), f32[32,128]{1,0:T(8,128)}) %reduce-scatter.7.cloned.1.call-update) | async-done | bytes 16400 | tf_op jit(solution)/shard_map/reduce_scatter | solution.py:87
  583.4 0.7 convert_bitcast_fusion.2
  584.1 147.7 %reduce-scatter.9.cloned.1.call-done = f32[32,128]{1,0:T(8,128)} async-done(((f32[32,4096]{1,0:T(8,128)}), f32[32,128]{1,0:T(8,128)}) %reduce-scatter.9.cloned.1.call-update) | async-done | bytes 16400 | tf_op jit(solution)/shard_map/reduce_scatter | solution.py:87
  731.8 0.7 convert_bitcast_fusion.1
  732.5 147.7 %reduce-scatter.11.cloned.1.call-done = f32[32,128]{1,0:T(8,128)} async-done(((f32[32,4096]{1,0:T(8,128)}), f32[32,128]{1,0:T(8,128)}) %reduce-scatter.11.cloned.1.call-update) | async-done | bytes 16400 | tf_op jit(solution)/shard_map/reduce_scatter | solution.py:87
  880.2 0.7 convert_bitcast_fusion
  880.9 0.6 pad_maximum_fusion
  (51 shorter events, 0.6 us)
Async XLA Ops:
  6.5 2.3 copy-start
  6.5 3.9 copy-start.6
  6.5 240.3 %all-gather.6.cloned.1.call-start = ((), (), s32[]{:S(2)}) async-start(), calls=%async_computation.4 | async-start | bytes 7241728 | tf_op jit(solution)/shard_map/all_gather | solution.py:70
  10.4 424.3 %reduce-scatter.5.cloned.1.call-start = ((), (), s32[]{:S(2)}) async-start(), calls=%async_computation.5 | async-start | bytes 540672 | tf_op jit(solution)/shard_map/reduce_scatter | solution.py:87
  12.6 5.5 copy-start.1
  12.6 6.4 copy-start.5
  134.5 109.1 %copy-start.2 = (bf16[4096,3,128]{0,2,1:T(8,128)(2,1)S(1)}, bf16[4096,3,128]{0,2,1:T(8,128)(2,1)}, u32[]{:S(2)}) copy-start(bf16[4096,3,128]{0,2,1:T(8,128)(2,1)} %copy.14) | copy-start | bytes 9437188
  266.1 1.4 copy-start.4
  266.1 3.3 copy-start.3
  266.1 3.3 copy-start.7
  270.6 312.9 %reduce-scatter.7.cloned.1.call-start = ((), (), s32[]{:S(2)}) async-start(), calls=%async_computation.6 | async-start | bytes 540672 | tf_op jit(solution)/shard_map/reduce_scatter | solution.py:87
  275.8 456.0 %reduce-scatter.9.cloned.1.call-start = ((), (), s32[]{:S(2)}) async-start(), calls=%async_computation.7 | async-start | bytes 540672 | tf_op jit(solution)/shard_map/reduce_scatter | solution.py:87
  281.3 598.9 %reduce-scatter.11.cloned.1.call-start = ((), (), s32[]{:S(2)}) async-start(), calls=%async_computation.8 | async-start | bytes 540672 | tf_op jit(solution)/shard_map/reduce_scatter | solution.py:87
Sparse Core Ops, SparseCore 0:
  10.5 170.2 all-gather.5
  270.7 164.0 reduce-scatter.4
  437.8 145.6 reduce-scatter.6
  586.1 145.6 reduce-scatter.8
  734.7 145.5 reduce-scatter.10
where the time goes:
time: 889 us; the launch traced here: 888 us
  waiting for transfers between devices  591 us (66%)
  blocking collectives  222 us (25%)
  matrix products  24.9 us (3%)
  other arithmetic  19.9 us (2%)
  local copies, waits for them, and re-layouts  16.5 us (2%)
  between operations  14.1 us (2%)
    reduce_scatter x4, waiting for transfers between devices, body(): lax.psum_scatter(partial_value, 'tensor', scatter_dimension=1, tiled=True)  591 us
    all_gather x4, blocking collectives, body(): lax.all_gather(step_inputs[step_index], 'tensor', axis=1, tiled=True)  222 us
  transfers between devices with their start and end apart: 5, of which 4 were waited for; matrix products, arithmetic and copies ran while one was open for 4% of the time, Pallas kernels for 0%

commit v1 on v0

v1 whole, which is shorter than its diff:
```python
import jax
import jax.numpy as jnp
from jax import lax
from jax.sharding import PartitionSpec as P

STEPS = 4
XS, ZS, CORES = 4, 4, 2
SLOTS = 2


def tensor_id(x, z, c):
    return (x * ZS + z) * CORES + c


Z_LINES = [[tensor_id(x, z, c) for z in range(ZS)] for x in range(XS) for c in range(CORES)]
X_RINGS = [[tensor_id(x, z, c) for x in range(XS)] for z in range(ZS) for c in range(CORES)]
CORE_SWAP = [
    (tensor_id(x, z, c), tensor_id(x, z, 1 - c))
    for x in range(XS)
    for z in range(ZS)
    for c in range(CORES)
]


def ranks(same):
    rows = same.shape[-1]
    earlier = jnp.arange(rows)[None, :] < jnp.arange(rows)[:, None]
    return jnp.sum((same & earlier).astype(jnp.int32), axis=-1)


def move_states(states, migration_plan, own_group, groups):
    rows = states.shape[0]
    plan = migration_plan.reshape(groups, rows)
    source_group, source_slot = plan // rows, plan % rows
    from_here = source_group == own_group
    order = ranks(jnp.broadcast_to(from_here[:, None, :], (groups, rows, rows)))
    wanted = from_here[:, None, :] & (order[:, None, :] == jnp.arange(SLOTS)[None, :, None])
    chosen = jnp.sum(jnp.where(wanted, source_slot[:, None, :], 0), axis=-1)
    outgoing = jnp.take(states, chosen.reshape(-1), axis=0).astype(jnp.bfloat16)
    outgoing = outgoing.reshape(groups, SLOTS, *states.shape[1:])
    incoming = lax.all_to_all(outgoing, "group", 0, 0, tiled=True)
    return incoming.reshape(groups * SLOTS, *states.shape[1:])


def gather_features(own, core):
    line = lax.all_gather(own, "tensor", axis=0, axis_index_groups=Z_LINES)
    plane = lax.all_gather(line, "tensor", axis=0, axis_index_groups=X_RINGS)
    other = lax.ppermute(plane, "tensor", CORE_SWAP)
    even = jnp.where(core == 0, plane, other)
    odd = jnp.where(core == 0, other, plane)
    whole = jnp.stack([even, odd], axis=2)
    return jnp.transpose(whole, (3, 0, 1, 2, 4)).reshape(own.shape[0], -1)


def scatter_sums(normed, out_weight, core):
    rows, depth = normed.shape
    split = out_weight.reshape(depth, XS * ZS, CORES, -1)

    def part(which):
        weight = lax.dynamic_index_in_dim(split, which, axis=2, keepdims=False)
        value = jnp.einsum("rd,dpk->prk", normed, weight, preferred_element_type=jnp.float32)
        return value

    received = lax.ppermute(part(1 - core).astype(jnp.bfloat16), "tensor", CORE_SWAP)
    plane = (part(core) + received.astype(jnp.float32)).astype(jnp.bfloat16)
    plane = plane.reshape(XS, ZS, rows, -1)
    pieces = lax.all_to_all(plane, "tensor", 0, 0, tiled=True, axis_index_groups=X_RINGS)
    line = jnp.sum(pieces.astype(jnp.float32), axis=0).astype(jnp.bfloat16)
    pieces = lax.all_to_all(line, "tensor", 0, 0, tiled=True, axis_index_groups=Z_LINES)
    return jnp.sum(pieces.astype(jnp.float32), axis=0).astype(jnp.bfloat16)


def body(
    step_inputs,
    qkv_weight,
    out_weight,
    head_gain,
    head_decay,
    states_in,
    remaining_steps,
    migration_plan,
):
    rows = states_in.shape[0]
    size = states_in.shape[2]
    groups = lax.axis_size("group")
    own_group = lax.axis_index("group")
    core = lax.axis_index("tensor") % CORES
    states_in = states_in.reshape(rows, size, size)

    incoming = move_states(states_in, migration_plan, own_group, groups)
    own_plan = lax.dynamic_slice_in_dim(migration_plan, own_group * rows, rows)
    source_group, source_slot = own_plan // rows, own_plan % rows
    arrival = source_group * SLOTS + ranks(source_group[:, None] == source_group[None, :])
    steps_left = jnp.take(remaining_steps, own_plan, axis=0)

    features = gather_features(step_inputs.reshape(STEPS * rows, -1), core)
    projected = jnp.dot(
        features, qkv_weight.reshape(qkv_weight.shape[0], -1), preferred_element_type=jnp.float32
    ).reshape(STEPS, rows, 3, size)
    query = jax.nn.silu(projected[:, :, 0])
    key = jax.nn.silu(projected[:, :, 1])
    value = projected[:, :, 2]

    kept = jnp.take(states_in, source_slot, axis=0)
    moved = jnp.take(incoming, jnp.clip(arrival, 0, groups * SLOTS - 1), axis=0)
    states = jnp.where(
        (source_group != own_group)[:, None, None], moved.astype(jnp.float32), kept
    )

    decay = head_decay[0]
    from_states = jnp.einsum("trd,rde->tre", query, states, precision=lax.Precision.HIGHEST)
    outs = []
    power = decay
    for t in range(STEPS):
        readout = power * from_states[t]
        power = power * decay
        weight = jnp.ones((), jnp.float32)
        for s in range(t, -1, -1):
            score = jnp.sum(query[t] * key[s], axis=-1, keepdims=True)
            readout = readout + (weight * score) * value[s]
            weight = weight * decay
        scale = lax.rsqrt(jnp.mean(readout * readout, axis=-1, keepdims=True) + 1e-05)
        normed = readout * scale * head_gain[None]
        outs.append(jnp.where((steps_left > t)[:, None], normed, 0.0))
    normed = jnp.stack(outs).astype(jnp.bfloat16).reshape(STEPS * rows, size)
    result = scatter_sums(normed, out_weight, core)
    return result.reshape(STEPS, rows, size)


def solution(mesh):
    placed = (
        P(None, "group", "tensor"),
        P(None, None, "tensor"),
        P("tensor", None),
        P("tensor"),
        P("tensor"),
        P("group", "tensor", None, None),
        P(),
        P(),
    )
    return jax.shard_map(
        body, mesh=mesh, in_specs=placed, out_specs=P(None, "group", "tensor"), check_vma=False
    )
```

time: 889 us -> 158 us (0.18)
  the two profiles are of different devices: /device:TPU:24 before, /device:TPU:16 now
where the time goes in v1:
time: 158 us; the launch traced here: 157 us
  blocking collectives  91.6 us (58%)
  local copies, waits for them, and re-layouts  26.4 us (17%)
  starting transfers between devices  22.4 us (14%)
  matrix products  10 us (6%)
  other arithmetic  5.96 us (4%)
    all_gather x1, blocking collectives, gather_features(): line = lax.all_gather(own, 'tensor', axis=0, axis_index_groups=Z_LINES)  55.8 us
    all_to_all x1, starting transfers between devices, move_states(): incoming = lax.all_to_all(outgoing, 'group', 0, 0, tiled=True)  18.1 us
    all_gather x1, blocking collectives, gather_features(): plane = lax.all_gather(line, 'tensor', axis=0, axis_index_groups=X_RINGS)  14.4 us
    all_to_all x1, blocking collectives, scatter_sums(): lax.all_to_all(plane, 'tensor', 0, 0, tiled=True, axis_index_groups=X_RINGS)  13 us
    unnamed x15, local copies, waits for them, and re-layouts  10.1 us
    all_to_all x1, blocking collectives, scatter_sums(): lax.all_to_all(line, 'tensor', 0, 0, tiled=True, axis_index_groups=Z_LINES)  8.31 us
    dot_general x1, matrix products, body(): jnp.einsum('trd,rde->tre', query, states, precision=lax.Precision.HIGHEST)  4.19 us
    dynamic_slice x1, local copies, waits for them, and re-layouts, part(): weight = lax.dynamic_index_in_dim(split, which, axis=2, keepdims=False)  3.58 us
  transfers between devices with their start and end apart: 3, of which 0 were waited for; matrix products, arithmetic and copies ran while one was open for 17% of the time, Pallas kernels for 0%

profile of v1, /device:TPU:16, one launch (start us, length us, event | category | flops | bytes accessed | tf_op | source)
XLA Modules:
  0.0 157.4 jit_solution(6410316953880689334)
XLA Ops:
  0.0 0.0 copy-start
  0.0 0.9 reshape.586
  1.0 0.3 convert_reduce_fusion
  1.3 0.1 select_reduce_fusion
  1.4 0.1 copy.47
  1.5 0.1 reshape.587
  1.6 0.8 compare_select_fusion.1
  2.4 0.7 gather_fusion.2
  3.1 0.0 copy-start.4
  3.1 1.3 select_convert_fusion
  4.4 18.1 %all-to-all-start = ((bf16[16,2,128,128]{3,2,1,0:T(8,128)(2,1)}), bf16[16,2,128,128]{3,2,1,0:T(8,128)(2,1)}, u32[]{:S(2)}, u32[]{:S(2)}) async-start(bf16[16,2,128,128]{3,2,1,0:T(8,128)(2,1)} %bitcast.216), calls=%async_computation | async-start | bytes 2097152 | tf_op jit(solution)/shard_map/all_to_all | solution.py:41
  22.5 0.0 copy-done.4
  22.5 55.8 %all_gather.9 = bf16[4,128,128]{2,1,0:T(8,128)(2,1)S(1)} all-gather(bf16[1,128,128]{2,1,0:T(8,128)(2,1)S(1)} %bitcast.224), channel_id=1, replica_groups={{0,2,4,6},{1,3,5,7},{8,10,12,14},{9,11,13,15},{16,18,20,22},{17,19,21,2..., dimensions={0}, use_global_device_ids=true | all-gather | bytes 163840 | tf_op jit(solution)/shard_map/all_gather | solution.py:46
  78.3 14.4 %all-gather = bf16[16,128,128]{2,1,0:T(8,128)(2,1)} all-gather(bf16[4,128,128]{2,1,0:T(8,128)(2,1)S(1)} %all_gather.9), channel_id=2, replica_groups={{0,8,16,24},{1,9,17,25},{2,10,18,26},{3,11,19,27},{4,12,20,28},{5,13,21..., dimensions={0}, use_global_device_ids=true | all-gather | bytes 655360 | tf_op jit(solution)/shard_map/all_gather | solution.py:47
  92.7 1.9 %collective-permute-start = (bf16[4,4,128,128]{3,2,1,0:T(8,128)(2,1)}, bf16[4,4,128,128]{3,2,1,0:T(8,128)(2,1)}, u32[]{:S(2)}, u32[]{:S(2)}) collective-permute-start(bf16[4,4,128,128]{3,2,1,0:T(8,128)(2,1)} %bitcast.6), channel_id=1, source_target_pairs={{0,1},{1,0},{2,3},{3,2},{4,5},{5,4},{6,7},{7,6},{8,9},{9,8},{10,11... | collective-permute-start | bytes 1572872 | tf_op jit(solution)/shard_map/ppermute | solution.py:48
  94.6 4.7 %copy.49 = bf16[4096,3,128]{0,2,1:T(8,128)(2,1)} copy(bf16[4096,3,128]{2,0,1:T(8,128)(2,1)} %param.11) | data formatting | bytes 6291456 | tf_op args[1]
  100.0 0.8 broadcast_compare_fusion.2
  100.8 0.2 convert_reduce_fusion.1
  101.0 2.1 %gather_fusion.3 = f32[32,128,128]{2,1,0:T(8,128)} fusion(f32[32,128,128]{2,1,0:T(8,128)S(1)} %bitcast.215, s32[1024]{0:T(1024)S(1)} %pad_clamp_fusion), kind=kCustom, calls=%fused_computation.1.clone | custom fusion | bytes 4194432 | tf_op jit(solution)/shard_map/jit(_take)/gather | solution.py:104
  103.0 1.8 %reshape.584 = bf16[128,16,2,128]{3,2,1,0:T(2,128)(2,1)S(1)} reshape(bf16[128,4096]{1,0:T(8,128)(2,1)} %param.12) | data formatting | bytes 2097152 | tf_op jit(solution)/shard_map/reshape | solution.py:57
  104.8 0.0 copy-start.1
  104.8 3.6 %constant_dynamic-slice_fusion.1 = (bf16[128,16,1,128]{3,2,1,0:T(2,128)(2,1)}, bf16[128,16,1,128]{3,2,1,0:T(2,128)(2,1)}) fusion(bf16[128,16,2,128]{3,2,1,0:T(2,128)(2,1)S(1)} %reshape.584, s32[]{:T(128)S(6)} %select_n.112, s32[]{:T(128)S(6)} %select_n.131), kind=kLoop, calls=%fused_computation.150 | loop fusion | bytes 2097160 | tf_op jit(solution)/shard_map/jit(dynamic_index_in_dim)/dynamic_slice | solution.py:60
  108.4 3.5 %copy.58 = bf16[128,16,1,128]{0,3,1,2:T(8,128)(2,1)} copy(bf16[128,16,1,128]{3,2,1,0:T(2,128)(2,1)} %get-tuple-element.29) | data formatting | bytes 1048576
  111.9 0.0 copy-done.1
  111.9 0.7 gather_fusion
  112.7 0.0 collective-permute-done
  112.7 1.3 select_bitcast_fusion.1
  114.0 0.1 maximum_bitcast_fusion
  114.1 1.1 copy.48
  115.2 1.7 %reshape.634 = bf16[4,32,4096,1]{2,1,0,3:T(8,128)(2,1)} reshape(bf16[128,4,4,2,128]{4,3,2,1,0:T(2,128)(2,1)S(1)} %copy.48) | data formatting | bytes 2097152 | tf_op jit(solution)/shard_map/dot_general | solution.py:97
  116.8 3.3 %fusion = f32[4,32,3,128]{3,1,2,0:T(8,128)S(1)} fusion(bf16[4096,3,128]{0,2,1:T(8,128)(2,1)} %copy.49, bf16[4,32,4096,1]{2,1,0,3:T(8,128)(2,1)} %reshape.634), kind=kOutput, calls=%fused_computation.4 | convolution fusion | flops 402653184 | bytes 4390912 | tf_op jit(solution)/shard_map/dot_general | solution.py:97
  120.2 0.3 fusion.18
  120.5 0.0 all-to-all-done
  120.5 2.9 %gather_fusion.1 = bf16[32,128,128]{2,1,0:T(8,128)(2,1)} fusion(bf16[32,128,128]{2,1,0:T(8,128)(2,1)} %bitcast.4, s32[1024]{0:T(1024)S(1)} %pad_clamp_fusion.1), kind=kCustom, calls=%fused_computation.3 | custom fusion | bytes 2097280 | tf_op jit(solution)/shard_map/jit(_take)/gather | solution.py:105
  123.4 4.2 %fusion.2 = f32[32,128,4]{1,2,0:T(4,128)S(1)} fusion(f32[32,128,128]{2,1,0:T(8,128)} %gather_fusion.3, bf16[32,128,128]{2,1,0:T(8,128)(2,1)} %gather_fusion.1, pred[32]{0:T(512)(128)(4,1)S(1)} %get-tuple-element.26, pred[32]{0:T(512)(128)(4,1)S(1)} %get-tuple-element.44, pred[32]{0:T(512)(128)(4,1)S(1)} %get-tuple-element.21, ...), kind=kOutput, calls=%fused_computation.7 | convolution fusion | flops 27262976 | bytes 3276896 | tf_op jit(solution)/shard_map/trd,rde->tre/dot_general | solution.py:111
  127.6 0.2 fusion.48
  127.8 0.2 fusion.57
  128.1 0.1 fusion.54
  128.2 0.1 fusion.62
  128.3 1.1 fusion.4
  129.4 2.4 %collective-permute-start.1 = (bf16[16,128,128]{1,2,0:T(8,128)(2,1)}, bf16[16,128,128]{1,2,0:T(8,128)(2,1)}, u32[]{:S(2)}, u32[]{:S(2)}) collective-permute-start(bf16[16,128,128]{1,2,0:T(8,128)(2,1)} %fusion.4), channel_id=1, source_target_pairs={{0,1},{1,0},{2,3},{3,2},{4,5},{5,4},{6,7},{7,6},{8,9},{9,8},{10,11... | collective-permute-start | bytes 1572872 | tf_op jit(solution)/shard_map/ppermute | solution.py:64
  131.8 1.9 %copy.56 = bf16[128,16,1,128]{0,3,1,2:T(8,128)(2,1)} copy(bf16[128,16,1,128]{3,2,1,0:T(2,128)(2,1)S(1)} %copy-done.2) | data formatting | bytes 1048576
  133.7 0.0 collective-permute-done.1
  133.7 1.5 add_convert_fusion
  135.2 13.0 %all_to_all.15 = bf16[4,4,128,128]{2,3,1,0:T(8,128)(2,1)S(1)} all-to-all(bf16[4,4,128,128]{2,3,1,0:T(8,128)(2,1)S(1)} %bitcast.217), channel_id=1, replica_groups={{0,8,16,24},{1,9,17,25},{2,10,18,26},{3,11,19,27},{4,12,20,28},{5,13,21..., dimensions={0} | all-to-all | bytes 1048576 | tf_op jit(solution)/shard_map/all_to_all | solution.py:67
  148.2 0.1 reduce_sum.194
  148.3 8.3 %all_to_all.16 = bf16[4,128,128]{1,2,0:T(8,128)(2,1)S(1)} all-to-all(bf16[4,128,128]{1,2,0:T(8,128)(2,1)S(1)} %reduce_sum.194), channel_id=1, replica_groups={{0,2,4,6},{1,3,5,7},{8,10,12,14},{9,11,13,15},{16,18,20,22},{17,19,21,2..., dimensions={0} | all-to-all | bytes 262144 | tf_op jit(solution)/shard_map/all_to_all | solution.py:69
  156.7 0.7 copy.54
  (29 shorter events, 0.2 us)
Async XLA Ops:
  0.0 2.4 %copy-start = (f32[32,1,128,128]{3,2,1,0:T(8,128)S(1)}, f32[32,1,128,128]{3,2,1,0:T(8,128)}, u32[]{:S(2)}) copy-start(f32[32,1,128,128]{3,2,1,0:T(8,128)} %param.15) | copy-start | bytes 6291460
  3.1 19.3 %copy-start.4 = (bf16[4,32,128]{2,1,0:T(8,128)(2,1)S(1)}, bf16[4,32,128]{2,1,0:T(8,128)(2,1)}, u32[]{:S(2)}) copy-start(bf16[4,32,128]{2,1,0:T(8,128)(2,1)} %param.10) | copy-start | bytes 98308
  4.4 116.1 %all-to-all-start = ((bf16[16,2,128,128]{3,2,1,0:T(8,128)(2,1)}), bf16[16,2,128,128]{3,2,1,0:T(8,128)(2,1)}, u32[]{:S(2)}, u32[]{:S(2)}) async-start(bf16[16,2,128,128]{3,2,1,0:T(8,128)(2,1)} %bitcast.216), calls=%async_computation | async-start | bytes 2097152 | tf_op jit(solution)/shard_map/all_to_all | solution.py:41
  92.7 20.0 %collective-permute-start = (bf16[4,4,128,128]{3,2,1,0:T(8,128)(2,1)}, bf16[4,4,128,128]{3,2,1,0:T(8,128)(2,1)}, u32[]{:S(2)}, u32[]{:S(2)}) collective-permute-start(bf16[4,4,128,128]{3,2,1,0:T(8,128)(2,1)} %bitcast.6), channel_id=1, source_target_pairs={{0,1},{1,0},{2,3},{3,2},{4,5},{5,4},{6,7},{7,6},{8,9},{9,8},{10,11... | collective-permute-start | bytes 1572872 | tf_op jit(solution)/shard_map/ppermute | solution.py:48
  104.8 7.1 %copy-start.1 = (s32[512]{0:T(512)S(1)}, s32[512]{0:T(512)}, u32[]{:S(2)}) copy-start(s32[512]{0:T(512)} %param.16) | copy-start | bytes 6148
  123.4 4.7 %copy-start.5 = (f32[128]{0:T(128)S(1)}, f32[128]{0:T(128)}, u32[]{:S(2)}) copy-start(f32[128]{0:T(128)} %param.13) | copy-start | bytes 1540
  123.4 4.9 %copy-start.3 = (bf16[128,16,1,128]{0,3,1,2:T(8,128)(2,1)S(1)}, bf16[128,16,1,128]{0,3,1,2:T(8,128)(2,1)}, u32[]{:S(2)}) copy-start(bf16[128,16,1,128]{0,3,1,2:T(8,128)(2,1)} %copy.58) | copy-start | bytes 1572868
  123.4 8.4 %copy-start.2 = (bf16[128,16,1,128]{3,2,1,0:T(2,128)(2,1)S(1)}, bf16[128,16,1,128]{3,2,1,0:T(2,128)(2,1)}, u32[]{:S(2)}) copy-start(bf16[128,16,1,128]{3,2,1,0:T(2,128)(2,1)} %get-tuple-element.28) | copy-start | bytes 1572868
  129.4 4.3 %collective-permute-start.1 = (bf16[16,128,128]{1,2,0:T(8,128)(2,1)}, bf16[16,128,128]{1,2,0:T(8,128)(2,1)}, u32[]{:S(2)}, u32[]{:S(2)}) collective-permute-start(bf16[16,128,128]{1,2,0:T(8,128)(2,1)} %fusion.4), channel_id=1, source_target_pairs={{0,1},{1,0},{2,3},{3,2},{4,5},{5,4},{6,7},{7,6},{8,9},{9,8},{10,11... | collective-permute-start | bytes 1572872 | tf_op jit(solution)/shard_map/ppermute | solution.py:64

commit v2 on v1

v2 whole, which is shorter than its diff:
```python
import functools

import jax
import jax.numpy as jnp
from jax import lax
from jax.experimental import pallas as pl
from jax.experimental.pallas import tpu as pltpu
from jax.sharding import PartitionSpec as P

STEPS = 4
SIZE = 128
MOVED = 13
XS, ZS, CORES = 4, 4, 2
CHIPS = XS * ZS
SLOTS = 2


def tensor_id(x, z, c):
    return (x * ZS + z) * CORES + c


Z_LINES = [[tensor_id(x, z, c) for z in range(ZS)] for x in range(XS) for c in range(CORES)]
X_RINGS = [[tensor_id(x, z, c) for x in range(XS)] for z in range(ZS) for c in range(CORES)]
CORE_SWAP = [
    (tensor_id(x, z, c), tensor_id(x, z, 1 - c))
    for x in range(XS)
    for z in range(ZS)
    for c in range(CORES)
]

VMEM = pl.BlockSpec(memory_space=pltpu.VMEM)
SMEM = pl.BlockSpec(memory_space=pltpu.SMEM)
ANY = pl.BlockSpec(memory_space=pl.ANY)


def ranks(same):
    rows = same.shape[-1]
    earlier = jnp.arange(rows)[None, :] < jnp.arange(rows)[:, None]
    return jnp.sum((same & earlier).astype(jnp.int32), axis=-1)


def after_kernel(x_ref, dep_ref, out_ref):
    pass


def after(x, dep):
    return pl.pallas_call(
        after_kernel,
        out_shape=jax.ShapeDtypeStruct(x.shape, x.dtype),
        in_specs=[ANY, ANY],
        out_specs=ANY,
        input_output_aliases={0: 0},
        name="after",
    )(x, dep)


def pack_states(states, migration_plan, own_group, groups):
    rows = states.shape[0]
    plan = migration_plan.reshape(groups, rows)
    source_group, source_slot = plan // rows, plan % rows
    from_here = source_group == own_group
    order = ranks(jnp.broadcast_to(from_here[:, None, :], (groups, rows, rows)))
    wanted = from_here[:, None, :] & (order[:, None, :] == jnp.arange(SLOTS)[None, :, None])
    chosen = jnp.sum(jnp.where(wanted, source_slot[:, None, :], 0), axis=-1)
    outgoing = jnp.take(states, chosen.reshape(-1), axis=0).astype(jnp.bfloat16)
    return outgoing.reshape(groups, SLOTS, *states.shape[1:])


def split_rows(q):
    high = q.astype(jnp.bfloat16)
    low = (q - high.astype(jnp.float32)).astype(jnp.bfloat16)
    return jnp.concatenate([high, low], axis=0)


def project_kernel(
    rows, where_ref, plan_ref, decay_ref, own_ref, other_ref, weight_ref, states_ref,
    query_ref, partial_ref, kept_ref,
):
    group, core = where_ref[0], where_ref[1]
    count = STEPS * rows
    acc = [jnp.zeros((count, SIZE), jnp.float32) for _ in range(3)]
    for chip in range(CHIPS):
        a, b = own_ref[chip], other_ref[chip]
        even = jnp.where(core == 0, a, b)
        odd = jnp.where(core == 0, b, a)
        both = jnp.concatenate([even, odd], axis=1)
        for i in range(3):
            weight = weight_ref[i, 2 * SIZE * chip : 2 * SIZE * (chip + 1), :]
            acc[i] += jnp.dot(both, weight, preferred_element_type=jnp.float32)
    query = acc[0] / (1.0 + jnp.exp(-acc[0]))
    key = acc[1] / (1.0 + jnp.exp(-acc[1]))
    value = acc[2]
    query_ref[...] = query
    for row in range(rows):
        source = plan_ref[group * rows + row]
        state = states_ref[source % rows]
        high = state.astype(jnp.bfloat16)
        low = (state - high.astype(jnp.float32)).astype(jnp.bfloat16)
        mine = query_ref[pl.ds(row, STEPS, stride=rows), :]
        pair = split_rows(mine)
        first = jnp.dot(pair, high, preferred_element_type=jnp.float32)
        second = jnp.dot(pair[:STEPS], low, preferred_element_type=jnp.float32)
        product = first[:STEPS] + first[STEPS:] + second
        stays = (source // rows == group).astype(jnp.float32)
        kept_ref[pl.ds(row, STEPS, stride=rows), :] = product * stays
    decay = decay_ref[0]
    at = lambda x, t: x[t * rows : (t + 1) * rows]
    power = decay
    for t in range(STEPS):
        readout = power * at(kept_ref, t)
        power = power * decay
        weight = jnp.float32(1.0)
        for s in range(t, -1, -1):
            score = jnp.sum(at(query, t) * at(key, s), axis=-1, keepdims=True)
            readout = readout + (weight * score) * at(value, s)
            weight = weight * decay
        partial_ref[t * rows : (t + 1) * rows] = readout


def finish_kernel(
    rows, where_ref, plan_ref, remaining_ref, decay_ref, query_ref, partial_ref, incoming_ref,
    gain_ref, weight_ref, own_ref, other_ref, readout_ref, active_ref, row_ref, slot_ref, seen_ref,
):
    group, core = where_ref[0], where_ref[1]
    groups = where_ref[2]
    decay = decay_ref[0]

    def clear(i, carry):
        seen_ref[i] = 0
        return carry

    lax.fori_loop(0, groups, clear, 0)
    for i in range(MOVED):
        row_ref[i] = 0
        slot_ref[i] = 0

    def scan(row, count):
        source = plan_ref[group * rows + row]
        source_group = source // rows
        rank = seen_ref[source_group]
        seen_ref[source_group] = rank + 1
        moved = source_group != group
        place = jnp.minimum(count, MOVED - 1)

        @pl.when(moved)
        def _():
            row_ref[place] = row
            slot_ref[place] = source_group * SLOTS + jnp.minimum(rank, SLOTS - 1)

        steps = remaining_ref[source]
        active_ref[pl.ds(row, 1), :] = jnp.full((1, SIZE), steps, jnp.int32)
        return count + moved.astype(jnp.int32)

    lax.fori_loop(0, rows, scan, 0)
    readout_ref[...] = partial_ref[...]
    power = lax.broadcasted_iota(jnp.int32, (STEPS, SIZE), 0)
    scale = jnp.where(power == 0, decay, 0.0)
    running = decay
    for t in range(1, STEPS):
        running = running * decay
        scale = jnp.where(power == t, running, scale)
    for i in range(MOVED):
        row = row_ref[i]
        mine = query_ref[pl.ds(row, STEPS, stride=rows), :]
        product = jnp.dot(
            split_rows(mine), incoming_ref[slot_ref[i]], preferred_element_type=jnp.float32
        )
        product = product[:STEPS] + product[STEPS:]
        readout_ref[pl.ds(row, STEPS, stride=rows), :] += scale * product
    pieces = []
    for t in range(STEPS):
        readout = readout_ref[t * rows : (t + 1) * rows]
        norm = lax.rsqrt(jnp.mean(readout * readout, axis=-1, keepdims=True) + 1e-05)
        normed = readout * norm * gain_ref[...]
        pieces.append(jnp.where(active_ref[...] > t, normed, 0.0))
    normed = jnp.concatenate(pieces, axis=0).astype(jnp.bfloat16)
    for chip in range(CHIPS):
        weight = weight_ref[:, 2 * SIZE * chip : 2 * SIZE * (chip + 1)]
        both = jnp.dot(normed, weight, preferred_element_type=jnp.float32)
        even, odd = both[:, :SIZE], both[:, SIZE:]
        own_ref[chip] = jnp.where(core == 0, even, odd)
        other_ref[chip] = jnp.where(core == 0, odd, even).astype(jnp.bfloat16)


def body(
    step_inputs,
    qkv_weight,
    out_weight,
    head_gain,
    head_decay,
    states_in,
    remaining_steps,
    migration_plan,
):
    rows = states_in.shape[0]
    count = STEPS * rows
    groups = lax.axis_size("group")
    own_group = lax.axis_index("group")
    core = lax.axis_index("tensor") % CORES
    where = jnp.stack([own_group, core, jnp.int32(groups)]).astype(jnp.int32)
    states = states_in.reshape(rows, SIZE, SIZE)

    line = lax.all_gather(
        step_inputs.reshape(count, SIZE), "tensor", axis=0, axis_index_groups=Z_LINES
    )
    outgoing = after(pack_states(states, migration_plan, own_group, groups), line)
    incoming = lax.all_to_all(outgoing, "group", 0, 0, tiled=True)
    incoming = incoming.reshape(groups * SLOTS, SIZE, SIZE)

    plane = lax.all_gather(line, "tensor", axis=0, axis_index_groups=X_RINGS)
    plane = plane.reshape(CHIPS, count, SIZE)
    other = lax.ppermute(plane, "tensor", CORE_SWAP)
    f32 = jnp.float32
    query, partial = pl.pallas_call(
        functools.partial(project_kernel, rows),
        out_shape=[jax.ShapeDtypeStruct((count, SIZE), f32)] * 2,
        in_specs=[SMEM, SMEM, SMEM, VMEM, VMEM, VMEM, VMEM],
        out_specs=[VMEM, VMEM],
        scratch_shapes=[pltpu.VMEM((count, SIZE), f32)],
        compiler_params=pltpu.CompilerParams(vmem_limit_bytes=24 * 2**20),
        cost_estimate=pl.CostEstimate(
            flops=2 * count * 4096 * 384, bytes_accessed=6 * 2**20, transcendentals=0
        ),
        name="project",
    )(where, migration_plan, head_decay, plane, other, jnp.transpose(qkv_weight, (1, 0, 2)), states)
    own, away = pl.pallas_call(
        functools.partial(finish_kernel, rows),
        out_shape=[
            jax.ShapeDtypeStruct((CHIPS, count, SIZE), f32),
            jax.ShapeDtypeStruct((CHIPS, count, SIZE), jnp.bfloat16),
        ],
        in_specs=[SMEM, SMEM, SMEM, SMEM, VMEM, VMEM, VMEM, VMEM, VMEM],
        out_specs=[VMEM, VMEM],
        scratch_shapes=[
            pltpu.VMEM((count, SIZE), f32),
            pltpu.VMEM((rows, SIZE), jnp.int32),
            pltpu.SMEM((MOVED,), jnp.int32),
            pltpu.SMEM((MOVED,), jnp.int32),
            pltpu.SMEM((groups,), jnp.int32),
        ],
        compiler_params=pltpu.CompilerParams(vmem_limit_bytes=24 * 2**20),
        cost_estimate=pl.CostEstimate(
            flops=2 * count * 4096 * 128, bytes_accessed=4 * 2**20, transcendentals=0
        ),
        name="finish",
    )(
        where, migration_plan, remaining_steps, head_decay, query, partial, incoming,
        head_gain.reshape(1, SIZE), out_weight,
    )
    received = lax.ppermute(away, "tensor", CORE_SWAP)
    plane = (own + received.astype(f32)).astype(jnp.bfloat16).reshape(XS, ZS, count, SIZE)
    pieces = lax.all_to_all(plane, "tensor", 0, 0, tiled=True, axis_index_groups=X_RINGS)
    line = jnp.sum(pieces.astype(f32), axis=0).astype(jnp.bfloat16)
    pieces = lax.all_to_all(line, "tensor", 0, 0, tiled=True, axis_index_groups=Z_LINES)
    result = jnp.sum(pieces.astype(f32), axis=0).astype(jnp.bfloat16)
    return result.reshape(STEPS, rows, SIZE)


def solution(mesh):
    placed = (
        P(None, "group", "tensor"),
        P(None, None, "tensor"),
        P("tensor", None),
        P("tensor"),
        P("tensor"),
        P("group", "tensor", None, None),
        P(),
        P(),
    )
    return jax.shard_map(
        body, mesh=mesh, in_specs=placed, out_specs=P(None, "group", "tensor"), check_vma=False
    )
```

time: 158 us -> 118 us (0.75)
  the two profiles are of different devices: /device:TPU:16 before, /device:TPU:32 now
where the time goes in v2:
time: 118 us
  blocking collectives  61.7 us (52%)
  waiting for transfers between devices  24.3 us (21%)
  starting transfers between devices  17 us (14%)
  local copies, waits for them, and re-layouts  6.47 us (5%)
  Pallas kernels  4.89 us (4%)
  other arithmetic  2.71 us (2%)
    all_to_all x1, waiting for transfers between devices, body(): incoming = lax.all_to_all(outgoing, 'group', 0, 0, tiled=True)  20.9 us
    all_gather x1, blocking collectives, body(): lax.all_gather(step_inputs.reshape(count, SIZE), 'tensor', axis=0, axis_i...  17.3 us
    all_to_all x1, blocking collectives, body(): lax.all_to_all(line, 'tensor', 0, 0, tiled=True, axis_index_groups=Z_LINES)  16.7 us
    all_gather x1, blocking collectives, body(): plane = lax.all_gather(line, 'tensor', axis=0, axis_index_groups=X_RINGS)  13.9 us
    all_to_all x1, blocking collectives, body(): lax.all_to_all(plane, 'tensor', 0, 0, tiled=True, axis_index_groups=X_RINGS)  13.9 us
    all_to_all x1, starting transfers between devices, body(): incoming = lax.all_to_all(outgoing, 'group', 0, 0, tiled=True)  13.2 us
    unnamed x14, local copies, waits for them, and re-layouts  3.13 us
    pallas_call x1, Pallas kernels, body(): pl.pallas_call(functools.partial(project_kernel, rows), out_shape=[jax.Sh...  2.86 us
  transfers between devices with their start and end apart: 3, of which 3 were waited for; matrix products, arithmetic and copies ran while one was open for 0% of the time, Pallas kernels for 2%

profile of v2, /device:TPU:32, one launch (start us, length us, event | category | flops | bytes accessed | tf_op | source)
XLA Modules:
  0.0 117.8 jit_solution(113586375234943314)
XLA Ops:
  0.0 0.8 reshape.126
  0.8 0.3 convert_reduce_fusion
  1.2 0.1 select_reduce_fusion
  1.3 0.1 copy.11
  1.4 0.1 copy.10
  1.5 0.1 reshape.127
  1.6 17.3 %all_gather.9.dep_ref = bf16[4,128,128]{2,1,0:T(8,128)(2,1)} all-gather(bf16[1,128,128]{2,1,0:T(8,128)(2,1)} %bitcast.19), channel_id=1, replica_groups={{0,2,4,6},{1,3,5,7},{8,10,12,14},{9,11,13,15},{16,18,20,22},{17,19,21,2..., dimensions={0}, use_global_device_ids=true | all-gather | bytes 163840 | tf_op jit(solution)/shard_map/all_gather | solution.py:203
  18.9 2.3 %gather_fusion = bf16[32,128,128]{2,1,0:T(8,128)(2,1)S(1)} fusion(f32[32,128,128]{2,1,0:T(8,128)} %bitcast.12, s32[1024]{0:T(1024)S(1)} %pad_clamp_fusion), kind=kCustom, calls=%fused_computation | custom fusion | bytes 2097280 | tf_op jit(solution)/shard_map/jit(_take)/gather | solution.py:65
  21.2 1.3 %select_convert_fusion.x_ref = bf16[16,2,128,128]{3,2,1,0:T(8,128)(2,1)} fusion(bf16[16,2,128,128]{3,2,1,0:T(8,128)(2,1)S(1)} %bitcast.17, pred[16,2]{1,0:T(8,128)(4,1)S(1)} %copy.10), kind=kLoop, calls=%fused_computation.1 | loop fusion | flops 524288 | bytes 2097184 | tf_op jit(solution)/shard_map/convert_element_type | solution.py:65
  22.5 0.0 copy-start.6
  22.5 0.0 copy-start
  22.5 0.0 copy-start.3
  22.5 13.2 %all-to-all-start = ((bf16[16,2,128,128]{3,2,1,0:T(8,128)(2,1)}), bf16[16,2,128,128]{3,2,1,0:T(8,128)(2,1)S(1)}, u32[]{:S(2)}, u32[]{:S(2)}) async-start(bf16[16,2,128,128]{3,2,1,0:T(8,128)(2,1)} %after.1), calls=%async_computation | async-start | bytes 2097152 | tf_op jit(solution)/shard_map/all_to_all | solution.py:207
  35.7 0.0 copy-done.6
  35.7 13.9 %all-gather.own_ref = bf16[16,128,128]{2,1,0:T(8,128)(2,1)} all-gather(bf16[4,128,128]{2,1,0:T(8,128)(2,1)S(1)} %copy-done.6), channel_id=2, replica_groups={{0,8,16,24},{1,9,17,25},{2,10,18,26},{3,11,19,27},{4,12,20,28},{5,13,21..., dimensions={0}, use_global_device_ids=true | all-gather | bytes 655360 | tf_op jit(solution)/shard_map/all_gather | solution.py:210
  49.5 1.9 %collective-permute-start = (bf16[16,128,128]{2,1,0:T(8,128)(2,1)}, bf16[16,128,128]{2,1,0:T(8,128)(2,1)}, u32[]{:S(2)}, u32[]{:S(2)}) collective-permute-start(bf16[16,128,128]{2,1,0:T(8,128)(2,1)} %all-gather.own_ref), channel_id=1, source_target_pairs={{0,1},{1,0},{2,3},{3,2},{4,5},{5,4},{6,7},{7,6},{8,9},{9,8},{10,11... | collective-permute-start | bytes 1572872 | tf_op jit(solution)/shard_map/ppermute | solution.py:212
  52.1 0.1 pad_add_fusion.where_ref
  52.2 1.5 %collective-permute-done.other_ref = bf16[16,128,128]{2,1,0:T(8,128)(2,1)} collective-permute-done((bf16[16,128,128]{2,1,0:T(8,128)(2,1)}, bf16[16,128,128]{2,1,0:T(8,128)(2,1)}, u32[]{:S(2)}, u32[]{:S(2)}) %collective-permute-start) | collective-permute-done | bytes 524320 | tf_op jit(solution)/shard_map/ppermute | solution.py:212
  53.7 0.0 copy-done
  53.7 0.0 copy-done.3
  53.7 0.0 copy-start.1
  53.7 1.9 %copy-done.1 = bf16[4096,3,128]{2,0,1:T(8,128)(2,1)S(1)} copy-done((bf16[4096,3,128]{2,0,1:T(8,128)(2,1)S(1)}, bf16[4096,3,128]{2,0,1:T(8,128)(2,1)}, u32[]{:S(2)}) %copy-start.1) | copy-done | bytes 3145752
  55.6 0.0 copy-start.4
  55.6 0.0 copy-start.5
  55.6 2.9 %project.1 = (f32[128,128]{1,0:T(8,128)S(1)}, f32[128,128]{1,0:T(8,128)S(1)}) custom-call(s32[3]{0:T(128)S(1)} %pad_add_fusion.where_ref, s32[512]{0:T(512)S(1)} %copy-done.3, f32[1]{0:T(128)S(6)} %copy.13.decay_ref, bf16[16,128,128]{2,1,0:T(8,128)(2,1)} %all-gather.own_ref, bf16[16,128,128]{2,1,0:T(8,128)(2,1)} %collective-permute-done.other_ref, ...), custom_call_target="tpu_custom_call" | custom-call | flops 402653184 | bytes 6291456 | tf_op jit(solution)/shard_map/project/pallas_call | solution.py:214
  58.5 20.9 %all-to-all-done = bf16[16,2,128,128]{3,2,1,0:T(8,128)(2,1)S(1)} async-done(((bf16[16,2,128,128]{3,2,1,0:T(8,128)(2,1)}), bf16[16,2,128,128]{3,2,1,0:T(8,128)(2,1)S(1)}, u32[]{:S(2)}, u32[]{:S(2)}) %all-to-all-start) | async-done | bytes 1048608 | tf_op jit(solution)/shard_map/all_to_all | solution.py:207
  79.4 0.0 copy-done.4
  79.4 0.0 copy-done.5
  79.4 0.0 copy-start.2
  79.4 1.2 %copy-done.2 = bf16[128,4096]{1,0:T(8,128)(2,1)S(1)} copy-done((bf16[128,4096]{1,0:T(8,128)(2,1)S(1)}, bf16[128,4096]{1,0:T(8,128)(2,1)}, u32[]{:S(2)}) %copy-start.2) | copy-done | bytes 1048600
  80.6 2.0 %finish.1 = (f32[16,128,128]{2,1,0:T(8,128)S(1)}, bf16[16,128,128]{2,1,0:T(8,128)(2,1)S(1)}) custom-call(s32[3]{0:T(128)S(1)} %pad_add_fusion.where_ref, s32[512]{0:T(512)S(1)} %copy-done.3, s32[512]{0:T(512)S(1)} %copy-done.4, f32[1]{0:T(128)S(6)} %copy.13.decay_ref, f32[128,128]{1,0:T(8,128)S(1)} %get-tuple-element.9.query_ref, ...), custom_call_target="tpu_custom_call" | custom-call | flops 134217728 | bytes 4194304 | tf_op jit(solution)/shard_map/finish/pallas_call | solution.py:226
  82.6 1.9 %collective-permute-start.1 = (bf16[16,128,128]{2,1,0:T(8,128)(2,1)S(1)}, bf16[16,128,128]{2,1,0:T(8,128)(2,1)S(1)}, u32[]{:S(2)}, u32[]{:S(2)}) collective-permute-start(bf16[16,128,128]{2,1,0:T(8,128)(2,1)S(1)} %get-tuple-element.12), channel_id=1, source_target_pairs={{0,1},{1,0},{2,3},{3,2},{4,5},{5,4},{6,7},{7,6},{8,9},{9,8},{10,11... | collective-permute-start | bytes 1572872 | tf_op jit(solution)/shard_map/ppermute | solution.py:250
  84.6 1.9 %collective-permute-done.1 = bf16[16,128,128]{2,1,0:T(8,128)(2,1)S(1)} collective-permute-done((bf16[16,128,128]{2,1,0:T(8,128)(2,1)S(1)}, bf16[16,128,128]{2,1,0:T(8,128)(2,1)S(1)}, u32[]{:S(2)}, u32[]{:S(2)}) %collective-permute-start.1) | collective-permute-done | bytes 524320 | tf_op jit(solution)/shard_map/ppermute | solution.py:250
  86.4 0.1 add_convert_fusion
  86.6 13.9 %all_to_all.15 = bf16[4,4,128,128]{3,2,1,0:T(8,128)(2,1)S(1)} all-to-all(bf16[4,4,128,128]{3,2,1,0:T(8,128)(2,1)S(1)} %bitcast.18), channel_id=1, replica_groups={{0,8,16,24},{1,9,17,25},{2,10,18,26},{3,11,19,27},{4,12,20,28},{5,13,21..., dimensions={0} | all-to-all | bytes 1048576 | tf_op jit(solution)/shard_map/all_to_all | solution.py:252
  100.5 0.1 reduce_sum.44
  100.5 16.7 %all_to_all.16 = bf16[4,128,128]{2,1,0:T(8,128)(2,1)S(1)} all-to-all(bf16[4,128,128]{2,1,0:T(8,128)(2,1)S(1)} %reduce_sum.44), channel_id=1, replica_groups={{0,2,4,6},{1,3,5,7},{8,10,12,14},{9,11,13,15},{16,18,20,22},{17,19,21,2..., dimensions={0} | all-to-all | bytes 262144 | tf_op jit(solution)/shard_map/all_to_all | solution.py:254
  117.2 0.6 reduce_sum.45
  (7 shorter events, 0.1 us)
Async XLA Ops:
  22.5 13.2 %copy-start.6 = (bf16[4,128,128]{2,1,0:T(8,128)(2,1)S(1)}, bf16[4,128,128]{2,1,0:T(8,128)(2,1)}, u32[]{:S(2)}) copy-start(bf16[4,128,128]{2,1,0:T(8,128)(2,1)} %all_gather.9.dep_ref) | copy-start | bytes 393220
  22.5 31.2 %copy-start = (f32[32,1,128,128]{3,2,1,0:T(8,128)S(1)}, f32[32,1,128,128]{3,2,1,0:T(8,128)}, u32[]{:S(2)}) copy-start(f32[32,1,128,128]{3,2,1,0:T(8,128)} %param.13) | copy-start | bytes 6291460
  22.5 31.2 %copy-start.3 = (s32[512]{0:T(512)S(1)}, s32[512]{0:T(512)}, u32[]{:S(2)}) copy-start(s32[512]{0:T(512)} %plan_ref.3) | copy-start | bytes 6148
  22.5 56.9 %all-to-all-start = ((bf16[16,2,128,128]{3,2,1,0:T(8,128)(2,1)}), bf16[16,2,128,128]{3,2,1,0:T(8,128)(2,1)S(1)}, u32[]{:S(2)}, u32[]{:S(2)}) async-start(bf16[16,2,128,128]{3,2,1,0:T(8,128)(2,1)} %after.1), calls=%async_computation | async-start | bytes 2097152 | tf_op jit(solution)/shard_map/all_to_all | solution.py:207
  49.5 4.1 %collective-permute-start = (bf16[16,128,128]{2,1,0:T(8,128)(2,1)}, bf16[16,128,128]{2,1,0:T(8,128)(2,1)}, u32[]{:S(2)}, u32[]{:S(2)}) collective-permute-start(bf16[16,128,128]{2,1,0:T(8,128)(2,1)} %all-gather.own_ref), channel_id=1, source_target_pairs={{0,1},{1,0},{2,3},{3,2},{4,5},{5,4},{6,7},{7,6},{8,9},{9,8},{10,11... | collective-permute-start | bytes 1572872 | tf_op jit(solution)/shard_map/ppermute | solution.py:212
  53.7 1.9 %copy-start.1 = (bf16[4096,3,128]{2,0,1:T(8,128)(2,1)S(1)}, bf16[4096,3,128]{2,0,1:T(8,128)(2,1)}, u32[]{:S(2)}) copy-start(bf16[4096,3,128]{2,0,1:T(8,128)(2,1)} %param.9) | copy-start | bytes 9437188
  55.6 23.8 %copy-start.4 = (s32[512]{0:T(512)S(1)}, s32[512]{0:T(512)}, u32[]{:S(2)}) copy-start(s32[512]{0:T(512)} %remaining_ref.1) | copy-start | bytes 6148
  55.6 23.8 %copy-start.5 = (f32[128]{0:T(128)S(1)}, f32[128]{0:T(128)}, u32[]{:S(2)}) copy-start(f32[128]{0:T(128)} %param.11) | copy-start | bytes 1540
  79.4 1.2 %copy-start.2 = (bf16[128,4096]{1,0:T(8,128)(2,1)S(1)}, bf16[128,4096]{1,0:T(8,128)(2,1)}, u32[]{:S(2)}) copy-start(bf16[128,4096]{1,0:T(8,128)(2,1)} %weight_ref.1) | copy-start | bytes 3145732
  82.6 3.8 %collective-permute-start.1 = (bf16[16,128,128]{2,1,0:T(8,128)(2,1)S(1)}, bf16[16,128,128]{2,1,0:T(8,128)(2,1)S(1)}, u32[]{:S(2)}, u32[]{:S(2)}) collective-permute-start(bf16[16,128,128]{2,1,0:T(8,128)(2,1)S(1)} %get-tuple-element.12), channel_id=1, source_target_pairs={{0,1},{1,0},{2,3},{3,2},{4,5},{5,4},{6,7},{7,6},{8,9},{9,8},{10,11... | collective-permute-start | bytes 1572872 | tf_op jit(solution)/shard_map/ppermute | solution.py:250

commit v3 on v2

--- a/solution.py
+++ b/solution.py
@@ -12,7 +12,9 @@
 MOVED = 13
 XS, ZS, CORES = 4, 4, 2
 CHIPS = XS * ZS
+ZH, YS = 4, 4
 SLOTS = 2
+PASSING = 5
 
 
 def tensor_id(x, z, c):
@@ -21,6 +23,8 @@
 
 Z_LINES = [[tensor_id(x, z, c) for z in range(ZS)] for x in range(XS) for c in range(CORES)]
 X_RINGS = [[tensor_id(x, z, c) for x in range(XS)] for z in range(ZS) for c in range(CORES)]
+Y_RINGS = [[z * YS + y for y in range(YS)] for z in range(ZH)]
+Z_RINGS = [[z * YS + y for z in range(ZH)] for y in range(YS)]
 CORE_SWAP = [
     (tensor_id(x, z, c), tensor_id(x, z, 1 - c))
     for x in range(XS)
@@ -33,37 +37,44 @@
 ANY = pl.BlockSpec(memory_space=pl.ANY)
 
 
-def ranks(same):
+def earlier(same):
     rows = same.shape[-1]
-    earlier = jnp.arange(rows)[None, :] < jnp.arange(rows)[:, None]
-    return jnp.sum((same & earlier).astype(jnp.int32), axis=-1)
-
-
-def after_kernel(x_ref, dep_ref, out_ref):
-    pass
-
-
-def after(x, dep):
-    return pl.pallas_call(
-        after_kernel,
-        out_shape=jax.ShapeDtypeStruct(x.shape, x.dtype),
-        in_specs=[ANY, ANY],
-        out_specs=ANY,
-        input_output_aliases={0: 0},
-        name="after",
-    )(x, dep)
-
-
-def pack_states(states, migration_plan, own_group, groups):
-    rows = states.shape[0]
+    before = jnp.arange(rows)[None, :] < jnp.arange(rows)[:, None]
+    return jnp.sum((same & before).astype(jnp.int32), axis=-1)
+
+
+def rows_out(migration_plan, own_group, groups, rows):
     plan = migration_plan.reshape(groups, rows)
-    source_group, source_slot = plan // rows, plan % rows
-    from_here = source_group == own_group
-    order = ranks(jnp.broadcast_to(from_here[:, None, :], (groups, rows, rows)))
-    wanted = from_here[:, None, :] & (order[:, None, :] == jnp.arange(SLOTS)[None, :, None])
-    chosen = jnp.sum(jnp.where(wanted, source_slot[:, None, :], 0), axis=-1)
-    outgoing = jnp.take(states, chosen.reshape(-1), axis=0).astype(jnp.bfloat16)
-    return outgoing.reshape(groups, SLOTS, *states.shape[1:])
+    source = plan // rows
+    here = source == own_group
+    order = earlier(jnp.broadcast_to(here[:, None, :], (groups, rows, rows)))
+    wanted = here[:, None, :] & (order[:, None, :] == jnp.arange(SLOTS)[None, :, None])
+    chosen = jnp.sum(jnp.where(wanted, (plan % rows)[:, None, :], 0), axis=-1)
+    return jnp.transpose(chosen.reshape(ZH, YS, SLOTS), (1, 0, 2)).reshape(-1)
+
+
+def rows_on(migration_plan, own_group, groups, rows):
+    plan = migration_plan.reshape(ZH, YS, rows)
+    plan = lax.dynamic_index_in_dim(plan, own_group % YS, axis=1, keepdims=False)
+    source = plan // rows
+    target = jnp.arange(ZH) * YS + own_group % YS
+    passing = (source // YS == own_group // YS) & (source != target[:, None])
+    order = earlier(jnp.broadcast_to(passing[:, None, :], (ZH, rows, rows)))
+    slot = earlier(source[:, :, None] == source[:, None, :])
+    place = (source % YS) * (ZH * SLOTS) + jnp.arange(ZH)[:, None] * SLOTS + slot
+    wanted = passing[:, None, :] & (order[:, None, :] == jnp.arange(PASSING)[None, :, None])
+    return jnp.sum(jnp.where(wanted, place[:, None, :], 0), axis=-1).reshape(-1)
+
+
+def pack_kernel(index_ref, states_ref, inputs_ref, out_ref, same_ref):
+    for i in range(out_ref.shape[0]):
+        out_ref[i] = states_ref[index_ref[i]].astype(jnp.bfloat16)
+    same_ref[...] = inputs_ref[...]
+
+
+def pass_kernel(index_ref, rows_ref, dep_ref, out_ref):
+    for i in range(out_ref.shape[0]):
+        out_ref[i] = rows_ref[index_ref[i]]
 
 
 def split_rows(q):
@@ -122,14 +133,9 @@
     gain_ref, weight_ref, own_ref, other_ref, readout_ref, active_ref, row_ref, slot_ref, seen_ref,
 ):
     group, core = where_ref[0], where_ref[1]
-    groups = where_ref[2]
     decay = decay_ref[0]
-
-    def clear(i, carry):
+    for i in range(ZH):
         seen_ref[i] = 0
-        return carry
-
-    lax.fori_loop(0, groups, clear, 0)
     for i in range(MOVED):
         row_ref[i] = 0
         slot_ref[i] = 0
@@ -137,15 +143,16 @@
     def scan(row, count):
         source = plan_ref[group * rows + row]
         source_group = source // rows
-        rank = seen_ref[source_group]
-        seen_ref[source_group] = rank + 1
         moved = source_group != group
         place = jnp.minimum(count, MOVED - 1)
 
         @pl.when(moved)
         def _():
+            far = source_group // YS
+            rank = seen_ref[far]
+            seen_ref[far] = rank + 1
             row_ref[place] = row
-            slot_ref[place] = source_group * SLOTS + jnp.minimum(rank, SLOTS - 1)
+            slot_ref[place] = far * PASSING + jnp.minimum(rank, PASSING - 1)
 
         steps = remaining_ref[source]
         active_ref[pl.ds(row, 1), :] = jnp.full((1, SIZE), steps, jnp.int32)
@@ -197,20 +204,40 @@
     groups = lax.axis_size("group")
     own_group = lax.axis_index("group")
     core = lax.axis_index("tensor") % CORES
-    where = jnp.stack([own_group, core, jnp.int32(groups)]).astype(jnp.int32)
+    where = jnp.stack([own_group, core]).astype(jnp.int32)
     states = states_in.reshape(rows, SIZE, SIZE)
-
-    line = lax.all_gather(
-        step_inputs.reshape(count, SIZE), "tensor", axis=0, axis_index_groups=Z_LINES
-    )
-    outgoing = after(pack_states(states, migration_plan, own_group, groups), line)
-    incoming = lax.all_to_all(outgoing, "group", 0, 0, tiled=True)
-    incoming = incoming.reshape(groups * SLOTS, SIZE, SIZE)
+    bf16, f32 = jnp.bfloat16, jnp.float32
+
+    outgoing, inputs = pl.pallas_call(
+        pack_kernel,
+        out_shape=[
+            jax.ShapeDtypeStruct((groups * SLOTS, SIZE, SIZE), bf16),
+            jax.ShapeDtypeStruct((count, SIZE), bf16),
+        ],
+        in_specs=[SMEM, VMEM, VMEM],
+        out_specs=[VMEM, VMEM],
+        compiler_params=pltpu.CompilerParams(vmem_limit_bytes=16 * 2**20),
+        name="pack",
+    )(
+        rows_out(migration_plan, own_group, groups, rows),
+        states,
+        step_inputs.reshape(count, SIZE),
+    )
+    passing = lax.all_to_all(outgoing, "group", 0, 0, tiled=True, axis_index_groups=Y_RINGS)
+    line = lax.all_gather(inputs, "tensor", axis=0, axis_index_groups=Z_LINES)
+    passing = pl.pallas_call(
+        pass_kernel,
+        out_shape=jax.ShapeDtypeStruct((ZH * PASSING, SIZE, SIZE), bf16),
+        in_specs=[SMEM, VMEM, ANY],
+        out_specs=VMEM,
+        compiler_params=pltpu.CompilerParams(vmem_limit_bytes=16 * 2**20),
+        name="pass_on",
+    )(rows_on(migration_plan, own_group, groups, rows), passing, line)
+    incoming = lax.all_to_all(passing, "group", 0, 0, tiled=True, axis_index_groups=Z_RINGS)
 
     plane = lax.all_gather(line, "tensor", axis=0, axis_index_groups=X_RINGS)
     plane = plane.reshape(CHIPS, count, SIZE)
     other = lax.ppermute(plane, "tensor", CORE_SWAP)
-    f32 = jnp.float32
     query, partial = pl.pallas_call(
         functools.partial(project_kernel, rows),
         out_shape=[jax.ShapeDtypeStruct((count, SIZE), f32)] * 2,
@@ -236,7 +263,7 @@
             pltpu.VMEM((rows, SIZE), jnp.int32),
             pltpu.SMEM((MOVED,), jnp.int32),
             pltpu.SMEM((MOVED,), jnp.int32),
-            pltpu.SMEM((groups,), jnp.int32),
+            pltpu.SMEM((ZH,), jnp.int32),
         ],
         compiler_params=pltpu.CompilerParams(vmem_limit_bytes=24 * 2**20),
         cost_estimate=pl.CostEstimate(

time: 118 us -> 107 us (0.907)
  blocking collectives: 61.7 us -> 50.6 us
  waiting for transfers between devices: 24.3 us -> 16 us
  starting transfers between devices: 17 us -> 22.5 us
  local copies, waits for them, and re-layouts: 6.47 us -> 8.68 us
    all_to_all x1, blocking collectives: 16.7 us -> 8.7 us  [body(): lax.all_to_all(line, 'tensor', 0, 0, tiled=True, axis_index_groups=Z_LINES)]
    all_to_all x1 -> x2, waiting for transfers between devices: 20.9 us -> 13 us  [the longest x1 13 us: body(): lax.all_to_all(passing, 'group', 0, 0, tiled=True, axis_index_groups=Z_RI...]
    all_to_all x1 -> x2, starting transfers between devices: 13.2 us -> 18.7 us  [the longest x1 14.1 us: body(): lax.all_to_all(passing, 'group', 0, 0, tiled=True, axis_index_groups=Z_RI...]
    unnamed x14 -> x21, local copies, waits for them, and re-layouts: 3.13 us -> 7.31 us
    all_gather x1, blocking collectives: 17.3 us -> 14.3 us  [body(): line = lax.all_gather(inputs, 'tensor', axis=0, axis_index_groups=Z_LINES)]
    gather x1 -> x0, local copies, waits for them, and re-layouts: 2.3 us -> none  [pack_states(): outgoing = jnp.take(states, chosen.reshape(-1), axis=0).astype(jnp.bfloat16)]
    convert_element_type x1 -> x0, other arithmetic: 1.25 us -> none  [pack_states(): outgoing = jnp.take(states, chosen.reshape(-1), axis=0).astype(jnp.bfloat16)]
    pallas_call x1 -> x2, Pallas kernels: 0.01 us -> 1.24 us  [the longest x1 0.65 us: body(): pl.pallas_call(pack_kernel, out_shape=[jax.ShapeDtypeStruct((groups * SLO...]
  transfers between devices with their start and end apart: 3 -> 4, of which waited for: 3 -> 3; matrix products, arithmetic and copies ran while one was open for 0% -> 1% of each run, Pallas kernels for 2% -> 2%
where the time goes in v3:
time: 107 us
  blocking collectives  50.6 us (47%)
  starting transfers between devices  22.5 us (21%)
  waiting for transfers between devices  16 us (15%)
  local copies, waits for them, and re-layouts  8.68 us (8%)
  Pallas kernels  6.05 us (6%)
  other arithmetic  2.02 us (2%)
    all_gather x1, blocking collectives, body(): line = lax.all_gather(inputs, 'tensor', axis=0, axis_index_groups=Z_LINES)  14.3 us
    all_to_all x1, starting transfers between devices, body(): lax.all_to_all(passing, 'group', 0, 0, tiled=True, axis_index_groups=Z_RI...  14.1 us
    all_to_all x1, blocking collectives, body(): lax.all_to_all(plane, 'tensor', 0, 0, tiled=True, axis_index_groups=X_RINGS)  13.9 us
    all_gather x1, blocking collectives, body(): plane = lax.all_gather(line, 'tensor', axis=0, axis_index_groups=X_RINGS)  13.8 us
    all_to_all x1, waiting for transfers between devices, body(): lax.all_to_all(passing, 'group', 0, 0, tiled=True, axis_index_groups=Z_RI...  13 us
    all_to_all x1, blocking collectives, body(): lax.all_to_all(line, 'tensor', 0, 0, tiled=True, axis_index_groups=Z_LINES)  8.7 us
    unnamed x21, local copies, waits for them, and re-layouts  7.31 us
    all_to_all x1, starting transfers between devices, body(): lax.all_to_all(outgoing, 'group', 0, 0, tiled=True, axis_index_groups=Y_R...  4.59 us
  transfers between devices with their start and end apart: 4, of which 3 were waited for; matrix products, arithmetic and copies ran while one was open for 1% of the time, Pallas kernels for 2%

profile of v3, /device:TPU:32, one launch (start us, length us, event | category | flops | bytes accessed | tf_op | source)
XLA Modules:
  0.0 106.7 jit_solution(16668792649455942191)
XLA Ops:
  0.0 0.8 reshape.148
  0.9 0.3 convert_reduce_fusion
  1.2 0.1 select_reduce_fusion
  1.3 0.1 reshape.149
  1.4 0.1 copy.16
  1.5 0.1 reshape.150.index_ref
  1.6 0.0 copy-start
  1.6 1.6 %copy-done = f32[32,1,128,128]{3,2,1,0:T(8,128)S(1)} copy-done((f32[32,1,128,128]{3,2,1,0:T(8,128)S(1)}, f32[32,1,128,128]{3,2,1,0:T(8,128)}, u32[]{:S(2)}) %copy-start) | copy-done | bytes 2097176
  3.2 0.0 copy-start.7
  3.2 0.8 copy-done.7
  4.0 0.6 pack.1
  4.6 0.0 copy-start.5
  4.7 1.0 copy-done.5
  5.6 0.0 copy-start.1
  5.6 4.6 %all-to-all-start = ((bf16[32,128,128]{2,1,0:T(8,128)(2,1)}), bf16[32,128,128]{2,1,0:T(8,128)(2,1)S(1)}, u32[]{:S(2)}, u32[]{:S(2)}) async-start(bf16[32,128,128]{2,1,0:T(8,128)(2,1)} %copy-done.5), calls=%async_computation | async-start | bytes 2097152 | tf_op jit(solution)/shard_map/all_to_all | solution.py:226
  10.2 0.0 copy-done.6
  10.2 0.1 reshape.154
  10.3 0.1 compare_and_fusion
  10.4 0.3 convert_reduce_fusion.2
  10.7 0.1 fusion.8
  10.8 0.2 select_reduce_fusion.1
  10.9 0.1 copy.18
  11.0 0.1 reshape.155.index_ref
  11.1 14.3 %all-gather = bf16[512,128]{1,0:T(8,128)(2,1)S(1)} all-gather(bf16[128,128]{1,0:T(8,128)(2,1)S(1)} %get-tuple-element.11), channel_id=2, replica_groups={{0,2,4,6},{1,3,5,7},{8,10,12,14},{9,11,13,15},{16,18,20,22},{17,19,21,2..., dimensions={0}, use_global_device_ids=true | all-gather | bytes 163840 | tf_op jit(solution)/shard_map/all_gather | solution.py:227
  25.4 0.0 all-to-all-done.rows_ref
  25.4 0.6 pass_on.1
  26.0 0.0 copy-start.3
  26.0 0.8 copy-done.3
  26.8 14.1 %all-to-all-start.1 = ((bf16[20,128,128]{2,1,0:T(8,128)(2,1)}), bf16[20,128,128]{2,1,0:T(8,128)(2,1)}, u32[]{:S(2)}, u32[]{:S(2)}) async-start(bf16[20,128,128]{2,1,0:T(8,128)(2,1)} %copy-done.3), calls=%async_computation.1 | async-start | bytes 1310720 | tf_op jit(solution)/shard_map/all_to_all | solution.py:236
  41.0 13.8 %all-gather.1.own_ref = bf16[16,128,128]{2,1,0:T(8,128)(2,1)S(1)} all-gather(bf16[4,128,128]{2,1,0:T(8,128)(2,1)S(1)} %bitcast.25), channel_id=3, replica_groups={{0,8,16,24},{1,9,17,25},{2,10,18,26},{3,11,19,27},{4,12,20,28},{5,13,21..., dimensions={0}, use_global_device_ids=true | all-gather | bytes 655360 | tf_op jit(solution)/shard_map/all_gather | solution.py:238
  54.7 1.9 %collective-permute-start = (bf16[16,128,128]{2,1,0:T(8,128)(2,1)S(1)}, bf16[16,128,128]{2,1,0:T(8,128)(2,1)S(1)}, u32[]{:S(2)}, u32[]{:S(2)}) collective-permute-start(bf16[16,128,128]{2,1,0:T(8,128)(2,1)S(1)} %all-gather.1.own_ref), channel_id=1, source_target_pairs={{0,1},{1,0},{2,3},{3,2},{4,5},{5,4},{6,7},{7,6},{8,9},{9,8},{10,11... | collective-permute-start | bytes 1572872 | tf_op jit(solution)/shard_map/ppermute | solution.py:240
  57.3 0.1 pad_add_fusion.where_ref
  57.4 1.1 %collective-permute-done.other_ref = bf16[16,128,128]{2,1,0:T(8,128)(2,1)S(1)} collective-permute-done((bf16[16,128,128]{2,1,0:T(8,128)(2,1)S(1)}, bf16[16,128,128]{2,1,0:T(8,128)(2,1)S(1)}, u32[]{:S(2)}, u32[]{:S(2)}) %collective-permute-start) | collective-permute-done | bytes 524320 | tf_op jit(solution)/shard_map/ppermute | solution.py:240
  58.5 0.0 copy-done.1
  58.5 1.9 %copy-done.2 = bf16[4096,3,128]{2,0,1:T(8,128)(2,1)S(1)} copy-done((bf16[4096,3,128]{2,0,1:T(8,128)(2,1)S(1)}, bf16[4096,3,128]{2,0,1:T(8,128)(2,1)}, u32[]{:S(2)}) %copy-start.2) | copy-done | bytes 3145752
  60.4 2.2 %project.1 = (f32[128,128]{1,0:T(8,128)S(1)}, f32[128,128]{1,0:T(8,128)S(1)}) custom-call(s32[2]{0:T(128)S(1)} %pad_add_fusion.where_ref, s32[512]{0:T(512)S(1)} %copy-done.6, f32[1]{0:T(128)S(6)} %copy.22.decay_ref, bf16[16,128,128]{2,1,0:T(8,128)(2,1)S(1)} %all-gather.1.own_ref, bf16[16,128,128]{2,1,0:T(8,128)(2,1)S(1)} %collective-permute-done.other_ref, ...), custom_call_target="tpu_custom_call" | custom-call | flops 402653184 | bytes 6291456 | tf_op jit(solution)/shard_map/project/pallas_call | solution.py:241
  62.6 13.0 %all-to-all-done.1.incoming_ref = bf16[20,128,128]{2,1,0:T(8,128)(2,1)} async-done(((bf16[20,128,128]{2,1,0:T(8,128)(2,1)}), bf16[20,128,128]{2,1,0:T(8,128)(2,1)}, u32[]{:S(2)}, u32[]{:S(2)}) %all-to-all-start.1) | async-done | bytes 655392 | tf_op jit(solution)/shard_map/all_to_all | solution.py:236
  75.6 0.0 copy-done.8
  75.6 0.0 copy-done.9
  75.6 1.2 %copy-done.4 = bf16[128,4096]{1,0:T(8,128)(2,1)S(1)} copy-done((bf16[128,4096]{1,0:T(8,128)(2,1)S(1)}, bf16[128,4096]{1,0:T(8,128)(2,1)}, u32[]{:S(2)}) %copy-start.4) | copy-done | bytes 1048600
  76.9 2.6 %finish.1 = (f32[16,128,128]{2,1,0:T(8,128)S(1)}, bf16[16,128,128]{2,1,0:T(8,128)(2,1)S(1)}) custom-call(s32[2]{0:T(128)S(1)} %pad_add_fusion.where_ref, s32[512]{0:T(512)S(1)} %copy-done.6, s32[512]{0:T(512)S(1)} %copy-done.8, f32[1]{0:T(128)S(6)} %copy.22.decay_ref, f32[128,128]{1,0:T(8,128)S(1)} %get-tuple-element.12.query_ref, ...), custom_call_target="tpu_custom_call" | custom-call | flops 134217728 | bytes 4194304 | tf_op jit(solution)/shard_map/finish/pallas_call | solution.py:253
  79.5 1.9 %collective-permute-start.1 = (bf16[16,128,128]{2,1,0:T(8,128)(2,1)S(1)}, bf16[16,128,128]{2,1,0:T(8,128)(2,1)S(1)}, u32[]{:S(2)}, u32[]{:S(2)}) collective-permute-start(bf16[16,128,128]{2,1,0:T(8,128)(2,1)S(1)} %get-tuple-element.16), channel_id=1, source_target_pairs={{0,1},{1,0},{2,3},{3,2},{4,5},{5,4},{6,7},{7,6},{8,9},{9,8},{10,11... | collective-permute-start | bytes 1572872 | tf_op jit(solution)/shard_map/ppermute | solution.py:277
  81.4 1.9 %collective-permute-done.1 = bf16[16,128,128]{2,1,0:T(8,128)(2,1)S(1)} collective-permute-done((bf16[16,128,128]{2,1,0:T(8,128)(2,1)S(1)}, bf16[16,128,128]{2,1,0:T(8,128)(2,1)S(1)}, u32[]{:S(2)}, u32[]{:S(2)}) %collective-permute-start.1) | collective-permute-done | bytes 524320 | tf_op jit(solution)/shard_map/ppermute | solution.py:277
  83.3 0.1 add_convert_fusion
  83.4 13.9 %all_to_all.20 = bf16[4,4,128,128]{3,2,1,0:T(8,128)(2,1)S(1)} all-to-all(bf16[4,4,128,128]{3,2,1,0:T(8,128)(2,1)S(1)} %bitcast.28), channel_id=1, replica_groups={{0,8,16,24},{1,9,17,25},{2,10,18,26},{3,11,19,27},{4,12,20,28},{5,13,21..., dimensions={0} | all-to-all | bytes 1048576 | tf_op jit(solution)/shard_map/all_to_all | solution.py:279
  97.3 0.1 reduce_sum.77
  97.4 8.7 %all_to_all.21 = bf16[4,128,128]{2,1,0:T(8,128)(2,1)S(1)} all-to-all(bf16[4,128,128]{2,1,0:T(8,128)(2,1)S(1)} %reduce_sum.77), channel_id=1, replica_groups={{0,2,4,6},{1,3,5,7},{8,10,12,14},{9,11,13,15},{16,18,20,22},{17,19,21,2..., dimensions={0} | all-to-all | bytes 262144 | tf_op jit(solution)/shard_map/all_to_all | solution.py:281
  106.1 0.6 reduce_sum.78
  (12 shorter events, 0.1 us)
Async XLA Ops:
  0.0 10.2 %copy-start.6 = (s32[512]{0:T(512)S(1)}, s32[512]{0:T(512)}, u32[]{:S(2)}) copy-start(s32[512]{0:T(512)} %plan_ref.3) | copy-start | bytes 6148
  1.6 1.6 %copy-start = (f32[32,1,128,128]{3,2,1,0:T(8,128)S(1)}, f32[32,1,128,128]{3,2,1,0:T(8,128)}, u32[]{:S(2)}) copy-start(f32[32,1,128,128]{3,2,1,0:T(8,128)} %param.13) | copy-start | bytes 6291460
  3.2 0.8 copy-start.7
  4.6 1.0 copy-start.5
  5.6 52.9 %copy-start.1 = (f32[32,1,128,128]{3,2,1,0:T(8,128)S(1)}, f32[32,1,128,128]{3,2,1,0:T(8,128)}, u32[]{:S(2)}) copy-start(f32[32,1,128,128]{3,2,1,0:T(8,128)} %param.13) | copy-start | bytes 6291460
  5.6 19.7 %all-to-all-start = ((bf16[32,128,128]{2,1,0:T(8,128)(2,1)}), bf16[32,128,128]{2,1,0:T(8,128)(2,1)S(1)}, u32[]{:S(2)}, u32[]{:S(2)}) async-start(bf16[32,128,128]{2,1,0:T(8,128)(2,1)} %copy-done.5), calls=%async_computation | async-start | bytes 2097152 | tf_op jit(solution)/shard_map/all_to_all | solution.py:226
  26.0 0.9 copy-start.3
  26.8 48.8 %all-to-all-start.1 = ((bf16[20,128,128]{2,1,0:T(8,128)(2,1)}), bf16[20,128,128]{2,1,0:T(8,128)(2,1)}, u32[]{:S(2)}, u32[]{:S(2)}) async-start(bf16[20,128,128]{2,1,0:T(8,128)(2,1)} %copy-done.3), calls=%async_computation.1 | async-start | bytes 1310720 | tf_op jit(solution)/shard_map/all_to_all | solution.py:236
  54.7 3.8 %collective-permute-start = (bf16[16,128,128]{2,1,0:T(8,128)(2,1)S(1)}, bf16[16,128,128]{2,1,0:T(8,128)(2,1)S(1)}, u32[]{:S(2)}, u32[]{:S(2)}) collective-permute-start(bf16[16,128,128]{2,1,0:T(8,128)(2,1)S(1)} %all-gather.1.own_ref), channel_id=1, source_target_pairs={{0,1},{1,0},{2,3},{3,2},{4,5},{5,4},{6,7},{7,6},{8,9},{9,8},{10,11... | collective-permute-start | bytes 1572872 | tf_op jit(solution)/shard_map/ppermute | solution.py:240
  58.5 1.9 %copy-start.2 = (bf16[4096,3,128]{2,0,1:T(8,128)(2,1)S(1)}, bf16[4096,3,128]{2,0,1:T(8,128)(2,1)}, u32[]{:S(2)}) copy-start(bf16[4096,3,128]{2,0,1:T(8,128)(2,1)} %param.9) | copy-start | bytes 9437188
  60.4 15.2 %copy-start.8 = (s32[512]{0:T(512)S(1)}, s32[512]{0:T(512)}, u32[]{:S(2)}) copy-start(s32[512]{0:T(512)} %remaining_ref.1) | copy-start | bytes 6148
  60.4 15.2 %copy-start.9 = (f32[128]{0:T(128)S(1)}, f32[128]{0:T(128)}, u32[]{:S(2)}) copy-start(f32[128]{0:T(128)} %param.11) | copy-start | bytes 1540
  75.6 1.2 %copy-start.4 = (bf16[128,4096]{1,0:T(8,128)(2,1)S(1)}, bf16[128,4096]{1,0:T(8,128)(2,1)}, u32[]{:S(2)}) copy-start(bf16[128,4096]{1,0:T(8,128)(2,1)} %weight_ref.1) | copy-start | bytes 3145732
  79.5 3.8 %collective-permute-start.1 = (bf16[16,128,128]{2,1,0:T(8,128)(2,1)S(1)}, bf16[16,128,128]{2,1,0:T(8,128)(2,1)S(1)}, u32[]{:S(2)}, u32[]{:S(2)}) collective-permute-start(bf16[16,128,128]{2,1,0:T(8,128)(2,1)S(1)} %get-tuple-element.16), channel_id=1, source_target_pairs={{0,1},{1,0},{2,3},{3,2},{4,5},{5,4},{6,7},{7,6},{8,9},{9,8},{10,11... | collective-permute-start | bytes 1572872 | tf_op jit(solution)/shard_map/ppermute | solution.py:277

commit v4 on v3

v4 whole, which is shorter than its diff:
```python
import functools

import jax
import jax.numpy as jnp
from jax import lax
from jax.experimental import pallas as pl
from jax.experimental.pallas import tpu as pltpu
from jax.sharding import PartitionSpec as P

STEPS = 4
SIZE = 128
MOVED = 13
XS, ZS, CORES = 4, 4, 2
CHIPS = XS * ZS
ZH, YS = 4, 4
SLOTS = 2
CODE = 64
PASSING = 5


def tensor_id(x, z, c):
    return (x * ZS + z) * CORES + c


SPOTS = [(x, z, c) for x in range(XS) for z in range(ZS) for c in range(CORES)]
Z_LINES = [[tensor_id(x, z, c) for z in range(ZS)] for x in range(XS) for c in range(CORES)]
X_RINGS = [[tensor_id(x, z, c) for x in range(XS)] for z in range(ZS) for c in range(CORES)]
CORE_SWAP = [(tensor_id(x, z, c), tensor_id(x, z, 1 - c)) for x, z, c in SPOTS]
X_SHIFTS = [
    [(tensor_id(x, z, c), tensor_id((x + k) % XS, z, c)) for x, z, c in SPOTS] for k in range(XS)
]
Y_RINGS = [[z * YS + y for y in range(YS)] for z in range(ZH)]
Z_RINGS = [[z * YS + y for z in range(ZH)] for y in range(YS)]

VMEM = pl.BlockSpec(memory_space=pltpu.VMEM)
SMEM = pl.BlockSpec(memory_space=pltpu.SMEM)
ANY = pl.BlockSpec(memory_space=pl.ANY)
SMALL = pltpu.CompilerParams(vmem_limit_bytes=16 * 2**20)
ROOMY = pltpu.CompilerParams(vmem_limit_bytes=56 * 2**20)
DMA = pltpu.SemaphoreType.DMA


def after_kernel(x_ref, dep_ref, out_ref):
    pass


def after(x, dep):
    return pl.pallas_call(
        after_kernel,
        out_shape=jax.ShapeDtypeStruct(x.shape, x.dtype),
        in_specs=[ANY, ANY],
        out_specs=ANY,
        input_output_aliases={0: 0},
        name="after",
    )(x, dep)


def targets(migration_plan, own_group, rows):
    wanted = migration_plan[None, :] == (own_group * rows + jnp.arange(rows))[:, None]
    return jnp.sum(jnp.where(wanted, jnp.arange(migration_plan.shape[0])[None, :], 0), axis=1)


def rows_on(migration_plan, own_group, groups, rows):
    plan = migration_plan.reshape(ZH, YS, rows)
    plan = lax.dynamic_index_in_dim(plan, own_group % YS, axis=1, keepdims=False)
    source = plan // rows
    target = jnp.arange(ZH) * YS + own_group % YS
    passing = (source // YS == own_group // YS) & (source != target[:, None])
    before = jnp.arange(rows)[None, :] < jnp.arange(rows)[:, None]
    order = jnp.sum((passing[:, None, :] & before).astype(jnp.int32), axis=-1)
    same = source[:, :, None] == source[:, None, :]
    slot = jnp.sum((same & (plan[:, None, :] < plan[:, :, None])).astype(jnp.int32), axis=-1)
    place = (source % YS) * (ZH * SLOTS) + jnp.arange(ZH)[:, None] * SLOTS + slot
    wanted = passing[:, None, :] & (order[:, None, :] == jnp.arange(PASSING)[None, :, None])
    place = jnp.sum(jnp.where(wanted, place[:, None, :], 0), axis=-1)
    return jnp.clip(place, 0, groups * SLOTS - 1).reshape(-1)


def pack_kernel(
    rows, target_ref, states_ref, inputs_ref, out_ref, same_ref,
    wide_ref, narrow_ref, inputs_vmem, slot_ref, seen_ref, in_sem, out_sem, copy_sem,
):
    group = group_here()
    load = pltpu.make_async_copy(inputs_ref, inputs_vmem, copy_sem.at[0])
    load.start()
    for i in range(ZH * YS):
        seen_ref[i] = 0

    def scan(row, count):
        goal = target_ref[row] // rows
        leaves = (goal != group) & (count < MOVED)

        @pl.when(leaves)
        def _():
            rank = seen_ref[goal]
            seen_ref[goal] = rank + 1
            slot_ref[count] = (
                (goal % YS) * (ZH * SLOTS) + goal // YS * SLOTS + jnp.minimum(rank, SLOTS - 1)
            )
            pltpu.make_async_copy(
                states_ref.at[row], wide_ref.at[count], in_sem.at[count]
            ).start()

        return count + leaves.astype(jnp.int32)

    count = lax.fori_loop(0, rows, scan, jnp.int32(0), unroll=8)
    load.wait()
    store = pltpu.make_async_copy(inputs_vmem, same_ref, copy_sem.at[1])
    store.start()
    for i in range(MOVED):

        @pl.when(i < count)
        def _(i=i):
            pltpu.make_async_copy(states_ref.at[0], wide_ref.at[i], in_sem.at[i]).wait()
            narrow_ref[i] = wide_ref[i].astype(jnp.bfloat16)
            pltpu.make_async_copy(
                narrow_ref.at[i], out_ref.at[slot_ref[i]], out_sem.at[i]
            ).start()

    for i in range(MOVED):

        @pl.when(i < count)
        def _(i=i):
            pltpu.make_async_copy(narrow_ref.at[i], out_ref.at[0], out_sem.at[i]).wait()

    store.wait()


def pass_kernel(index_ref, rows_ref, dep_ref, out_ref, sem):
    copies = [
        pltpu.make_async_copy(rows_ref.at[index_ref[i]], out_ref.at[i], sem.at[i])
        for i in range(out_ref.shape[0])
    ]
    for copy in copies:
        copy.start()
    for copy in copies:
        copy.wait()


def group_here():
    return lax.axis_index("group")


def core_here():
    return lax.rem(lax.axis_index("tensor"), CORES)


def x_here():
    return lax.div(lax.axis_index("tensor"), CORES * ZS)


def deal_kernel(weight_ref, dep_ref, *out_refs):
    x = x_here()
    width = weight_ref.shape[1] // XS
    for k in range(XS):
        start = pl.multiple_of(lax.rem(x + k, XS) * width, width)
        out_refs[k][...] = weight_ref[:, pl.ds(start, width)]


def split_rows(q):
    high = q.astype(jnp.bfloat16)
    low = (q - high.astype(jnp.float32)).astype(jnp.bfloat16)
    return jnp.concatenate([high, low], axis=0)


def project_kernel(
    rows, plan_ref, remaining_ref, decay_ref, gain_ref, own_ref, other_ref, weight_ref,
    states_ref, scaled_ref, partial_ref, gains_ref, code_ref, query_ref, kept_ref, active_ref,
    seen_ref,
):
    group, core = group_here(), core_here()
    count = STEPS * rows
    for i in range(ZH):
        seen_ref[i] = 0
    for i in range(code_ref.shape[0]):
        code_ref[i] = rows * CODE
    found = jnp.int32(0)
    for row in range(rows):
        source = plan_ref[group * rows + row]
        source_group = source // rows
        moved = (source_group != group) & (found < MOVED)
        far = source_group // YS
        rank = seen_ref[far]
        slot = far * PASSING + jnp.minimum(rank, PASSING - 1)
        step = moved.astype(jnp.int32)
        seen_ref[far] = rank + step
        code_ref[found] = jnp.where(moved, row * CODE + slot, rows * CODE)
        found = found + step
        active_ref[row : row + 1, :] = jnp.full((1, SIZE), remaining_ref[source], jnp.int32)
    acc = [jnp.zeros((count, SIZE), jnp.float32) for _ in range(3)]
    for chip in range(CHIPS):
        a, b = own_ref[chip], other_ref[chip]
        even = jnp.where(core == 0, a, b)
        odd = jnp.where(core == 0, b, a)
        both = jnp.concatenate([even, odd], axis=1)
        for i in range(3):
            weight = weight_ref[i, 2 * SIZE * chip : 2 * SIZE * (chip + 1), :]
            acc[i] += jnp.dot(both, weight, preferred_element_type=jnp.float32)
    query = acc[0] / (1.0 + jnp.exp(-acc[0]))
    key = acc[1] / (1.0 + jnp.exp(-acc[1]))
    value = acc[2]
    query_ref[...] = query
    for row in range(rows):
        source = plan_ref[group * rows + row]
        state = states_ref[source % rows]
        high = state.astype(jnp.bfloat16)
        low = (state - high.astype(jnp.float32)).astype(jnp.bfloat16)
        mine = query_ref[pl.ds(row, STEPS, stride=rows), :]
        pair = split_rows(mine)
        first = jnp.dot(pair, high, preferred_element_type=jnp.float32)
        second = jnp.dot(pair[:STEPS], low, preferred_element_type=jnp.float32)
        product = first[:STEPS] + first[STEPS:] + second
        stays = (source // rows == group).astype(jnp.float32)
        kept_ref[pl.ds(row, STEPS, stride=rows), :] = product * stays
    decay = decay_ref[0]
    at = lambda x, t: x[t * rows : (t + 1) * rows]
    power = decay
    for t in range(STEPS):
        here = slice(t * rows, (t + 1) * rows)
        scaled_ref[here] = power * at(query, t)
        readout = power * kept_ref[here]
        power = power * decay
        weight = jnp.float32(1.0)
        for s in range(t, -1, -1):
            score = jnp.sum(at(query, t) * at(key, s), axis=-1, keepdims=True)
            readout = readout + (weight * score) * at(value, s)
            weight = weight * decay
        partial_ref[here] = readout
        gains_ref[here] = jnp.where(active_ref[...] > t, gain_ref[...], 0.0)


def finish_kernel(
    rows, code_ref, scaled_ref, partial_ref, gains_ref, incoming_ref, normed_ref, moved_ref
):
    room = moved_ref.shape[0] // STEPS
    moved_ref[...] = jnp.zeros_like(moved_ref)
    for i in range(MOVED):
        row = lax.div(code_ref[i], CODE)
        mine = scaled_ref[pl.ds(jnp.minimum(row, rows - 1), STEPS, stride=rows), :]
        state = incoming_ref[lax.rem(code_ref[i], CODE)]
        product = jnp.dot(split_rows(mine), state, preferred_element_type=jnp.float32)
        moved_ref[pl.ds(row, STEPS, stride=room), :] = product[:STEPS] + product[STEPS:]
    for t in range(STEPS):
        here = slice(t * rows, (t + 1) * rows)
        readout = partial_ref[here] + moved_ref[t * room : t * room + rows]
        norm = lax.rsqrt(jnp.mean(readout * readout, axis=-1, keepdims=True) + 1e-05)
        normed_ref[here] = (readout * norm * gains_ref[here]).astype(jnp.bfloat16)


def output_kernel(ring_ref, *refs):
    weights, (own_ref, other_ref) = refs[:XS], refs[XS:]
    core, x = core_here(), x_here()
    rows = [ring_ref[lax.rem(x + XS - k, XS)] for k in range(XS)]
    pairs = [
        (jnp.concatenate(rows[k : k + 2], axis=1), weights[k], weights[k + 1])
        for k in range(0, XS, 2)
    ]
    width = CORES * SIZE
    for z in range(ZS):
        part = slice(z * width, (z + 1) * width)
        total = 0.0
        for both, first, second in pairs:
            weight = jnp.concatenate([first[:, part], second[:, part]], axis=0)
            total = total + jnp.dot(both, weight, preferred_element_type=jnp.float32)
        even, odd = total[:, :SIZE], total[:, SIZE:]
        own_ref[z] = jnp.where(core == 0, even, odd)
        other_ref[z] = jnp.where(core == 0, odd, even).astype(jnp.bfloat16)


def body(
    step_inputs,
    qkv_weight,
    out_weight,
    head_gain,
    head_decay,
    states_in,
    remaining_steps,
    migration_plan,
):
    rows = states_in.shape[0]
    count = STEPS * rows
    groups = lax.axis_size("group")
    own_group = lax.axis_index("group")
    states = states_in.reshape(rows, SIZE, SIZE)
    bf16, f32 = jnp.bfloat16, jnp.float32

    outgoing, inputs = pl.pallas_call(
        functools.partial(pack_kernel, rows),
        out_shape=[
            jax.ShapeDtypeStruct((groups * SLOTS, SIZE, SIZE), bf16),
            jax.ShapeDtypeStruct((count, SIZE), bf16),
        ],
        in_specs=[SMEM, ANY, ANY],
        out_specs=[ANY, ANY],
        scratch_shapes=[
            pltpu.VMEM((MOVED, SIZE, SIZE), f32),
            pltpu.VMEM((MOVED, SIZE, SIZE), bf16),
            pltpu.VMEM((count, SIZE), bf16),
            pltpu.SMEM((MOVED,), jnp.int32),
            pltpu.SMEM((ZH * YS,), jnp.int32),
            DMA((MOVED,)),
            DMA((MOVED,)),
            DMA((2,)),
        ],
        compiler_params=ROOMY,
        name="pack",
    )(targets(migration_plan, own_group, rows), states, step_inputs.reshape(count, SIZE))
    passing = lax.all_to_all(outgoing, "group", 0, 0, tiled=True, axis_index_groups=Y_RINGS)
    line = lax.all_gather(inputs, "tensor", axis=0, axis_index_groups=Z_LINES)
    passing = pl.pallas_call(
        pass_kernel,
        out_shape=jax.ShapeDtypeStruct((ZH * PASSING, SIZE, SIZE), bf16),
        in_specs=[SMEM, VMEM, ANY],
        out_specs=ANY,
        scratch_shapes=[DMA((ZH * PASSING,))],
        compiler_params=SMALL,
        name="pass_on",
    )(rows_on(migration_plan, own_group, groups, rows), passing, line)
    incoming = lax.all_to_all(passing, "group", 0, 0, tiled=True, axis_index_groups=Z_RINGS)

    plane = lax.all_gather(after(line, passing), "tensor", axis=0, axis_index_groups=X_RINGS)
    plane = plane.reshape(CHIPS, count, SIZE)
    other = lax.ppermute(plane, "tensor", CORE_SWAP)
    scaled, partial, gains, code = pl.pallas_call(
        functools.partial(project_kernel, rows),
        out_shape=[
            jax.ShapeDtypeStruct((count, SIZE), f32),
            jax.ShapeDtypeStruct((count, SIZE), f32),
            jax.ShapeDtypeStruct((count, SIZE), f32),
            jax.ShapeDtypeStruct((MOVED + 1,), jnp.int32),
        ],
        in_specs=[SMEM, SMEM, SMEM, VMEM, VMEM, VMEM, VMEM, VMEM],
        out_specs=[VMEM, VMEM, VMEM, SMEM],
        scratch_shapes=[
            pltpu.VMEM((count, SIZE), f32),
            pltpu.VMEM((count, SIZE), f32),
            pltpu.VMEM((rows, SIZE), jnp.int32),
            pltpu.SMEM((ZH,), jnp.int32),
        ],
        compiler_params=pltpu.CompilerParams(vmem_limit_bytes=24 * 2**20),
        cost_estimate=pl.CostEstimate(
            flops=2 * count * 4096 * 384, bytes_accessed=6 * 2**20, transcendentals=0
        ),
        name="project",
    )(
        migration_plan, remaining_steps, head_decay, head_gain.reshape(1, SIZE), plane, other,
        jnp.transpose(qkv_weight, (1, 0, 2)), states,
    )

    dealt = pl.pallas_call(
        deal_kernel,
        out_shape=[jax.ShapeDtypeStruct((SIZE, out_weight.shape[1] // XS), bf16)] * XS,
        in_specs=[VMEM, ANY],
        out_specs=[VMEM] * XS,
        compiler_params=SMALL,
        name="deal",
    )(out_weight, plane)
    dealt = [dealt[0]] + [lax.ppermute(dealt[k], "tensor", X_SHIFTS[k]) for k in range(1, XS)]

    normed = pl.pallas_call(
        functools.partial(finish_kernel, rows),
        out_shape=jax.ShapeDtypeStruct((count, SIZE), bf16),
        in_specs=[SMEM, VMEM, VMEM, VMEM, VMEM],
        out_specs=VMEM,
        scratch_shapes=[pltpu.VMEM((STEPS * (rows + 8), SIZE), f32)],
        compiler_params=SMALL,
        name="finish",
    )(code, scaled, partial, gains, incoming)
    ring = lax.all_gather(normed, "tensor", axis=0, axis_index_groups=X_RINGS)
    own, away = pl.pallas_call(
        output_kernel,
        out_shape=[
            jax.ShapeDtypeStruct((ZS, count, SIZE), f32),
            jax.ShapeDtypeStruct((ZS, count, SIZE), bf16),
        ],
        in_specs=[VMEM] * (1 + XS),
        out_specs=[VMEM, VMEM],
        compiler_params=SMALL,
        name="output",
    )(ring, *dealt)
    received = lax.ppermute(away, "tensor", CORE_SWAP)
    sums = (own + received.astype(f32)).astype(bf16)
    pieces = lax.all_to_all(sums, "tensor", 0, 0, tiled=True, axis_index_groups=Z_LINES)
    result = jnp.sum(pieces.astype(f32), axis=0).astype(bf16)
    return result.reshape(STEPS, rows, SIZE)


def solution(mesh):
    placed = (
        P(None, "group", "tensor"),
        P(None, None, "tensor"),
        P("tensor", None),
        P("tensor"),
        P("tensor"),
        P("group", "tensor", None, None),
        P(),
        P(),
    )
    return jax.shard_map(
        body, mesh=mesh, in_specs=placed, out_specs=P(None, "group", "tensor"), check_vma=False
    )
```

time: 107 us -> 103 us (0.963)
  the two profiles are of different devices: /device:TPU:32 before, /device:TPU:16 now
where the time goes in v4:
time: 103 us
  blocking collectives  48.5 us (47%)
  starting transfers between devices  33.7 us (33%)
  Pallas kernels  10.6 us (10%)
  local copies, waits for them, and re-layouts  3.4 us (3%)
  other arithmetic  2.89 us (3%)
  waiting for transfers between devices  2.76 us (3%)
    all_gather x1, blocking collectives, body(): lax.all_gather(after(line, passing), 'tensor', axis=0, axis_index_groups=...  13.7 us
    all_gather x1, blocking collectives, body(): line = lax.all_gather(inputs, 'tensor', axis=0, axis_index_groups=Z_LINES)  13.6 us
    all_gather x1, blocking collectives, body(): ring = lax.all_gather(normed, 'tensor', axis=0, axis_index_groups=X_RINGS)  12.3 us
    all_to_all x1, starting transfers between devices, body(): lax.all_to_all(passing, 'group', 0, 0, tiled=True, axis_index_groups=Z_RI...  10.8 us
    ppermute x3, starting transfers between devices, body(): lax.ppermute(dealt[k], 'tensor', X_SHIFTS[k])  9.81 us
    all_to_all x1, starting transfers between devices, body(): lax.all_to_all(outgoing, 'group', 0, 0, tiled=True, axis_index_groups=Y_R...  9.26 us
    all_to_all x1, blocking collectives, body(): lax.all_to_all(sums, 'tensor', 0, 0, tiled=True, axis_index_groups=Z_LINES)  8.81 us
    unnamed x15, local copies, waits for them, and re-layouts  3.14 us
  transfers between devices with their start and end apart: 7, of which 2 were waited for; matrix products, arithmetic and copies ran while one was open for 1% of the time, Pallas kernels for 5%

profile of v4, /device:TPU:16, one launch (start us, length us, event | category | flops | bytes accessed | tf_op | source)
XLA Modules:
  0.0 102.7 jit_solution(9722739354737035319)
XLA Ops:
  0.0 0.0 copy-start.4
  0.0 1.5 %select_reduce_fusion.target_ref = s32[32]{0:T(128)} fusion(s32[512]{0:T(512)} %plan_ref.1, s32[32]{0:T(128)S(1)} %iota_add_fusion), kind=kLoop, calls=%fused_computation.3 | loop fusion | flops 49120 | bytes 2304 | tf_op jit(solution)/shard_map/reduce_sum | solution.py:60
  1.5 3.0 %pack.1 = (bf16[32,128,128]{2,1,0:T(8,128)(2,1)}, bf16[128,128]{1,0:T(8,128)(2,1)}) custom-call(s32[32]{0:T(128)} %select_reduce_fusion.target_ref, f32[32,128,128]{2,1,0:T(8,128)} %bitcast.16, bf16[128,128]{1,0:T(8,128)(2,1)} %bitcast.23), custom_call_target="tpu_custom_call" | custom-call | tf_op jit(solution)/shard_map/pack/pallas_call | solution.py:287
  4.4 9.3 %all-to-all-start = ((bf16[32,128,128]{2,1,0:T(8,128)(2,1)}), bf16[32,128,128]{2,1,0:T(8,128)(2,1)S(1)}, u32[]{:S(2)}, u32[]{:S(2)}) async-start(bf16[32,128,128]{2,1,0:T(8,128)(2,1)} %get-tuple-element.18), calls=%async_computation | async-start | bytes 2097152 | tf_op jit(solution)/shard_map/all_to_all | solution.py:308
  13.7 0.0 copy-done.4
  13.7 0.1 reshape.97
  13.8 0.1 compare_and_fusion
  13.9 0.1 convert_reduce_fusion.1
  14.1 0.2 convert_reduce_fusion
  14.3 0.1 fusion.4
  14.4 0.2 select_reduce_fusion.1
  14.6 0.1 copy.14
  14.7 0.1 min.12.index_ref
  14.8 13.6 %all-gather = bf16[512,128]{1,0:T(8,128)(2,1)S(1)} all-gather(bf16[128,128]{1,0:T(8,128)(2,1)} %get-tuple-element.17), channel_id=2, replica_groups={{0,2,4,6},{1,3,5,7},{8,10,12,14},{9,11,13,15},{16,18,20,22},{17,19,21,2..., dimensions={0}, use_global_device_ids=true | all-gather | bytes 163840 | tf_op jit(solution)/shard_map/all_gather | solution.py:309
  28.3 0.0 copy-start.2
  28.3 0.0 all-to-all-done.rows_ref
  28.3 0.0 copy-start
  28.4 0.0 copy-start.5
  28.4 0.0 copy-start.6
  28.4 1.5 %pass_on.1.dep_ref = bf16[20,128,128]{2,1,0:T(8,128)(2,1)} custom-call(s32[20]{0:T(128)S(1)} %min.12.index_ref, bf16[32,128,128]{2,1,0:T(8,128)(2,1)S(1)} %all-to-all-done.rows_ref, bf16[4,128,128]{2,1,0:T(8,128)(2,1)S(1)} %bitcast.19), custom_call_target="tpu_custom_call" | custom-call | tf_op jit(solution)/shard_map/pass_on/pallas_call | solution.py:310
  29.9 10.8 %all-to-all-start.1 = ((bf16[20,128,128]{2,1,0:T(8,128)(2,1)}), bf16[20,128,128]{2,1,0:T(8,128)(2,1)S(1)}, u32[]{:S(2)}, u32[]{:S(2)}) async-start(bf16[20,128,128]{2,1,0:T(8,128)(2,1)} %pass_on.1.dep_ref), calls=%async_computation.1 | async-start | bytes 1310720 | tf_op jit(solution)/shard_map/all_to_all | solution.py:319
  40.7 0.0 copy-done.2
  40.7 13.7 %all-gather.1.own_ref.dep_ref = bf16[16,128,128]{2,1,0:T(8,128)(2,1)S(1)} all-gather(bf16[4,128,128]{2,1,0:T(8,128)(2,1)} %after.1), channel_id=3, replica_groups={{0,8,16,24},{1,9,17,25},{2,10,18,26},{3,11,19,27},{4,12,20,28},{5,13,21..., dimensions={0}, use_global_device_ids=true | all-gather | bytes 655360 | tf_op jit(solution)/shard_map/all_gather | solution.py:321
  54.5 1.9 %collective-permute-start = (bf16[16,128,128]{2,1,0:T(8,128)(2,1)S(1)}, bf16[16,128,128]{2,1,0:T(8,128)(2,1)S(1)}, u32[]{:S(2)}, u32[]{:S(2)}) collective-permute-start(bf16[16,128,128]{2,1,0:T(8,128)(2,1)S(1)} %all-gather.1.own_ref.dep_ref), channel_id=1, source_target_pairs={{0,1},{1,0},{2,3},{3,2},{4,5},{5,4},{6,7},{7,6},{8,9},{9,8},{10,11... | collective-permute-start | bytes 1572872 | tf_op jit(solution)/shard_map/ppermute | solution.py:323
  56.4 0.0 copy-start.3
  56.4 1.2 %copy-done.3 = bf16[128,4096]{1,0:T(8,128)(2,1)S(1)} copy-done((bf16[128,4096]{1,0:T(8,128)(2,1)S(1)}, bf16[128,4096]{1,0:T(8,128)(2,1)}, u32[]{:S(2)}) %copy-start.3) | copy-done | bytes 1048600
  57.6 1.0 deal.1
  58.6 3.1 %collective-permute-start.1 = (bf16[128,1024]{1,0:T(8,128)(2,1)}, bf16[128,1024]{1,0:T(8,128)(2,1)}, u32[]{:S(2)}, u32[]{:S(2)}) collective-permute-start(bf16[128,1024]{1,0:T(8,128)(2,1)} %get-tuple-element.24), channel_id=1, source_target_pairs={{0,8},{1,9},{2,10},{3,11},{4,12},{5,13},{6,14},{7,15},{8,16},{9,17... | collective-permute-start | bytes 786440 | tf_op jit(solution)/shard_map/ppermute | solution.py:358
  61.7 4.6 %collective-permute-start.2 = (bf16[128,1024]{1,0:T(8,128)(2,1)}, bf16[128,1024]{1,0:T(8,128)(2,1)}, u32[]{:S(2)}, u32[]{:S(2)}) collective-permute-start(bf16[128,1024]{1,0:T(8,128)(2,1)} %get-tuple-element.25), channel_id=1, source_target_pairs={{0,16},{1,17},{2,18},{3,19},{4,20},{5,21},{6,22},{7,23},{8,24},{9,... | collective-permute-start | bytes 786440 | tf_op jit(solution)/shard_map/ppermute | solution.py:358
  66.3 2.1 %collective-permute-start.3 = (bf16[128,1024]{1,0:T(8,128)(2,1)}, bf16[128,1024]{1,0:T(8,128)(2,1)}, u32[]{:S(2)}, u32[]{:S(2)}) collective-permute-start(bf16[128,1024]{1,0:T(8,128)(2,1)} %get-tuple-element.26), channel_id=1, source_target_pairs={{0,24},{1,25},{2,26},{3,27},{4,28},{5,29},{6,30},{7,31},{8,0},{9,1... | collective-permute-start | bytes 786440 | tf_op jit(solution)/shard_map/ppermute | solution.py:358
  69.1 0.0 collective-permute-done.other_ref
  69.1 0.0 copy-done
  69.1 0.0 copy-done.5
  69.1 0.0 copy-done.6
  69.1 0.0 copy-start.1
  69.1 1.9 %copy-done.1 = bf16[4096,3,128]{2,0,1:T(8,128)(2,1)S(1)} copy-done((bf16[4096,3,128]{2,0,1:T(8,128)(2,1)S(1)}, bf16[4096,3,128]{2,0,1:T(8,128)(2,1)}, u32[]{:S(2)}) %copy-start.1) | copy-done | bytes 3145752
  71.0 2.8 %project.1 = (f32[128,128]{1,0:T(8,128)S(1)}, f32[128,128]{1,0:T(8,128)S(1)}, f32[128,128]{1,0:T(8,128)S(1)}, s32[14]{0:T(128)S(1)}) custom-call(s32[512]{0:T(512)S(1)} %copy-done.4, s32[512]{0:T(512)S(1)} %copy-done.5, f32[1]{0:T(128)S(6)} %copy.19.decay_ref, f32[1,128]{1,0:T(1,128)S(1)} %bitcast.22, bf16[16,128,128]{2,1,0:T(8,128)(2,1)S(1)} %all-gather.1.own_ref.dep_ref, ...), custom_call_target="tpu_custom_call" | custom-call | flops 402653184 | bytes 6291456 | tf_op jit(solution)/shard_map/project/pallas_call | solution.py:324
  73.9 1.4 %all-to-all-done.1.incoming_ref = bf16[20,128,128]{2,1,0:T(8,128)(2,1)S(1)} async-done(((bf16[20,128,128]{2,1,0:T(8,128)(2,1)}), bf16[20,128,128]{2,1,0:T(8,128)(2,1)S(1)}, u32[]{:S(2)}, u32[]{:S(2)}) %all-to-all-start.1) | async-done | bytes 655392 | tf_op jit(solution)/shard_map/all_to_all | solution.py:319
  75.3 0.9 finish.1
  76.2 12.3 %all-gather.2 = bf16[512,128]{1,0:T(8,128)(2,1)S(1)} all-gather(bf16[128,128]{1,0:T(8,128)(2,1)S(1)} %finish.1), channel_id=4, replica_groups={{0,8,16,24},{1,9,17,25},{2,10,18,26},{3,11,19,27},{4,12,20,28},{5,13,21..., dimensions={0}, use_global_device_ids=true | all-gather | bytes 163840 | tf_op jit(solution)/shard_map/all_gather | solution.py:369
  88.5 0.0 collective-permute-done.1.refs_1_
  88.5 0.0 collective-permute-done.2.refs_2_
  88.5 0.0 collective-permute-done.3.refs_3_
  88.5 1.4 %output.1 = (f32[4,128,128]{2,1,0:T(8,128)S(1)}, bf16[4,128,128]{2,1,0:T(8,128)(2,1)S(1)}) custom-call(bf16[4,128,128]{2,1,0:T(8,128)(2,1)S(1)} %bitcast.21, bf16[128,1024]{1,0:T(8,128)(2,1)S(1)} %get-tuple-element.23.refs_0_, bf16[128,1024]{1,0:T(8,128)(2,1)} %collective-permute-done.1.refs_1_, bf16[128,1024]{1,0:T(8,128)(2,1)} %collective-permute-done.2.refs_2_, ...), custom_call_target="tpu_custom_call" | custom-call | tf_op jit(solution)/shard_map/output/pallas_call | solution.py:370
  90.0 1.9 %collective-permute-start.4 = (bf16[4,128,128]{2,1,0:T(8,128)(2,1)S(1)}, bf16[4,128,128]{2,1,0:T(8,128)(2,1)S(1)}, u32[]{:S(2)}, u32[]{:S(2)}) collective-permute-start(bf16[4,128,128]{2,1,0:T(8,128)(2,1)S(1)} %get-tuple-element.28), channel_id=1, source_target_pairs={{0,1},{1,0},{2,3},{3,2},{4,5},{5,4},{6,7},{7,6},{8,9},{9,8},{10,11... | collective-permute-start | bytes 393224 | tf_op jit(solution)/shard_map/ppermute | solution.py:381
  91.9 1.3 %collective-permute-done.4 = bf16[4,128,128]{2,1,0:T(8,128)(2,1)S(1)} collective-permute-done((bf16[4,128,128]{2,1,0:T(8,128)(2,1)S(1)}, bf16[4,128,128]{2,1,0:T(8,128)(2,1)S(1)}, u32[]{:S(2)}, u32[]{:S(2)}) %collective-permute-start.4) | collective-permute-done | bytes 131104 | tf_op jit(solution)/shard_map/ppermute | solution.py:381
  93.3 8.8 %all_to_all.15 = bf16[4,128,128]{2,1,0:T(8,128)(2,1)S(1)} all-to-all(bf16[4,128,128]{2,1,0:T(8,128)(2,1)S(1)} %add_convert_fusion), channel_id=1, replica_groups={{0,2,4,6},{1,3,5,7},{8,10,12,14},{9,11,13,15},{16,18,20,22},{17,19,21,2..., dimensions={0} | all-to-all | bytes 262144 | tf_op jit(solution)/shard_map/all_to_all | solution.py:383
  102.1 0.6 reduce_sum.55
  (9 shorter events, 0.1 us)
Async XLA Ops:
  0.0 13.7 %copy-start.4 = (s32[512]{0:T(512)S(1)}, s32[512]{0:T(512)}, u32[]{:S(2)}) copy-start(s32[512]{0:T(512)} %plan_ref.1) | copy-start | bytes 6148
  4.4 23.9 %all-to-all-start = ((bf16[32,128,128]{2,1,0:T(8,128)(2,1)}), bf16[32,128,128]{2,1,0:T(8,128)(2,1)S(1)}, u32[]{:S(2)}, u32[]{:S(2)}) async-start(bf16[32,128,128]{2,1,0:T(8,128)(2,1)} %get-tuple-element.18), calls=%async_computation | async-start | bytes 2097152 | tf_op jit(solution)/shard_map/all_to_all | solution.py:308
  28.3 12.4 %copy-start.2 = (bf16[512,128]{1,0:T(8,128)(2,1)}, bf16[512,128]{1,0:T(8,128)(2,1)S(1)}, u32[]{:S(2)}) copy-start(bf16[512,128]{1,0:T(8,128)(2,1)S(1)} %all-gather) | copy-start | bytes 393220
  28.3 40.7 %copy-start = (f32[32,1,128,128]{3,2,1,0:T(8,128)S(1)}, f32[32,1,128,128]{3,2,1,0:T(8,128)}, u32[]{:S(2)}) copy-start(f32[32,1,128,128]{3,2,1,0:T(8,128)} %param.13) | copy-start | bytes 6291460
  28.4 40.7 %copy-start.5 = (s32[512]{0:T(512)S(1)}, s32[512]{0:T(512)}, u32[]{:S(2)}) copy-start(s32[512]{0:T(512)} %remaining_ref.1) | copy-start | bytes 6148
  28.4 40.7 %copy-start.6 = (f32[128]{0:T(128)S(1)}, f32[128]{0:T(128)}, u32[]{:S(2)}) copy-start(f32[128]{0:T(128)} %param.11) | copy-start | bytes 1540
  29.9 45.4 %all-to-all-start.1 = ((bf16[20,128,128]{2,1,0:T(8,128)(2,1)}), bf16[20,128,128]{2,1,0:T(8,128)(2,1)S(1)}, u32[]{:S(2)}, u32[]{:S(2)}) async-start(bf16[20,128,128]{2,1,0:T(8,128)(2,1)} %pass_on.1.dep_ref), calls=%async_computation.1 | async-start | bytes 1310720 | tf_op jit(solution)/shard_map/all_to_all | solution.py:319
  54.5 14.6 %collective-permute-start = (bf16[16,128,128]{2,1,0:T(8,128)(2,1)S(1)}, bf16[16,128,128]{2,1,0:T(8,128)(2,1)S(1)}, u32[]{:S(2)}, u32[]{:S(2)}) collective-permute-start(bf16[16,128,128]{2,1,0:T(8,128)(2,1)S(1)} %all-gather.1.own_ref.dep_ref), channel_id=1, source_target_pairs={{0,1},{1,0},{2,3},{3,2},{4,5},{5,4},{6,7},{7,6},{8,9},{9,8},{10,11... | collective-permute-start | bytes 1572872 | tf_op jit(solution)/shard_map/ppermute | solution.py:323
  56.4 1.2 %copy-start.3 = (bf16[128,4096]{1,0:T(8,128)(2,1)S(1)}, bf16[128,4096]{1,0:T(8,128)(2,1)}, u32[]{:S(2)}) copy-start(bf16[128,4096]{1,0:T(8,128)(2,1)} %weight_ref.1) | copy-start | bytes 3145732
  58.6 29.9 %collective-permute-start.1 = (bf16[128,1024]{1,0:T(8,128)(2,1)}, bf16[128,1024]{1,0:T(8,128)(2,1)}, u32[]{:S(2)}, u32[]{:S(2)}) collective-permute-start(bf16[128,1024]{1,0:T(8,128)(2,1)} %get-tuple-element.24), channel_id=1, source_target_pairs={{0,8},{1,9},{2,10},{3,11},{4,12},{5,13},{6,14},{7,15},{8,16},{9,17... | collective-permute-start | bytes 786440 | tf_op jit(solution)/shard_map/ppermute | solution.py:358
  61.7 26.8 %collective-permute-start.2 = (bf16[128,1024]{1,0:T(8,128)(2,1)}, bf16[128,1024]{1,0:T(8,128)(2,1)}, u32[]{:S(2)}, u32[]{:S(2)}) collective-permute-start(bf16[128,1024]{1,0:T(8,128)(2,1)} %get-tuple-element.25), channel_id=1, source_target_pairs={{0,16},{1,17},{2,18},{3,19},{4,20},{5,21},{6,22},{7,23},{8,24},{9,... | collective-permute-start | bytes 786440 | tf_op jit(solution)/shard_map/ppermute | solution.py:358
  66.3 22.3 %collective-permute-start.3 = (bf16[128,1024]{1,0:T(8,128)(2,1)}, bf16[128,1024]{1,0:T(8,128)(2,1)}, u32[]{:S(2)}, u32[]{:S(2)}) collective-permute-start(bf16[128,1024]{1,0:T(8,128)(2,1)} %get-tuple-element.26), channel_id=1, source_target_pairs={{0,24},{1,25},{2,26},{3,27},{4,28},{5,29},{6,30},{7,31},{8,0},{9,1... | collective-permute-start | bytes 786440 | tf_op jit(solution)/shard_map/ppermute | solution.py:358
  69.1 1.9 %copy-start.1 = (bf16[4096,3,128]{2,0,1:T(8,128)(2,1)S(1)}, bf16[4096,3,128]{2,0,1:T(8,128)(2,1)}, u32[]{:S(2)}) copy-start(bf16[4096,3,128]{2,0,1:T(8,128)(2,1)} %param.9) | copy-start | bytes 9437188
  90.0 3.2 %collective-permute-start.4 = (bf16[4,128,128]{2,1,0:T(8,128)(2,1)S(1)}, bf16[4,128,128]{2,1,0:T(8,128)(2,1)S(1)}, u32[]{:S(2)}, u32[]{:S(2)}) collective-permute-start(bf16[4,128,128]{2,1,0:T(8,128)(2,1)S(1)} %get-tuple-element.28), channel_id=1, source_target_pairs={{0,1},{1,0},{2,3},{3,2},{4,5},{5,4},{6,7},{7,6},{8,9},{9,8},{10,11... | collective-permute-start | bytes 393224 | tf_op jit(solution)/shard_map/ppermute | solution.py:381

commit v5 on v4

--- a/solution.py
+++ b/solution.py
@@ -25,6 +25,7 @@
 SPOTS = [(x, z, c) for x in range(XS) for z in range(ZS) for c in range(CORES)]
 Z_LINES = [[tensor_id(x, z, c) for z in range(ZS)] for x in range(XS) for c in range(CORES)]
 X_RINGS = [[tensor_id(x, z, c) for x in range(XS)] for z in range(ZS) for c in range(CORES)]
+X_CORES = [[tensor_id(x, z, c) for x in range(XS) for c in range(CORES)] for z in range(ZS)]
 CORE_SWAP = [(tensor_id(x, z, c), tensor_id(x, z, 1 - c)) for x, z, c in SPOTS]
 X_SHIFTS = [
     [(tensor_id(x, z, c), tensor_id((x + k) % XS, z, c)) for x, z, c in SPOTS] for k in range(XS)
@@ -149,12 +150,25 @@
     return lax.div(lax.axis_index("tensor"), CORES * ZS)
 
 
-def deal_kernel(weight_ref, dep_ref, *out_refs):
-    x = x_here()
-    width = weight_ref.shape[1] // XS
+def columns(shift, z, core):
+    spot = (lax.rem(x_here() + shift, XS) * ZS + z) * CORES + core
+    return pl.ds(pl.multiple_of(spot * SIZE, SIZE), SIZE)
+
+
+def lend_kernel(weight_ref, dep_ref, out_ref):
+    other = 1 - core_here()
     for k in range(XS):
-        start = pl.multiple_of(lax.rem(x + k, XS) * width, width)
-        out_refs[k][...] = weight_ref[:, pl.ds(start, width)]
+        for z in range(ZS):
+            out_ref[k, z] = weight_ref[:, columns(k, z, other)]
+
+
+def deal_kernel(weight_ref, lent_ref, *out_refs):
+    core = core_here()
+    for k in range(XS):
+        for z in range(ZS):
+            own, lent = weight_ref[:, columns(k, z, core)], lent_ref[k, z]
+            out_refs[k][z, :SIZE] = jnp.where(core == 0, own, lent)
+            out_refs[k][z, SIZE:] = jnp.where(core == 0, lent, own)
 
 
 def split_rows(q):
@@ -248,23 +262,17 @@
 
 
 def output_kernel(ring_ref, *refs):
-    weights, (own_ref, other_ref) = refs[:XS], refs[XS:]
-    core, x = core_here(), x_here()
-    rows = [ring_ref[lax.rem(x + XS - k, XS)] for k in range(XS)]
-    pairs = [
-        (jnp.concatenate(rows[k : k + 2], axis=1), weights[k], weights[k + 1])
-        for k in range(0, XS, 2)
+    weights, out_ref = refs[:XS], refs[XS]
+    x = x_here()
+    sources = [lax.rem(x + XS - k, XS) * CORES for k in range(XS)]
+    rows = [
+        jnp.concatenate([ring_ref[source + c] for c in range(CORES)], axis=1) for source in sources
     ]
-    width = CORES * SIZE
     for z in range(ZS):
-        part = slice(z * width, (z + 1) * width)
         total = 0.0
-        for both, first, second in pairs:
-            weight = jnp.concatenate([first[:, part], second[:, part]], axis=0)
-            total = total + jnp.dot(both, weight, preferred_element_type=jnp.float32)
-        even, odd = total[:, :SIZE], total[:, SIZE:]
-        own_ref[z] = jnp.where(core == 0, even, odd)
-        other_ref[z] = jnp.where(core == 0, odd, even).astype(jnp.bfloat16)
+        for k in range(XS):
+            total = total + jnp.dot(rows[k], weights[k][z], preferred_element_type=jnp.float32)
+        out_ref[z] = total.astype(jnp.bfloat16)
 
 
 def body(
@@ -347,14 +355,23 @@
         jnp.transpose(qkv_weight, (1, 0, 2)), states,
     )
 
+    lent = pl.pallas_call(
+        lend_kernel,
+        out_shape=jax.ShapeDtypeStruct((XS, ZS, SIZE, SIZE), bf16),
+        in_specs=[VMEM, ANY],
+        out_specs=VMEM,
+        compiler_params=SMALL,
+        name="lend",
+    )(out_weight, passing)
+    lent = lax.ppermute(lent, "tensor", CORE_SWAP)
     dealt = pl.pallas_call(
         deal_kernel,
-        out_shape=[jax.ShapeDtypeStruct((SIZE, out_weight.shape[1] // XS), bf16)] * XS,
-        in_specs=[VMEM, ANY],
+        out_shape=[jax.ShapeDtypeStruct((ZS, CORES * SIZE, SIZE), bf16)] * XS,
+        in_specs=[VMEM, VMEM],
         out_specs=[VMEM] * XS,
         compiler_params=SMALL,
         name="deal",
-    )(out_weight, plane)
+    )(out_weight, lent)
     dealt = [dealt[0]] + [lax.ppermute(dealt[k], "tensor", X_SHIFTS[k]) for k in range(1, XS)]
 
     normed = pl.pallas_call(
@@ -366,20 +383,15 @@
         compiler_params=SMALL,
         name="finish",
     )(code, scaled, partial, gains, incoming)
-    ring = lax.all_gather(normed, "tensor", axis=0, axis_index_groups=X_RINGS)
-    own, away = pl.pallas_call(
+    ring = lax.all_gather(normed, "tensor", axis=0, axis_index_groups=X_CORES)
+    sums = pl.pallas_call(
         output_kernel,
-        out_shape=[
-            jax.ShapeDtypeStruct((ZS, count, SIZE), f32),
-            jax.ShapeDtypeStruct((ZS, count, SIZE), bf16),
-        ],
+        out_shape=jax.ShapeDtypeStruct((ZS, count, SIZE), bf16),
         in_specs=[VMEM] * (1 + XS),
-        out_specs=[VMEM, VMEM],
+        out_specs=VMEM,
         compiler_params=SMALL,
         name="output",
     )(ring, *dealt)
-    received = lax.ppermute(away, "tensor", CORE_SWAP)
-    sums = (own + received.astype(f32)).astype(bf16)
     pieces = lax.all_to_all(sums, "tensor", 0, 0, tiled=True, axis_index_groups=Z_LINES)
     result = jnp.sum(pieces.astype(f32), axis=0).astype(bf16)
     return result.reshape(STEPS, rows, SIZE)

time: 103 us -> 101 us (0.981)
  local copies, waits for them, and re-layouts: 3.4 us -> 0.31 us
    unnamed x15, local copies, waits for them, and re-layouts: 3.14 us -> 0.04 us
    ppermute x1, waiting for transfers between devices: 1.31 us -> 0.01 us  [body(): lent = lax.ppermute(lent, 'tensor', CORE_SWAP)]
    pallas_call x2 -> x3, Pallas kernels: 2.4 us -> 1.65 us  [the longest x1 1.07 us: body(): pl.pallas_call(deal_kernel, out_shape=[jax.ShapeDtypeStruct((ZS, CORES *...]
  transfers between devices with their start and end apart: 7 -> 7, of which waited for: 2 -> 1; matrix products, arithmetic and copies ran while one was open for 1% -> 1% of each run, Pallas kernels for 5% -> 6%
where the time goes in v5:
time: 101 us; the launch traced here: 100 us
  blocking collectives  49.3 us (49%)
  starting transfers between devices  34.1 us (34%)
  Pallas kernels  10.5 us (10%)
  other arithmetic  2.89 us (3%)
  waiting for transfers between devices  2.45 us (2%)
    all_gather x1, blocking collectives, body(): line = lax.all_gather(inputs, 'tensor', axis=0, axis_index_groups=Z_LINES)  13.6 us
    all_gather x1, blocking collectives, body(): lax.all_gather(after(line, passing), 'tensor', axis=0, axis_index_groups=...  13.6 us
    all_gather x1, blocking collectives, body(): ring = lax.all_gather(normed, 'tensor', axis=0, axis_index_groups=X_CORES)  13.2 us
    all_to_all x1, starting transfers between devices, body(): lax.all_to_all(passing, 'group', 0, 0, tiled=True, axis_index_groups=Z_RI...  11 us
    ppermute x3, starting transfers between devices, body(): lax.ppermute(dealt[k], 'tensor', X_SHIFTS[k])  9.8 us
    all_to_all x1, starting transfers between devices, body(): lax.all_to_all(outgoing, 'group', 0, 0, tiled=True, axis_index_groups=Y_R...  9.36 us
    all_to_all x1, blocking collectives, body(): lax.all_to_all(sums, 'tensor', 0, 0, tiled=True, axis_index_groups=Z_LINES)  8.89 us
    pallas_call x1, Pallas kernels, body(): pl.pallas_call(functools.partial(pack_kernel, rows), out_shape=[jax.Shape...  2.99 us
  transfers between devices with their start and end apart: 7, of which 1 were waited for; matrix products, arithmetic and copies ran while one was open for 1% of the time, Pallas kernels for 6%

profile of v5, /device:TPU:16, one launch (start us, length us, event | category | flops | bytes accessed | tf_op | source)
XLA Modules:
  0.0 100.4 jit_solution(14946989738482059479)
XLA Ops:
  0.0 0.0 copy-start.4
  0.0 1.5 %select_reduce_fusion.target_ref = s32[32]{0:T(128)} fusion(s32[512]{0:T(512)} %plan_ref.1, s32[32]{0:T(128)S(1)} %iota_add_fusion), kind=kLoop, calls=%fused_computation.2 | loop fusion | flops 49120 | bytes 2304 | tf_op jit(solution)/shard_map/reduce_sum | solution.py:61
  1.5 3.0 %pack.1 = (bf16[32,128,128]{2,1,0:T(8,128)(2,1)}, bf16[128,128]{1,0:T(8,128)(2,1)}) custom-call(s32[32]{0:T(128)} %select_reduce_fusion.target_ref, f32[32,128,128]{2,1,0:T(8,128)} %bitcast.16, bf16[128,128]{1,0:T(8,128)(2,1)} %bitcast.23), custom_call_target="tpu_custom_call" | custom-call | tf_op jit(solution)/shard_map/pack/pallas_call | solution.py:295
  4.5 0.0 copy-start.1
  4.5 9.4 %all-to-all-start = ((bf16[32,128,128]{2,1,0:T(8,128)(2,1)}), bf16[32,128,128]{2,1,0:T(8,128)(2,1)S(1)}, u32[]{:S(2)}, u32[]{:S(2)}) async-start(bf16[32,128,128]{2,1,0:T(8,128)(2,1)} %get-tuple-element.16), calls=%async_computation | async-start | bytes 2097152 | tf_op jit(solution)/shard_map/all_to_all | solution.py:316
  13.9 0.0 copy-done.4
  13.9 0.1 reshape.97
  14.0 0.1 compare_and_fusion
  14.1 0.1 convert_reduce_fusion.1
  14.3 0.2 convert_reduce_fusion
  14.5 0.1 fusion.4
  14.6 0.2 select_reduce_fusion.1
  14.8 0.1 copy.14
  14.9 0.1 min.12.index_ref
  15.0 13.6 %all-gather = bf16[512,128]{1,0:T(8,128)(2,1)S(1)} all-gather(bf16[128,128]{1,0:T(8,128)(2,1)} %get-tuple-element.15), channel_id=2, replica_groups={{0,2,4,6},{1,3,5,7},{8,10,12,14},{9,11,13,15},{16,18,20,22},{17,19,21,2..., dimensions={0}, use_global_device_ids=true | all-gather | bytes 163840 | tf_op jit(solution)/shard_map/all_gather | solution.py:317
  28.6 0.0 all-to-all-done.rows_ref
  28.6 1.6 %pass_on.1.dep_ref = bf16[20,128,128]{2,1,0:T(8,128)(2,1)} custom-call(s32[20]{0:T(128)S(1)} %min.12.index_ref, bf16[32,128,128]{2,1,0:T(8,128)(2,1)S(1)} %all-to-all-done.rows_ref, bf16[4,128,128]{2,1,0:T(8,128)(2,1)S(1)} %bitcast.19), custom_call_target="tpu_custom_call" | custom-call | tf_op jit(solution)/shard_map/pass_on/pallas_call | solution.py:318
  30.1 0.0 copy-start
  30.2 0.0 copy-start.5
  30.2 0.0 copy-start.6
  30.2 11.0 %all-to-all-start.1 = ((bf16[20,128,128]{2,1,0:T(8,128)(2,1)}), bf16[20,128,128]{2,1,0:T(8,128)(2,1)}, u32[]{:S(2)}, u32[]{:S(2)}) async-start(bf16[20,128,128]{2,1,0:T(8,128)(2,1)} %pass_on.1.dep_ref), calls=%async_computation.1 | async-start | bytes 1310720 | tf_op jit(solution)/shard_map/all_to_all | solution.py:327
  41.1 0.0 copy-done.3
  41.1 0.0 copy-done.1
  41.2 0.0 copy-start.2
  41.2 0.2 lend.1
  41.3 2.1 %collective-permute-start.1 = (bf16[4,4,128,128]{3,2,1,0:T(8,128)(2,1)S(1)}, bf16[4,4,128,128]{3,2,1,0:T(8,128)(2,1)S(1)}, u32[]{:S(2)}, u32[]{:S(2)}) collective-permute-start(bf16[4,4,128,128]{3,2,1,0:T(8,128)(2,1)S(1)} %lend.1), channel_id=1, source_target_pairs={{0,1},{1,0},{2,3},{3,2},{4,5},{5,4},{6,7},{7,6},{8,9},{9,8},{10,11... | collective-permute-start | bytes 1572872 | tf_op jit(solution)/shard_map/ppermute | solution.py:366
  43.4 13.6 %all-gather.1.own_ref = bf16[16,128,128]{2,1,0:T(8,128)(2,1)S(1)} all-gather(bf16[4,128,128]{2,1,0:T(8,128)(2,1)} %after.1), channel_id=3, replica_groups={{0,8,16,24},{1,9,17,25},{2,10,18,26},{3,11,19,27},{4,12,20,28},{5,13,21..., dimensions={0}, use_global_device_ids=true | all-gather | bytes 655360 | tf_op jit(solution)/shard_map/all_gather | solution.py:329
  57.0 1.9 %collective-permute-start = (bf16[16,128,128]{2,1,0:T(8,128)(2,1)S(1)}, bf16[16,128,128]{2,1,0:T(8,128)(2,1)S(1)}, u32[]{:S(2)}, u32[]{:S(2)}) collective-permute-start(bf16[16,128,128]{2,1,0:T(8,128)(2,1)S(1)} %all-gather.1.own_ref), channel_id=1, source_target_pairs={{0,1},{1,0},{2,3},{3,2},{4,5},{5,4},{6,7},{7,6},{8,9},{9,8},{10,11... | collective-permute-start | bytes 1572872 | tf_op jit(solution)/shard_map/ppermute | solution.py:331
  58.9 0.0 collective-permute-done.1.lent_ref
  58.9 1.1 %deal.1 = (bf16[4,256,128]{2,1,0:T(8,128)(2,1)S(1)}, bf16[4,256,128]{2,1,0:T(8,128)(2,1)}, bf16[4,256,128]{2,1,0:T(8,128)(2,1)}, bf16[4,256,128]{2,1,0:T(8,128)(2,1)}) custom-call(bf16[128,4096]{1,0:T(8,128)(2,1)S(1)} %copy-done.1, bf16[4,4,128,128]{3,2,1,0:T(8,128)(2,1)S(1)} %collective-permute-done.1.lent_ref), custom_call_target="tpu_custom_call" | custom-call | tf_op jit(solution)/shard_map/deal/pallas_call | solution.py:367
  60.0 3.3 %collective-permute-start.2 = (bf16[4,256,128]{2,1,0:T(8,128)(2,1)}, bf16[4,256,128]{2,1,0:T(8,128)(2,1)S(1)}, u32[]{:S(2)}, u32[]{:S(2)}) collective-permute-start(bf16[4,256,128]{2,1,0:T(8,128)(2,1)} %get-tuple-element.22), channel_id=1, source_target_pairs={{0,8},{1,9},{2,10},{3,11},{4,12},{5,13},{6,14},{7,15},{8,16},{9,17... | collective-permute-start | bytes 786440 | tf_op jit(solution)/shard_map/ppermute | solution.py:375
  63.2 4.6 %collective-permute-start.3 = (bf16[4,256,128]{2,1,0:T(8,128)(2,1)}, bf16[4,256,128]{2,1,0:T(8,128)(2,1)S(1)}, u32[]{:S(2)}, u32[]{:S(2)}) collective-permute-start(bf16[4,256,128]{2,1,0:T(8,128)(2,1)} %get-tuple-element.23), channel_id=1, source_target_pairs={{0,16},{1,17},{2,18},{3,19},{4,20},{5,21},{6,22},{7,23},{8,24},{9,... | collective-permute-start | bytes 786440 | tf_op jit(solution)/shard_map/ppermute | solution.py:375
  67.8 2.0 %collective-permute-start.4 = (bf16[4,256,128]{2,1,0:T(8,128)(2,1)}, bf16[4,256,128]{2,1,0:T(8,128)(2,1)S(1)}, u32[]{:S(2)}, u32[]{:S(2)}) collective-permute-start(bf16[4,256,128]{2,1,0:T(8,128)(2,1)} %get-tuple-element.24), channel_id=1, source_target_pairs={{0,24},{1,25},{2,26},{3,27},{4,28},{5,29},{6,30},{7,31},{8,0},{9,1... | collective-permute-start | bytes 786440 | tf_op jit(solution)/shard_map/ppermute | solution.py:375
  70.4 0.0 collective-permute-done.other_ref
  70.5 0.0 copy-done
  70.5 0.0 copy-done.5
  70.5 0.0 copy-done.6
  70.5 0.0 copy-done.2
  70.5 2.9 %project.1 = (f32[128,128]{1,0:T(8,128)S(1)}, f32[128,128]{1,0:T(8,128)S(1)}, f32[128,128]{1,0:T(8,128)S(1)}, s32[14]{0:T(128)S(1)}) custom-call(s32[512]{0:T(512)S(1)} %copy-done.4, s32[512]{0:T(512)S(1)} %copy-done.5, f32[1]{0:T(128)S(6)} %copy.19.decay_ref, f32[1,128]{1,0:T(1,128)S(1)} %bitcast.22, bf16[16,128,128]{2,1,0:T(8,128)(2,1)S(1)} %all-gather.1.own_ref, ...), custom_call_target="tpu_custom_call" | custom-call | flops 402653184 | bytes 6291456 | tf_op jit(solution)/shard_map/project/pallas_call | solution.py:332
  73.4 2.4 %all-to-all-done.1.incoming_ref = bf16[20,128,128]{2,1,0:T(8,128)(2,1)} async-done(((bf16[20,128,128]{2,1,0:T(8,128)(2,1)}), bf16[20,128,128]{2,1,0:T(8,128)(2,1)}, u32[]{:S(2)}, u32[]{:S(2)}) %all-to-all-start.1) | async-done | bytes 655392 | tf_op jit(solution)/shard_map/all_to_all | solution.py:327
  75.8 1.4 %finish.1 = bf16[128,128]{1,0:T(8,128)(2,1)S(1)} custom-call(s32[14]{0:T(128)S(1)} %get-tuple-element.17.code_ref, f32[128,128]{1,0:T(8,128)S(1)} %get-tuple-element.18.scaled_ref, f32[128,128]{1,0:T(8,128)S(1)} %get-tuple-element.19.partial_ref, f32[128,128]{1,0:T(8,128)S(1)} %get-tuple-element.20.gains_ref, bf16[20,128,128]{2,1,0:T(8,128)(2,1)} %all-to-all-done.1.incoming_ref), custom_call_target="tpu_custom_call" | custom-call | tf_op jit(solution)/shard_map/finish/pallas_call | solution.py:377
  77.3 13.2 %all-gather.2 = bf16[1024,128]{1,0:T(8,128)(2,1)S(1)} all-gather(bf16[128,128]{1,0:T(8,128)(2,1)S(1)} %finish.1), channel_id=4, replica_groups={{0,1,8,9,16,17,24,25},{2,3,10,11,18,19,26,27},{4,5,12,13,20,21,28,29},{..., dimensions={0}, use_global_device_ids=true | all-gather | bytes 294912 | tf_op jit(solution)/shard_map/all_gather | solution.py:386
  90.4 0.0 collective-permute-done.2.refs_1_
  90.4 0.0 collective-permute-done.3.refs_2_
  90.4 0.0 collective-permute-done.4.refs_3_
  90.5 0.4 output.1
  90.9 8.9 %all_to_all.15 = bf16[4,128,128]{2,1,0:T(8,128)(2,1)S(1)} all-to-all(bf16[4,128,128]{2,1,0:T(8,128)(2,1)S(1)} %output.1), channel_id=1, replica_groups={{0,2,4,6},{1,3,5,7},{8,10,12,14},{9,11,13,15},{16,18,20,22},{17,19,21,2..., dimensions={0} | all-to-all | bytes 262144 | tf_op jit(solution)/shard_map/all_to_all | solution.py:395
  99.8 0.6 reduce_sum.55
  (9 shorter events, 0.0 us)
Async XLA Ops:
  0.0 13.9 %copy-start.4 = (s32[512]{0:T(512)S(1)}, s32[512]{0:T(512)}, u32[]{:S(2)}) copy-start(s32[512]{0:T(512)} %plan_ref.1) | copy-start | bytes 6148
  4.5 36.6 %copy-start.1 = (bf16[128,4096]{1,0:T(8,128)(2,1)S(1)}, bf16[128,4096]{1,0:T(8,128)(2,1)}, u32[]{:S(2)}) copy-start(bf16[128,4096]{1,0:T(8,128)(2,1)} %weight_ref.3) | copy-start | bytes 3145732
  4.5 24.1 %all-to-all-start = ((bf16[32,128,128]{2,1,0:T(8,128)(2,1)}), bf16[32,128,128]{2,1,0:T(8,128)(2,1)S(1)}, u32[]{:S(2)}, u32[]{:S(2)}) async-start(bf16[32,128,128]{2,1,0:T(8,128)(2,1)} %get-tuple-element.16), calls=%async_computation | async-start | bytes 2097152 | tf_op jit(solution)/shard_map/all_to_all | solution.py:316
  28.6 12.6 %copy-start.3 = (bf16[512,128]{1,0:T(8,128)(2,1)}, bf16[512,128]{1,0:T(8,128)(2,1)S(1)}, u32[]{:S(2)}) copy-start(bf16[512,128]{1,0:T(8,128)(2,1)S(1)} %all-gather) | copy-start | bytes 393220
  30.1 40.3 %copy-start = (f32[32,1,128,128]{3,2,1,0:T(8,128)S(1)}, f32[32,1,128,128]{3,2,1,0:T(8,128)}, u32[]{:S(2)}) copy-start(f32[32,1,128,128]{3,2,1,0:T(8,128)} %param.13) | copy-start | bytes 6291460
  30.2 40.3 %copy-start.5 = (s32[512]{0:T(512)S(1)}, s32[512]{0:T(512)}, u32[]{:S(2)}) copy-start(s32[512]{0:T(512)} %remaining_ref.1) | copy-start | bytes 6148
  30.2 40.3 %copy-start.6 = (f32[128]{0:T(128)S(1)}, f32[128]{0:T(128)}, u32[]{:S(2)}) copy-start(f32[128]{0:T(128)} %param.11) | copy-start | bytes 1540
  30.2 45.6 %all-to-all-start.1 = ((bf16[20,128,128]{2,1,0:T(8,128)(2,1)}), bf16[20,128,128]{2,1,0:T(8,128)(2,1)}, u32[]{:S(2)}, u32[]{:S(2)}) async-start(bf16[20,128,128]{2,1,0:T(8,128)(2,1)} %pass_on.1.dep_ref), calls=%async_computation.1 | async-start | bytes 1310720 | tf_op jit(solution)/shard_map/all_to_all | solution.py:327
  41.2 29.3 %copy-start.2 = (bf16[4096,3,128]{2,0,1:T(8,128)(2,1)S(1)}, bf16[4096,3,128]{2,0,1:T(8,128)(2,1)}, u32[]{:S(2)}) copy-start(bf16[4096,3,128]{2,0,1:T(8,128)(2,1)} %param.9) | copy-start | bytes 9437188
  41.3 17.6 %collective-permute-start.1 = (bf16[4,4,128,128]{3,2,1,0:T(8,128)(2,1)S(1)}, bf16[4,4,128,128]{3,2,1,0:T(8,128)(2,1)S(1)}, u32[]{:S(2)}, u32[]{:S(2)}) collective-permute-start(bf16[4,4,128,128]{3,2,1,0:T(8,128)(2,1)S(1)} %lend.1), channel_id=1, source_target_pairs={{0,1},{1,0},{2,3},{3,2},{4,5},{5,4},{6,7},{7,6},{8,9},{9,8},{10,11... | collective-permute-start | bytes 1572872 | tf_op jit(solution)/shard_map/ppermute | solution.py:366
  57.0 13.5 %collective-permute-start = (bf16[16,128,128]{2,1,0:T(8,128)(2,1)S(1)}, bf16[16,128,128]{2,1,0:T(8,128)(2,1)S(1)}, u32[]{:S(2)}, u32[]{:S(2)}) collective-permute-start(bf16[16,128,128]{2,1,0:T(8,128)(2,1)S(1)} %all-gather.1.own_ref), channel_id=1, source_target_pairs={{0,1},{1,0},{2,3},{3,2},{4,5},{5,4},{6,7},{7,6},{8,9},{9,8},{10,11... | collective-permute-start | bytes 1572872 | tf_op jit(solution)/shard_map/ppermute | solution.py:331
  60.0 30.5 %collective-permute-start.2 = (bf16[4,256,128]{2,1,0:T(8,128)(2,1)}, bf16[4,256,128]{2,1,0:T(8,128)(2,1)S(1)}, u32[]{:S(2)}, u32[]{:S(2)}) collective-permute-start(bf16[4,256,128]{2,1,0:T(8,128)(2,1)} %get-tuple-element.22), channel_id=1, source_target_pairs={{0,8},{1,9},{2,10},{3,11},{4,12},{5,13},{6,14},{7,15},{8,16},{9,17... | collective-permute-start | bytes 786440 | tf_op jit(solution)/shard_map/ppermute | solution.py:375
  63.2 27.2 %collective-permute-start.3 = (bf16[4,256,128]{2,1,0:T(8,128)(2,1)}, bf16[4,256,128]{2,1,0:T(8,128)(2,1)S(1)}, u32[]{:S(2)}, u32[]{:S(2)}) collective-permute-start(bf16[4,256,128]{2,1,0:T(8,128)(2,1)} %get-tuple-element.23), channel_id=1, source_target_pairs={{0,16},{1,17},{2,18},{3,19},{4,20},{5,21},{6,22},{7,23},{8,24},{9,... | collective-permute-start | bytes 786440 | tf_op jit(solution)/shard_map/ppermute | solution.py:375
  67.8 22.6 %collective-permute-start.4 = (bf16[4,256,128]{2,1,0:T(8,128)(2,1)}, bf16[4,256,128]{2,1,0:T(8,128)(2,1)S(1)}, u32[]{:S(2)}, u32[]{:S(2)}) collective-permute-start(bf16[4,256,128]{2,1,0:T(8,128)(2,1)} %get-tuple-element.24), channel_id=1, source_target_pairs={{0,24},{1,25},{2,26},{3,27},{4,28},{5,29},{6,30},{7,31},{8,0},{9,1... | collective-permute-start | bytes 786440 | tf_op jit(solution)/shard_map/ppermute | solution.py:375

commit v6 on v5

--- a/solution.py
+++ b/solution.py
@@ -36,7 +36,7 @@
 VMEM = pl.BlockSpec(memory_space=pltpu.VMEM)
 SMEM = pl.BlockSpec(memory_space=pltpu.SMEM)
 ANY = pl.BlockSpec(memory_space=pl.ANY)
-SMALL = pltpu.CompilerParams(vmem_limit_bytes=16 * 2**20)
+SMALL = pltpu.CompilerParams(vmem_limit_bytes=8 * 2**20)
 ROOMY = pltpu.CompilerParams(vmem_limit_bytes=56 * 2**20)
 DMA = pltpu.SemaphoreType.DMA
 
@@ -54,11 +54,6 @@
         input_output_aliases={0: 0},
         name="after",
     )(x, dep)
-
-
-def targets(migration_plan, own_group, rows):
-    wanted = migration_plan[None, :] == (own_group * rows + jnp.arange(rows))[:, None]
-    return jnp.sum(jnp.where(wanted, jnp.arange(migration_plan.shape[0])[None, :], 0), axis=1)
 
 
 def rows_on(migration_plan, own_group, groups, rows):
@@ -78,7 +73,7 @@
 
 
 def pack_kernel(
-    rows, target_ref, states_ref, inputs_ref, out_ref, same_ref,
+    rows, plan_ref, states_ref, inputs_ref, out_ref, same_ref,
     wide_ref, narrow_ref, inputs_vmem, slot_ref, seen_ref, in_sem, out_sem, copy_sem,
 ):
     group = group_here()
@@ -87,24 +82,29 @@
     for i in range(ZH * YS):
         seen_ref[i] = 0
 
-    def scan(row, count):
-        goal = target_ref[row] // rows
+    plan = plan_ref[...] - group * rows
+    everyone = lax.broadcasted_iota(jnp.int32, plan.shape, 0) * plan.shape[1]
+    everyone = everyone + lax.broadcasted_iota(jnp.int32, plan.shape, 1)
+    everyone = everyone.astype(jnp.float32)
+    targets = [jnp.max(jnp.where(plan == row, everyone, 0.0)).astype(jnp.int32) for row in range(rows)]
+    count = jnp.int32(0)
+    for row in range(rows):
+        goal = lax.shift_right_logical(targets[row], rows.bit_length() - 1)
         leaves = (goal != group) & (count < MOVED)
 
         @pl.when(leaves)
-        def _():
+        def _(row=row, goal=goal, count=count):
             rank = seen_ref[goal]
             seen_ref[goal] = rank + 1
             slot_ref[count] = (
-                (goal % YS) * (ZH * SLOTS) + goal // YS * SLOTS + jnp.minimum(rank, SLOTS - 1)
+                lax.rem(goal, YS) * (ZH * SLOTS) + lax.div(goal, YS) * SLOTS
+                + jnp.minimum(rank, SLOTS - 1)
             )
             pltpu.make_async_copy(
                 states_ref.at[row], wide_ref.at[count], in_sem.at[count]
             ).start()
 
-        return count + leaves.astype(jnp.int32)
-
-    count = lax.fori_loop(0, rows, scan, jnp.int32(0), unroll=8)
+        count = count + leaves.astype(jnp.int32)
     load.wait()
     store = pltpu.make_async_copy(inputs_vmem, same_ref, copy_sem.at[1])
     store.start()
@@ -298,7 +298,7 @@
             jax.ShapeDtypeStruct((groups * SLOTS, SIZE, SIZE), bf16),
             jax.ShapeDtypeStruct((count, SIZE), bf16),
         ],
-        in_specs=[SMEM, ANY, ANY],
+        in_specs=[VMEM, ANY, ANY],
         out_specs=[ANY, ANY],
         scratch_shapes=[
             pltpu.VMEM((MOVED, SIZE, SIZE), f32),
@@ -312,13 +312,13 @@
         ],
         compiler_params=ROOMY,
         name="pack",
-    )(targets(migration_plan, own_group, rows), states, step_inputs.reshape(count, SIZE))
+    )(migration_plan.reshape(ZH, YS * rows), states, step_inputs.reshape(count, SIZE))
     passing = lax.all_to_all(outgoing, "group", 0, 0, tiled=True, axis_index_groups=Y_RINGS)
     line = lax.all_gather(inputs, "tensor", axis=0, axis_index_groups=Z_LINES)
     passing = pl.pallas_call(
         pass_kernel,
         out_shape=jax.ShapeDtypeStruct((ZH * PASSING, SIZE, SIZE), bf16),
-        in_specs=[SMEM, VMEM, ANY],
+        in_specs=[SMEM, VMEM, VMEM],
         out_specs=ANY,
         scratch_shapes=[DMA((ZH * PASSING,))],
         compiler_params=SMALL,
@@ -345,7 +345,7 @@
             pltpu.VMEM((rows, SIZE), jnp.int32),
             pltpu.SMEM((ZH,), jnp.int32),
         ],
-        compiler_params=pltpu.CompilerParams(vmem_limit_bytes=24 * 2**20),
+        compiler_params=pltpu.CompilerParams(vmem_limit_bytes=16 * 2**20),
         cost_estimate=pl.CostEstimate(
             flops=2 * count * 4096 * 384, bytes_accessed=6 * 2**20, transcendentals=0
         ),

time: 101 us -> 99.5 us (0.985)
  other arithmetic: 2.89 us -> 1.38 us
    reduce_sum x1 -> x0, other arithmetic: 1.51 us -> none  [targets(): jnp.sum(jnp.where(wanted, jnp.arange(migration_plan.shape[0])[None, :], 0...]
where the time goes in v6:
time: 99.5 us; the launch traced here: 99 us
  blocking collectives  49.2 us (49%)
  starting transfers between devices  34.1 us (34%)
  Pallas kernels  10.6 us (11%)
  waiting for transfers between devices  2.47 us (2%)
  other arithmetic  1.38 us (1%)
    all_gather x1, blocking collectives, body(): lax.all_gather(after(line, passing), 'tensor', axis=0, axis_index_groups=...  13.6 us
    all_gather x1, blocking collectives, body(): line = lax.all_gather(inputs, 'tensor', axis=0, axis_index_groups=Z_LINES)  13.6 us
    all_gather x1, blocking collectives, body(): ring = lax.all_gather(normed, 'tensor', axis=0, axis_index_groups=X_CORES)  13.2 us
    all_to_all x1, starting transfers between devices, body(): lax.all_to_all(passing, 'group', 0, 0, tiled=True, axis_index_groups=Z_RI...  11 us
    ppermute x3, starting transfers between devices, body(): lax.ppermute(dealt[k], 'tensor', X_SHIFTS[k])  9.8 us
    all_to_all x1, starting transfers between devices, body(): lax.all_to_all(outgoing, 'group', 0, 0, tiled=True, axis_index_groups=Y_R...  9.35 us
    all_to_all x1, blocking collectives, body(): lax.all_to_all(sums, 'tensor', 0, 0, tiled=True, axis_index_groups=Z_LINES)  8.89 us
    pallas_call x1, Pallas kernels, body(): pl.pallas_call(functools.partial(pack_kernel, rows), out_shape=[jax.Shape...  3.1 us
  transfers between devices with their start and end apart: 7, of which 1 were waited for; matrix products, arithmetic and copies ran while one was open for 1% of the time, Pallas kernels for 6%

profile of v6, /device:TPU:16, one launch (start us, length us, event | category | flops | bytes accessed | tf_op | source)
XLA Modules:
  0.0 99.0 jit_solution(3873062776920880757)
XLA Ops:
  0.0 0.0 copy-start.4
  0.0 3.1 %pack.1 = (bf16[32,128,128]{2,1,0:T(8,128)(2,1)}, bf16[128,128]{1,0:T(8,128)(2,1)}) custom-call(s32[4,128]{1,0:T(4,128)} %bitcast.23, f32[32,128,128]{2,1,0:T(8,128)} %bitcast.17, bf16[128,128]{1,0:T(8,128)(2,1)} %bitcast.25), custom_call_target="tpu_custom_call" | custom-call | tf_op jit(solution)/shard_map/pack/pallas_call | solution.py:295
  3.1 0.0 copy-start.1
  3.1 9.3 %all-to-all-start = ((bf16[32,128,128]{2,1,0:T(8,128)(2,1)}), bf16[32,128,128]{2,1,0:T(8,128)(2,1)S(1)}, u32[]{:S(2)}, u32[]{:S(2)}) async-start(bf16[32,128,128]{2,1,0:T(8,128)(2,1)} %get-tuple-element.16), calls=%async_computation | async-start | bytes 2097152 | tf_op jit(solution)/shard_map/all_to_all | solution.py:316
  12.5 0.0 copy-done.4
  12.5 0.1 reshape.96
  12.6 0.1 compare_and_fusion
  12.7 0.1 convert_reduce_fusion.1
  12.9 0.2 convert_reduce_fusion
  13.1 0.1 fusion.4
  13.2 0.2 select_reduce_fusion
  13.4 0.1 copy.14
  13.5 0.1 min.12.index_ref
  13.5 13.6 %all-gather = bf16[512,128]{1,0:T(8,128)(2,1)S(1)} all-gather(bf16[128,128]{1,0:T(8,128)(2,1)} %get-tuple-element.15), channel_id=2, replica_groups={{0,2,4,6},{1,3,5,7},{8,10,12,14},{9,11,13,15},{16,18,20,22},{17,19,21,2..., dimensions={0}, use_global_device_ids=true | all-gather | bytes 163840 | tf_op jit(solution)/shard_map/all_gather | solution.py:317
  27.1 0.0 copy-start.3
  27.1 0.0 all-to-all-done.rows_ref
  27.1 1.6 %pass_on.1.dep_ref = bf16[20,128,128]{2,1,0:T(8,128)(2,1)} custom-call(s32[20]{0:T(128)S(1)} %min.12.index_ref, bf16[32,128,128]{2,1,0:T(8,128)(2,1)S(1)} %all-to-all-done.rows_ref, bf16[4,128,128]{2,1,0:T(8,128)(2,1)S(1)} %bitcast.20), custom_call_target="tpu_custom_call" | custom-call | tf_op jit(solution)/shard_map/pass_on/pallas_call | solution.py:318
  28.7 0.0 copy-start
  28.7 0.0 copy-start.5
  28.7 0.0 copy-start.6
  28.7 11.0 %all-to-all-start.1 = ((bf16[20,128,128]{2,1,0:T(8,128)(2,1)}), bf16[20,128,128]{2,1,0:T(8,128)(2,1)}, u32[]{:S(2)}, u32[]{:S(2)}) async-start(bf16[20,128,128]{2,1,0:T(8,128)(2,1)} %pass_on.1.dep_ref), calls=%async_computation.1 | async-start | bytes 1310720 | tf_op jit(solution)/shard_map/all_to_all | solution.py:327
  39.7 0.0 copy-done.3
  39.7 0.0 copy-done.1
  39.8 0.0 copy-start.2
  39.8 0.2 lend.1
  39.9 2.1 %collective-permute-start.1 = (bf16[4,4,128,128]{3,2,1,0:T(8,128)(2,1)S(1)}, bf16[4,4,128,128]{3,2,1,0:T(8,128)(2,1)S(1)}, u32[]{:S(2)}, u32[]{:S(2)}) collective-permute-start(bf16[4,4,128,128]{3,2,1,0:T(8,128)(2,1)S(1)} %lend.1), channel_id=1, source_target_pairs={{0,1},{1,0},{2,3},{3,2},{4,5},{5,4},{6,7},{7,6},{8,9},{9,8},{10,11... | collective-permute-start | bytes 1572872 | tf_op jit(solution)/shard_map/ppermute | solution.py:366
  42.0 13.6 %all-gather.1.own_ref = bf16[16,128,128]{2,1,0:T(8,128)(2,1)S(1)} all-gather(bf16[4,128,128]{2,1,0:T(8,128)(2,1)} %after.1), channel_id=3, replica_groups={{0,8,16,24},{1,9,17,25},{2,10,18,26},{3,11,19,27},{4,12,20,28},{5,13,21..., dimensions={0}, use_global_device_ids=true | all-gather | bytes 655360 | tf_op jit(solution)/shard_map/all_gather | solution.py:329
  55.6 1.9 %collective-permute-start = (bf16[16,128,128]{2,1,0:T(8,128)(2,1)S(1)}, bf16[16,128,128]{2,1,0:T(8,128)(2,1)S(1)}, u32[]{:S(2)}, u32[]{:S(2)}) collective-permute-start(bf16[16,128,128]{2,1,0:T(8,128)(2,1)S(1)} %all-gather.1.own_ref), channel_id=1, source_target_pairs={{0,1},{1,0},{2,3},{3,2},{4,5},{5,4},{6,7},{7,6},{8,9},{9,8},{10,11... | collective-permute-start | bytes 1572872 | tf_op jit(solution)/shard_map/ppermute | solution.py:331
  57.5 0.0 collective-permute-done.1.lent_ref
  57.5 1.1 %deal.1 = (bf16[4,256,128]{2,1,0:T(8,128)(2,1)S(1)}, bf16[4,256,128]{2,1,0:T(8,128)(2,1)}, bf16[4,256,128]{2,1,0:T(8,128)(2,1)}, bf16[4,256,128]{2,1,0:T(8,128)(2,1)}) custom-call(bf16[128,4096]{1,0:T(8,128)(2,1)S(1)} %copy-done.1, bf16[4,4,128,128]{3,2,1,0:T(8,128)(2,1)S(1)} %collective-permute-done.1.lent_ref), custom_call_target="tpu_custom_call" | custom-call | tf_op jit(solution)/shard_map/deal/pallas_call | solution.py:367
  58.5 3.3 %collective-permute-start.2 = (bf16[4,256,128]{2,1,0:T(8,128)(2,1)}, bf16[4,256,128]{2,1,0:T(8,128)(2,1)S(1)}, u32[]{:S(2)}, u32[]{:S(2)}) collective-permute-start(bf16[4,256,128]{2,1,0:T(8,128)(2,1)} %get-tuple-element.22), channel_id=1, source_target_pairs={{0,8},{1,9},{2,10},{3,11},{4,12},{5,13},{6,14},{7,15},{8,16},{9,17... | collective-permute-start | bytes 786440 | tf_op jit(solution)/shard_map/ppermute | solution.py:375
  61.8 4.6 %collective-permute-start.3 = (bf16[4,256,128]{2,1,0:T(8,128)(2,1)}, bf16[4,256,128]{2,1,0:T(8,128)(2,1)S(1)}, u32[]{:S(2)}, u32[]{:S(2)}) collective-permute-start(bf16[4,256,128]{2,1,0:T(8,128)(2,1)} %get-tuple-element.23), channel_id=1, source_target_pairs={{0,16},{1,17},{2,18},{3,19},{4,20},{5,21},{6,22},{7,23},{8,24},{9,... | collective-permute-start | bytes 786440 | tf_op jit(solution)/shard_map/ppermute | solution.py:375
  66.4 2.0 %collective-permute-start.4 = (bf16[4,256,128]{2,1,0:T(8,128)(2,1)}, bf16[4,256,128]{2,1,0:T(8,128)(2,1)S(1)}, u32[]{:S(2)}, u32[]{:S(2)}) collective-permute-start(bf16[4,256,128]{2,1,0:T(8,128)(2,1)} %get-tuple-element.24), channel_id=1, source_target_pairs={{0,24},{1,25},{2,26},{3,27},{4,28},{5,29},{6,30},{7,31},{8,0},{9,1... | collective-permute-start | bytes 786440 | tf_op jit(solution)/shard_map/ppermute | solution.py:375
  69.0 0.0 collective-permute-done.other_ref
  69.0 0.0 copy-done
  69.0 0.0 copy-done.5
  69.0 0.0 copy-done.6
  69.1 0.0 copy-done.2
  69.1 2.9 %project.1 = (f32[128,128]{1,0:T(8,128)S(1)}, f32[128,128]{1,0:T(8,128)S(1)}, f32[128,128]{1,0:T(8,128)S(1)}, s32[14]{0:T(128)S(1)}) custom-call(s32[512]{0:T(512)S(1)} %copy-done.4, s32[512]{0:T(512)S(1)} %copy-done.5, f32[1]{0:T(128)S(6)} %copy.19.decay_ref, f32[1,128]{1,0:T(1,128)S(1)} %bitcast.24, bf16[16,128,128]{2,1,0:T(8,128)(2,1)S(1)} %all-gather.1.own_ref, ...), custom_call_target="tpu_custom_call" | custom-call | flops 402653184 | bytes 6291456 | tf_op jit(solution)/shard_map/project/pallas_call | solution.py:332
  71.9 2.5 %all-to-all-done.1.incoming_ref = bf16[20,128,128]{2,1,0:T(8,128)(2,1)} async-done(((bf16[20,128,128]{2,1,0:T(8,128)(2,1)}), bf16[20,128,128]{2,1,0:T(8,128)(2,1)}, u32[]{:S(2)}, u32[]{:S(2)}) %all-to-all-start.1) | async-done | bytes 655392 | tf_op jit(solution)/shard_map/all_to_all | solution.py:327
  74.4 1.4 %finish.1 = bf16[128,128]{1,0:T(8,128)(2,1)S(1)} custom-call(s32[14]{0:T(128)S(1)} %get-tuple-element.17.code_ref, f32[128,128]{1,0:T(8,128)S(1)} %get-tuple-element.18.scaled_ref, f32[128,128]{1,0:T(8,128)S(1)} %get-tuple-element.19.partial_ref, f32[128,128]{1,0:T(8,128)S(1)} %get-tuple-element.20.gains_ref, bf16[20,128,128]{2,1,0:T(8,128)(2,1)} %all-to-all-done.1.incoming_ref), custom_call_target="tpu_custom_call" | custom-call | tf_op jit(solution)/shard_map/finish/pallas_call | solution.py:377
  75.8 13.2 %all-gather.2 = bf16[1024,128]{1,0:T(8,128)(2,1)S(1)} all-gather(bf16[128,128]{1,0:T(8,128)(2,1)S(1)} %finish.1), channel_id=4, replica_groups={{0,1,8,9,16,17,24,25},{2,3,10,11,18,19,26,27},{4,5,12,13,20,21,28,29},{..., dimensions={0}, use_global_device_ids=true | all-gather | bytes 294912 | tf_op jit(solution)/shard_map/all_gather | solution.py:386
  89.0 0.0 collective-permute-done.2.refs_1_
  89.0 0.0 collective-permute-done.3.refs_2_
  89.0 0.0 collective-permute-done.4.refs_3_
  89.0 0.4 output.1
  89.5 8.9 %all_to_all.15 = bf16[4,128,128]{2,1,0:T(8,128)(2,1)S(1)} all-to-all(bf16[4,128,128]{2,1,0:T(8,128)(2,1)S(1)} %output.1), channel_id=1, replica_groups={{0,2,4,6},{1,3,5,7},{8,10,12,14},{9,11,13,15},{16,18,20,22},{17,19,21,2..., dimensions={0} | all-to-all | bytes 262144 | tf_op jit(solution)/shard_map/all_to_all | solution.py:395
  98.4 0.6 reduce_sum.45
  (7 shorter events, 0.0 us)
Async XLA Ops:
  0.0 12.5 %copy-start.4 = (s32[512]{0:T(512)S(1)}, s32[512]{0:T(512)}, u32[]{:S(2)}) copy-start(s32[512]{0:T(512)} %plan_ref.1) | copy-start | bytes 6148
  3.1 36.6 %copy-start.1 = (bf16[128,4096]{1,0:T(8,128)(2,1)S(1)}, bf16[128,4096]{1,0:T(8,128)(2,1)}, u32[]{:S(2)}) copy-start(bf16[128,4096]{1,0:T(8,128)(2,1)} %weight_ref.3) | copy-start | bytes 3145732
  3.1 24.0 %all-to-all-start = ((bf16[32,128,128]{2,1,0:T(8,128)(2,1)}), bf16[32,128,128]{2,1,0:T(8,128)(2,1)S(1)}, u32[]{:S(2)}, u32[]{:S(2)}) async-start(bf16[32,128,128]{2,1,0:T(8,128)(2,1)} %get-tuple-element.16), calls=%async_computation | async-start | bytes 2097152 | tf_op jit(solution)/shard_map/all_to_all | solution.py:316
  27.1 12.7 %copy-start.3 = (bf16[512,128]{1,0:T(8,128)(2,1)}, bf16[512,128]{1,0:T(8,128)(2,1)S(1)}, u32[]{:S(2)}) copy-start(bf16[512,128]{1,0:T(8,128)(2,1)S(1)} %all-gather) | copy-start | bytes 393220
  28.7 40.4 %copy-start = (f32[32,1,128,128]{3,2,1,0:T(8,128)S(1)}, f32[32,1,128,128]{3,2,1,0:T(8,128)}, u32[]{:S(2)}) copy-start(f32[32,1,128,128]{3,2,1,0:T(8,128)} %param.13) | copy-start | bytes 6291460
  28.7 40.4 %copy-start.5 = (s32[512]{0:T(512)S(1)}, s32[512]{0:T(512)}, u32[]{:S(2)}) copy-start(s32[512]{0:T(512)} %remaining_ref.1) | copy-start | bytes 6148
  28.7 40.4 %copy-start.6 = (f32[128]{0:T(128)S(1)}, f32[128]{0:T(128)}, u32[]{:S(2)}) copy-start(f32[128]{0:T(128)} %param.11) | copy-start | bytes 1540
  28.7 45.7 %all-to-all-start.1 = ((bf16[20,128,128]{2,1,0:T(8,128)(2,1)}), bf16[20,128,128]{2,1,0:T(8,128)(2,1)}, u32[]{:S(2)}, u32[]{:S(2)}) async-start(bf16[20,128,128]{2,1,0:T(8,128)(2,1)} %pass_on.1.dep_ref), calls=%async_computation.1 | async-start | bytes 1310720 | tf_op jit(solution)/shard_map/all_to_all | solution.py:327
  39.8 29.3 %copy-start.2 = (bf16[4096,3,128]{2,0,1:T(8,128)(2,1)S(1)}, bf16[4096,3,128]{2,0,1:T(8,128)(2,1)}, u32[]{:S(2)}) copy-start(bf16[4096,3,128]{2,0,1:T(8,128)(2,1)} %param.9) | copy-start | bytes 9437188
  39.9 17.6 %collective-permute-start.1 = (bf16[4,4,128,128]{3,2,1,0:T(8,128)(2,1)S(1)}, bf16[4,4,128,128]{3,2,1,0:T(8,128)(2,1)S(1)}, u32[]{:S(2)}, u32[]{:S(2)}) collective-permute-start(bf16[4,4,128,128]{3,2,1,0:T(8,128)(2,1)S(1)} %lend.1), channel_id=1, source_target_pairs={{0,1},{1,0},{2,3},{3,2},{4,5},{5,4},{6,7},{7,6},{8,9},{9,8},{10,11... | collective-permute-start | bytes 1572872 | tf_op jit(solution)/shard_map/ppermute | solution.py:366
  55.6 13.5 %collective-permute-start = (bf16[16,128,128]{2,1,0:T(8,128)(2,1)S(1)}, bf16[16,128,128]{2,1,0:T(8,128)(2,1)S(1)}, u32[]{:S(2)}, u32[]{:S(2)}) collective-permute-start(bf16[16,128,128]{2,1,0:T(8,128)(2,1)S(1)} %all-gather.1.own_ref), channel_id=1, source_target_pairs={{0,1},{1,0},{2,3},{3,2},{4,5},{5,4},{6,7},{7,6},{8,9},{9,8},{10,11... | collective-permute-start | bytes 1572872 | tf_op jit(solution)/shard_map/ppermute | solution.py:331
  58.5 30.5 %collective-permute-start.2 = (bf16[4,256,128]{2,1,0:T(8,128)(2,1)}, bf16[4,256,128]{2,1,0:T(8,128)(2,1)S(1)}, u32[]{:S(2)}, u32[]{:S(2)}) collective-permute-start(bf16[4,256,128]{2,1,0:T(8,128)(2,1)} %get-tuple-element.22), channel_id=1, source_target_pairs={{0,8},{1,9},{2,10},{3,11},{4,12},{5,13},{6,14},{7,15},{8,16},{9,17... | collective-permute-start | bytes 786440 | tf_op jit(solution)/shard_map/ppermute | solution.py:375
  61.8 27.2 %collective-permute-start.3 = (bf16[4,256,128]{2,1,0:T(8,128)(2,1)}, bf16[4,256,128]{2,1,0:T(8,128)(2,1)S(1)}, u32[]{:S(2)}, u32[]{:S(2)}) collective-permute-start(bf16[4,256,128]{2,1,0:T(8,128)(2,1)} %get-tuple-element.23), channel_id=1, source_target_pairs={{0,16},{1,17},{2,18},{3,19},{4,20},{5,21},{6,22},{7,23},{8,24},{9,... | collective-permute-start | bytes 786440 | tf_op jit(solution)/shard_map/ppermute | solution.py:375
  66.4 22.6 %collective-permute-start.4 = (bf16[4,256,128]{2,1,0:T(8,128)(2,1)}, bf16[4,256,128]{2,1,0:T(8,128)(2,1)S(1)}, u32[]{:S(2)}, u32[]{:S(2)}) collective-permute-start(bf16[4,256,128]{2,1,0:T(8,128)(2,1)} %get-tuple-element.24), channel_id=1, source_target_pairs={{0,24},{1,25},{2,26},{3,27},{4,28},{5,29},{6,30},{7,31},{8,0},{9,1... | collective-permute-start | bytes 786440 | tf_op jit(solution)/shard_map/ppermute | solution.py:375

commit v7 on v6

--- a/solution.py
+++ b/solution.py
@@ -73,20 +73,31 @@
 
 
 def pack_kernel(
-    rows, plan_ref, states_ref, inputs_ref, out_ref, same_ref,
-    wide_ref, narrow_ref, inputs_vmem, slot_ref, seen_ref, in_sem, out_sem, copy_sem,
+    rows, plan_hbm, states_hbm, inputs_hbm, out_ref, same_ref,
+    plan_ref, states_ref, inputs_ref, narrow_ref, seen_ref, in_sem, out_sem,
 ):
     group = group_here()
-    load = pltpu.make_async_copy(inputs_ref, inputs_vmem, copy_sem.at[0])
-    load.start()
+    loads = [
+        pltpu.make_async_copy(plan_hbm, plan_ref, in_sem.at[0]),
+        pltpu.make_async_copy(inputs_hbm, inputs_ref, in_sem.at[1]),
+        pltpu.make_async_copy(states_hbm, states_ref, in_sem.at[2]),
+    ]
+    for load in loads:
+        load.start()
     for i in range(ZH * YS):
         seen_ref[i] = 0
-
+    loads[0].wait()
     plan = plan_ref[...] - group * rows
     everyone = lax.broadcasted_iota(jnp.int32, plan.shape, 0) * plan.shape[1]
     everyone = everyone + lax.broadcasted_iota(jnp.int32, plan.shape, 1)
     everyone = everyone.astype(jnp.float32)
-    targets = [jnp.max(jnp.where(plan == row, everyone, 0.0)).astype(jnp.int32) for row in range(rows)]
+    targets = [
+        jnp.max(jnp.where(plan == row, everyone, 0.0)).astype(jnp.int32) for row in range(rows)
+    ]
+    loads[1].wait()
+    store = pltpu.make_async_copy(inputs_ref, same_ref, out_sem.at[MOVED])
+    store.start()
+    loads[2].wait()
     count = jnp.int32(0)
     for row in range(rows):
         goal = lax.shift_right_logical(targets[row], rows.bit_length() - 1)
@@ -96,28 +107,16 @@
         def _(row=row, goal=goal, count=count):
             rank = seen_ref[goal]
             seen_ref[goal] = rank + 1
-            slot_ref[count] = (
+            slot = (
                 lax.rem(goal, YS) * (ZH * SLOTS) + lax.div(goal, YS) * SLOTS
                 + jnp.minimum(rank, SLOTS - 1)
             )
+            narrow_ref[count] = states_ref[row].astype(jnp.bfloat16)
             pltpu.make_async_copy(
-                states_ref.at[row], wide_ref.at[count], in_sem.at[count]
+                narrow_ref.at[count], out_ref.at[slot], out_sem.at[count]
             ).start()
 
         count = count + leaves.astype(jnp.int32)
-    load.wait()
-    store = pltpu.make_async_copy(inputs_vmem, same_ref, copy_sem.at[1])
-    store.start()
-    for i in range(MOVED):
-
-        @pl.when(i < count)
-        def _(i=i):
-            pltpu.make_async_copy(states_ref.at[0], wide_ref.at[i], in_sem.at[i]).wait()
-            narrow_ref[i] = wide_ref[i].astype(jnp.bfloat16)
-            pltpu.make_async_copy(
-                narrow_ref.at[i], out_ref.at[slot_ref[i]], out_sem.at[i]
-            ).start()
-
     for i in range(MOVED):
 
         @pl.when(i < count)
@@ -127,13 +126,14 @@
     store.wait()
 
 
-def pass_kernel(index_ref, rows_ref, dep_ref, out_ref, sem):
-    copies = [
-        pltpu.make_async_copy(rows_ref.at[index_ref[i]], out_ref.at[i], sem.at[i])
-        for i in range(out_ref.shape[0])
-    ]
-    for copy in copies:
-        copy.start()
+def pass_kernel(index_ref, rows_ref, dep_ref, out_ref, held_ref, sem):
+    copies = []
+    for z in range(ZH):
+        part = pl.ds(z * PASSING, PASSING)
+        for i in range(z * PASSING, (z + 1) * PASSING):
+            held_ref[i] = rows_ref[index_ref[i]]
+        copies.append(pltpu.make_async_copy(held_ref.at[part], out_ref.at[part], sem.at[z]))
+        copies[z].start()
     for copy in copies:
         copy.wait()
 
@@ -298,17 +298,16 @@
             jax.ShapeDtypeStruct((groups * SLOTS, SIZE, SIZE), bf16),
             jax.ShapeDtypeStruct((count, SIZE), bf16),
         ],
-        in_specs=[VMEM, ANY, ANY],
+        in_specs=[ANY, ANY, ANY],
         out_specs=[ANY, ANY],
         scratch_shapes=[
-            pltpu.VMEM((MOVED, SIZE, SIZE), f32),
+            pltpu.VMEM((ZH, YS * rows), jnp.int32),
+            pltpu.VMEM((rows, SIZE, SIZE), f32),
+            pltpu.VMEM((count, SIZE), bf16),
             pltpu.VMEM((MOVED, SIZE, SIZE), bf16),
-            pltpu.VMEM((count, SIZE), bf16),
-            pltpu.SMEM((MOVED,), jnp.int32),
             pltpu.SMEM((ZH * YS,), jnp.int32),
-            DMA((MOVED,)),
-            DMA((MOVED,)),
-            DMA((2,)),
+            DMA((3,)),
+            DMA((MOVED + 1,)),
         ],
         compiler_params=ROOMY,
         name="pack",
@@ -320,7 +319,7 @@
         out_shape=jax.ShapeDtypeStruct((ZH * PASSING, SIZE, SIZE), bf16),
         in_specs=[SMEM, VMEM, VMEM],
         out_specs=ANY,
-        scratch_shapes=[DMA((ZH * PASSING,))],
+        scratch_shapes=[pltpu.VMEM((ZH * PASSING, SIZE, SIZE), bf16), DMA((ZH,))],
         compiler_params=SMALL,
         name="pass_on",
     )(rows_on(migration_plan, own_group, groups, rows), passing, line)

time: 99.5 us -> 99 us (level)
  no operation moved by 1% of the time
where the time goes in v7:
time: 99 us; the launch traced here: 98.5 us
  blocking collectives  49.2 us (50%)
  starting transfers between devices  34.1 us (34%)
  Pallas kernels  10.1 us (10%)
  waiting for transfers between devices  2.47 us (2%)
  other arithmetic  1.38 us (1%)
    all_gather x1, blocking collectives, body(): lax.all_gather(after(line, passing), 'tensor', axis=0, axis_index_groups=...  13.6 us
    all_gather x1, blocking collectives, body(): line = lax.all_gather(inputs, 'tensor', axis=0, axis_index_groups=Z_LINES)  13.6 us
    all_gather x1, blocking collectives, body(): ring = lax.all_gather(normed, 'tensor', axis=0, axis_index_groups=X_CORES)  13.2 us
    all_to_all x1, starting transfers between devices, body(): lax.all_to_all(passing, 'group', 0, 0, tiled=True, axis_index_groups=Z_RI...  11 us
    ppermute x3, starting transfers between devices, body(): lax.ppermute(dealt[k], 'tensor', X_SHIFTS[k])  9.8 us
    all_to_all x1, starting transfers between devices, body(): lax.all_to_all(outgoing, 'group', 0, 0, tiled=True, axis_index_groups=Y_R...  9.32 us
    all_to_all x1, blocking collectives, body(): lax.all_to_all(sums, 'tensor', 0, 0, tiled=True, axis_index_groups=Z_LINES)  8.89 us
    pallas_call x1, Pallas kernels, body(): pl.pallas_call(functools.partial(project_kernel, rows), out_shape=[jax.Sh...  2.86 us
  transfers between devices with their start and end apart: 7, of which 1 were waited for; matrix products, arithmetic and copies ran while one was open for 1% of the time, Pallas kernels for 6%

profile of v7, /device:TPU:16, one launch (start us, length us, event | category | flops | bytes accessed | tf_op | source)
XLA Modules:
  0.0 98.5 jit_solution(1156217093406648670)
XLA Ops:
  0.0 0.0 copy-start.4
  0.0 2.7 %pack.1 = (bf16[32,128,128]{2,1,0:T(8,128)(2,1)}, bf16[128,128]{1,0:T(8,128)(2,1)}) custom-call(s32[4,128]{1,0:T(4,128)} %bitcast.23, f32[32,128,128]{2,1,0:T(8,128)} %bitcast.17, bf16[128,128]{1,0:T(8,128)(2,1)} %bitcast.25), custom_call_target="tpu_custom_call" | custom-call | tf_op jit(solution)/shard_map/pack/pallas_call | solution.py:295
  2.7 0.0 copy-start.1
  2.7 9.3 %all-to-all-start = ((bf16[32,128,128]{2,1,0:T(8,128)(2,1)}), bf16[32,128,128]{2,1,0:T(8,128)(2,1)S(1)}, u32[]{:S(2)}, u32[]{:S(2)}) async-start(bf16[32,128,128]{2,1,0:T(8,128)(2,1)} %get-tuple-element.16), calls=%async_computation | async-start | bytes 2097152 | tf_op jit(solution)/shard_map/all_to_all | solution.py:315
  12.1 0.0 copy-done.4
  12.1 0.1 reshape.96
  12.2 0.1 compare_and_fusion
  12.3 0.1 convert_reduce_fusion.1
  12.4 0.2 convert_reduce_fusion
  12.7 0.1 fusion.4
  12.8 0.2 select_reduce_fusion
  13.0 0.1 copy.14
  13.0 0.1 min.12.index_ref
  13.1 13.6 %all-gather = bf16[512,128]{1,0:T(8,128)(2,1)S(1)} all-gather(bf16[128,128]{1,0:T(8,128)(2,1)} %get-tuple-element.15), channel_id=2, replica_groups={{0,2,4,6},{1,3,5,7},{8,10,12,14},{9,11,13,15},{16,18,20,22},{17,19,21,2..., dimensions={0}, use_global_device_ids=true | all-gather | bytes 163840 | tf_op jit(solution)/shard_map/all_gather | solution.py:316
  26.7 0.0 copy-start.3
  26.7 0.0 all-to-all-done.rows_ref
  26.7 1.4 %pass_on.1.dep_ref = bf16[20,128,128]{2,1,0:T(8,128)(2,1)} custom-call(s32[20]{0:T(128)S(1)} %min.12.index_ref, bf16[32,128,128]{2,1,0:T(8,128)(2,1)S(1)} %all-to-all-done.rows_ref, bf16[4,128,128]{2,1,0:T(8,128)(2,1)S(1)} %bitcast.20), custom_call_target="tpu_custom_call" | custom-call | tf_op jit(solution)/shard_map/pass_on/pallas_call | solution.py:317
  28.2 0.0 copy-start
  28.2 0.0 copy-start.5
  28.2 0.0 copy-start.6
  28.2 11.0 %all-to-all-start.1 = ((bf16[20,128,128]{2,1,0:T(8,128)(2,1)}), bf16[20,128,128]{2,1,0:T(8,128)(2,1)}, u32[]{:S(2)}, u32[]{:S(2)}) async-start(bf16[20,128,128]{2,1,0:T(8,128)(2,1)} %pass_on.1.dep_ref), calls=%async_computation.1 | async-start | bytes 1310720 | tf_op jit(solution)/shard_map/all_to_all | solution.py:326
  39.2 0.0 copy-done.3
  39.2 0.0 copy-done.1
  39.2 0.0 copy-start.2
  39.2 0.2 lend.1
  39.4 2.1 %collective-permute-start.1 = (bf16[4,4,128,128]{3,2,1,0:T(8,128)(2,1)S(1)}, bf16[4,4,128,128]{3,2,1,0:T(8,128)(2,1)S(1)}, u32[]{:S(2)}, u32[]{:S(2)}) collective-permute-start(bf16[4,4,128,128]{3,2,1,0:T(8,128)(2,1)S(1)} %lend.1), channel_id=1, source_target_pairs={{0,1},{1,0},{2,3},{3,2},{4,5},{5,4},{6,7},{7,6},{8,9},{9,8},{10,11... | collective-permute-start | bytes 1572872 | tf_op jit(solution)/shard_map/ppermute | solution.py:365
  41.5 13.6 %all-gather.1.own_ref = bf16[16,128,128]{2,1,0:T(8,128)(2,1)S(1)} all-gather(bf16[4,128,128]{2,1,0:T(8,128)(2,1)} %after.1), channel_id=3, replica_groups={{0,8,16,24},{1,9,17,25},{2,10,18,26},{3,11,19,27},{4,12,20,28},{5,13,21..., dimensions={0}, use_global_device_ids=true | all-gather | bytes 655360 | tf_op jit(solution)/shard_map/all_gather | solution.py:328
  55.0 1.9 %collective-permute-start = (bf16[16,128,128]{2,1,0:T(8,128)(2,1)S(1)}, bf16[16,128,128]{2,1,0:T(8,128)(2,1)S(1)}, u32[]{:S(2)}, u32[]{:S(2)}) collective-permute-start(bf16[16,128,128]{2,1,0:T(8,128)(2,1)S(1)} %all-gather.1.own_ref), channel_id=1, source_target_pairs={{0,1},{1,0},{2,3},{3,2},{4,5},{5,4},{6,7},{7,6},{8,9},{9,8},{10,11... | collective-permute-start | bytes 1572872 | tf_op jit(solution)/shard_map/ppermute | solution.py:330
  57.0 0.0 collective-permute-done.1.lent_ref
  57.0 1.1 %deal.1 = (bf16[4,256,128]{2,1,0:T(8,128)(2,1)S(1)}, bf16[4,256,128]{2,1,0:T(8,128)(2,1)}, bf16[4,256,128]{2,1,0:T(8,128)(2,1)}, bf16[4,256,128]{2,1,0:T(8,128)(2,1)}) custom-call(bf16[128,4096]{1,0:T(8,128)(2,1)S(1)} %copy-done.1, bf16[4,4,128,128]{3,2,1,0:T(8,128)(2,1)S(1)} %collective-permute-done.1.lent_ref), custom_call_target="tpu_custom_call" | custom-call | tf_op jit(solution)/shard_map/deal/pallas_call | solution.py:366
  58.0 3.3 %collective-permute-start.2 = (bf16[4,256,128]{2,1,0:T(8,128)(2,1)}, bf16[4,256,128]{2,1,0:T(8,128)(2,1)S(1)}, u32[]{:S(2)}, u32[]{:S(2)}) collective-permute-start(bf16[4,256,128]{2,1,0:T(8,128)(2,1)} %get-tuple-element.22), channel_id=1, source_target_pairs={{0,8},{1,9},{2,10},{3,11},{4,12},{5,13},{6,14},{7,15},{8,16},{9,17... | collective-permute-start | bytes 786440 | tf_op jit(solution)/shard_map/ppermute | solution.py:374
  61.3 4.6 %collective-permute-start.3 = (bf16[4,256,128]{2,1,0:T(8,128)(2,1)}, bf16[4,256,128]{2,1,0:T(8,128)(2,1)S(1)}, u32[]{:S(2)}, u32[]{:S(2)}) collective-permute-start(bf16[4,256,128]{2,1,0:T(8,128)(2,1)} %get-tuple-element.23), channel_id=1, source_target_pairs={{0,16},{1,17},{2,18},{3,19},{4,20},{5,21},{6,22},{7,23},{8,24},{9,... | collective-permute-start | bytes 786440 | tf_op jit(solution)/shard_map/ppermute | solution.py:374
  65.9 2.0 %collective-permute-start.4 = (bf16[4,256,128]{2,1,0:T(8,128)(2,1)}, bf16[4,256,128]{2,1,0:T(8,128)(2,1)S(1)}, u32[]{:S(2)}, u32[]{:S(2)}) collective-permute-start(bf16[4,256,128]{2,1,0:T(8,128)(2,1)} %get-tuple-element.24), channel_id=1, source_target_pairs={{0,24},{1,25},{2,26},{3,27},{4,28},{5,29},{6,30},{7,31},{8,0},{9,1... | collective-permute-start | bytes 786440 | tf_op jit(solution)/shard_map/ppermute | solution.py:374
  68.5 0.0 collective-permute-done.other_ref
  68.5 0.0 copy-done
  68.5 0.0 copy-done.5
  68.5 0.0 copy-done.6
  68.5 0.0 copy-done.2
  68.5 2.9 %project.1 = (f32[128,128]{1,0:T(8,128)S(1)}, f32[128,128]{1,0:T(8,128)S(1)}, f32[128,128]{1,0:T(8,128)S(1)}, s32[14]{0:T(128)S(1)}) custom-call(s32[512]{0:T(512)S(1)} %copy-done.4, s32[512]{0:T(512)S(1)} %copy-done.5, f32[1]{0:T(128)S(6)} %copy.19.decay_ref, f32[1,128]{1,0:T(1,128)S(1)} %bitcast.24, bf16[16,128,128]{2,1,0:T(8,128)(2,1)S(1)} %all-gather.1.own_ref, ...), custom_call_target="tpu_custom_call" | custom-call | flops 402653184 | bytes 6291456 | tf_op jit(solution)/shard_map/project/pallas_call | solution.py:331
  71.4 2.5 %all-to-all-done.1.incoming_ref = bf16[20,128,128]{2,1,0:T(8,128)(2,1)} async-done(((bf16[20,128,128]{2,1,0:T(8,128)(2,1)}), bf16[20,128,128]{2,1,0:T(8,128)(2,1)}, u32[]{:S(2)}, u32[]{:S(2)}) %all-to-all-start.1) | async-done | bytes 655392 | tf_op jit(solution)/shard_map/all_to_all | solution.py:326
  73.9 1.4 %finish.1 = bf16[128,128]{1,0:T(8,128)(2,1)S(1)} custom-call(s32[14]{0:T(128)S(1)} %get-tuple-element.17.code_ref, f32[128,128]{1,0:T(8,128)S(1)} %get-tuple-element.18.scaled_ref, f32[128,128]{1,0:T(8,128)S(1)} %get-tuple-element.19.partial_ref, f32[128,128]{1,0:T(8,128)S(1)} %get-tuple-element.20.gains_ref, bf16[20,128,128]{2,1,0:T(8,128)(2,1)} %all-to-all-done.1.incoming_ref), custom_call_target="tpu_custom_call" | custom-call | tf_op jit(solution)/shard_map/finish/pallas_call | solution.py:376
  75.3 13.2 %all-gather.2 = bf16[1024,128]{1,0:T(8,128)(2,1)S(1)} all-gather(bf16[128,128]{1,0:T(8,128)(2,1)S(1)} %finish.1), channel_id=4, replica_groups={{0,1,8,9,16,17,24,25},{2,3,10,11,18,19,26,27},{4,5,12,13,20,21,28,29},{..., dimensions={0}, use_global_device_ids=true | all-gather | bytes 294912 | tf_op jit(solution)/shard_map/all_gather | solution.py:385
  88.5 0.0 collective-permute-done.2.refs_1_
  88.5 0.0 collective-permute-done.3.refs_2_
  88.5 0.0 collective-permute-done.4.refs_3_
  88.5 0.4 output.1
  89.0 8.9 %all_to_all.15 = bf16[4,128,128]{2,1,0:T(8,128)(2,1)S(1)} all-to-all(bf16[4,128,128]{2,1,0:T(8,128)(2,1)S(1)} %output.1), channel_id=1, replica_groups={{0,2,4,6},{1,3,5,7},{8,10,12,14},{9,11,13,15},{16,18,20,22},{17,19,21,2..., dimensions={0} | all-to-all | bytes 262144 | tf_op jit(solution)/shard_map/all_to_all | solution.py:394
  97.8 0.6 reduce_sum.45
  (7 shorter events, 0.0 us)
Async XLA Ops:
  0.0 12.1 %copy-start.4 = (s32[512]{0:T(512)S(1)}, s32[512]{0:T(512)}, u32[]{:S(2)}) copy-start(s32[512]{0:T(512)} %plan_ref.1) | copy-start | bytes 6148
  2.7 36.5 %copy-start.1 = (bf16[128,4096]{1,0:T(8,128)(2,1)S(1)}, bf16[128,4096]{1,0:T(8,128)(2,1)}, u32[]{:S(2)}) copy-start(bf16[128,4096]{1,0:T(8,128)(2,1)} %weight_ref.3) | copy-start | bytes 3145732
  2.7 24.0 %all-to-all-start = ((bf16[32,128,128]{2,1,0:T(8,128)(2,1)}), bf16[32,128,128]{2,1,0:T(8,128)(2,1)S(1)}, u32[]{:S(2)}, u32[]{:S(2)}) async-start(bf16[32,128,128]{2,1,0:T(8,128)(2,1)} %get-tuple-element.16), calls=%async_computation | async-start | bytes 2097152 | tf_op jit(solution)/shard_map/all_to_all | solution.py:315
  26.7 12.5 %copy-start.3 = (bf16[512,128]{1,0:T(8,128)(2,1)}, bf16[512,128]{1,0:T(8,128)(2,1)S(1)}, u32[]{:S(2)}) copy-start(bf16[512,128]{1,0:T(8,128)(2,1)S(1)} %all-gather) | copy-start | bytes 393220
  28.2 40.4 %copy-start = (f32[32,1,128,128]{3,2,1,0:T(8,128)S(1)}, f32[32,1,128,128]{3,2,1,0:T(8,128)}, u32[]{:S(2)}) copy-start(f32[32,1,128,128]{3,2,1,0:T(8,128)} %param.13) | copy-start | bytes 6291460
  28.2 40.4 %copy-start.5 = (s32[512]{0:T(512)S(1)}, s32[512]{0:T(512)}, u32[]{:S(2)}) copy-start(s32[512]{0:T(512)} %remaining_ref.1) | copy-start | bytes 6148
  28.2 40.3 %copy-start.6 = (f32[128]{0:T(128)S(1)}, f32[128]{0:T(128)}, u32[]{:S(2)}) copy-start(f32[128]{0:T(128)} %param.11) | copy-start | bytes 1540
  28.2 45.7 %all-to-all-start.1 = ((bf16[20,128,128]{2,1,0:T(8,128)(2,1)}), bf16[20,128,128]{2,1,0:T(8,128)(2,1)}, u32[]{:S(2)}, u32[]{:S(2)}) async-start(bf16[20,128,128]{2,1,0:T(8,128)(2,1)} %pass_on.1.dep_ref), calls=%async_computation.1 | async-start | bytes 1310720 | tf_op jit(solution)/shard_map/all_to_all | solution.py:326
  39.2 29.3 %copy-start.2 = (bf16[4096,3,128]{2,0,1:T(8,128)(2,1)S(1)}, bf16[4096,3,128]{2,0,1:T(8,128)(2,1)}, u32[]{:S(2)}) copy-start(bf16[4096,3,128]{2,0,1:T(8,128)(2,1)} %param.9) | copy-start | bytes 9437188
  39.4 17.6 %collective-permute-start.1 = (bf16[4,4,128,128]{3,2,1,0:T(8,128)(2,1)S(1)}, bf16[4,4,128,128]{3,2,1,0:T(8,128)(2,1)S(1)}, u32[]{:S(2)}, u32[]{:S(2)}) collective-permute-start(bf16[4,4,128,128]{3,2,1,0:T(8,128)(2,1)S(1)} %lend.1), channel_id=1, source_target_pairs={{0,1},{1,0},{2,3},{3,2},{4,5},{5,4},{6,7},{7,6},{8,9},{9,8},{10,11... | collective-permute-start | bytes 1572872 | tf_op jit(solution)/shard_map/ppermute | solution.py:365
  55.0 13.5 %collective-permute-start = (bf16[16,128,128]{2,1,0:T(8,128)(2,1)S(1)}, bf16[16,128,128]{2,1,0:T(8,128)(2,1)S(1)}, u32[]{:S(2)}, u32[]{:S(2)}) collective-permute-start(bf16[16,128,128]{2,1,0:T(8,128)(2,1)S(1)} %all-gather.1.own_ref), channel_id=1, source_target_pairs={{0,1},{1,0},{2,3},{3,2},{4,5},{5,4},{6,7},{7,6},{8,9},{9,8},{10,11... | collective-permute-start | bytes 1572872 | tf_op jit(solution)/shard_map/ppermute | solution.py:330
  58.0 30.5 %collective-permute-start.2 = (bf16[4,256,128]{2,1,0:T(8,128)(2,1)}, bf16[4,256,128]{2,1,0:T(8,128)(2,1)S(1)}, u32[]{:S(2)}, u32[]{:S(2)}) collective-permute-start(bf16[4,256,128]{2,1,0:T(8,128)(2,1)} %get-tuple-element.22), channel_id=1, source_target_pairs={{0,8},{1,9},{2,10},{3,11},{4,12},{5,13},{6,14},{7,15},{8,16},{9,17... | collective-permute-start | bytes 786440 | tf_op jit(solution)/shard_map/ppermute | solution.py:374
  61.3 27.2 %collective-permute-start.3 = (bf16[4,256,128]{2,1,0:T(8,128)(2,1)}, bf16[4,256,128]{2,1,0:T(8,128)(2,1)S(1)}, u32[]{:S(2)}, u32[]{:S(2)}) collective-permute-start(bf16[4,256,128]{2,1,0:T(8,128)(2,1)} %get-tuple-element.23), channel_id=1, source_target_pairs={{0,16},{1,17},{2,18},{3,19},{4,20},{5,21},{6,22},{7,23},{8,24},{9,... | collective-permute-start | bytes 786440 | tf_op jit(solution)/shard_map/ppermute | solution.py:374
  65.9 22.6 %collective-permute-start.4 = (bf16[4,256,128]{2,1,0:T(8,128)(2,1)}, bf16[4,256,128]{2,1,0:T(8,128)(2,1)S(1)}, u32[]{:S(2)}, u32[]{:S(2)}) collective-permute-start(bf16[4,256,128]{2,1,0:T(8,128)(2,1)} %get-tuple-element.24), channel_id=1, source_target_pairs={{0,24},{1,25},{2,26},{3,27},{4,28},{5,29},{6,30},{7,31},{8,0},{9,1... | collective-permute-start | bytes 786440 | tf_op jit(solution)/shard_map/ppermute | solution.py:374

commit v8 on v7

--- a/solution.py
+++ b/solution.py
@@ -258,7 +258,9 @@
         here = slice(t * rows, (t + 1) * rows)
         readout = partial_ref[here] + moved_ref[t * room : t * room + rows]
         norm = lax.rsqrt(jnp.mean(readout * readout, axis=-1, keepdims=True) + 1e-05)
-        normed_ref[here] = (readout * norm * gains_ref[here]).astype(jnp.bfloat16)
+        normed = (readout * norm * gains_ref[here]).astype(jnp.bfloat16)
+        for i in range(normed_ref.shape[0]):
+            normed_ref[i, here] = normed
 
 
 def output_kernel(ring_ref, *refs):
@@ -375,14 +377,14 @@
 
     normed = pl.pallas_call(
         functools.partial(finish_kernel, rows),
-        out_shape=jax.ShapeDtypeStruct((count, SIZE), bf16),
+        out_shape=jax.ShapeDtypeStruct((XS * CORES, count, SIZE), bf16),
         in_specs=[SMEM, VMEM, VMEM, VMEM, VMEM],
         out_specs=VMEM,
         scratch_shapes=[pltpu.VMEM((STEPS * (rows + 8), SIZE), f32)],
         compiler_params=SMALL,
         name="finish",
     )(code, scaled, partial, gains, incoming)
-    ring = lax.all_gather(normed, "tensor", axis=0, axis_index_groups=X_CORES)
+    ring = lax.all_to_all(normed, "tensor", 0, 0, tiled=True, axis_index_groups=X_CORES)
     sums = pl.pallas_call(
         output_kernel,
         out_shape=jax.ShapeDtypeStruct((ZS, count, SIZE), bf16),

time: 99 us -> 98 us (0.990)
  blocking collectives: 49.2 us -> 35.6 us
  waiting for transfers between devices: 2.47 us -> 9.97 us
  starting transfers between devices: 34.1 us -> 38.5 us
    all_gather x1 -> x0, blocking collectives: 13.2 us -> none  [body(): ring = lax.all_gather(normed, 'tensor', axis=0, axis_index_groups=X_CORES)]
    all_to_all x0 -> x1, waiting for transfers between devices: none -> 7.51 us  [body(): lax.all_to_all(normed, 'tensor', 0, 0, tiled=True, axis_index_groups=X_CO...]
    all_to_all x0 -> x1, starting transfers between devices: none -> 4.3 us  [body(): lax.all_to_all(normed, 'tensor', 0, 0, tiled=True, axis_index_groups=X_CO...]
  transfers between devices with their start and end apart: 7 -> 8, of which waited for: 1 -> 2; matrix products, arithmetic and copies ran while one was open for 1% -> 1% of each run, Pallas kernels for 6% -> 6%
where the time goes in v8:
time: 98 us; the launch traced here: 97.4 us
  starting transfers between devices  38.5 us (39%)
  blocking collectives  35.6 us (36%)
  Pallas kernels  10.8 us (11%)
  waiting for transfers between devices  9.97 us (10%)
  other arithmetic  1.38 us (1%)
    all_gather x1, blocking collectives, body(): lax.all_gather(after(line, passing), 'tensor', axis=0, axis_index_groups=...  13.6 us
    all_gather x1, blocking collectives, body(): line = lax.all_gather(inputs, 'tensor', axis=0, axis_index_groups=Z_LINES)  13.6 us
    all_to_all x1, starting transfers between devices, body(): lax.all_to_all(passing, 'group', 0, 0, tiled=True, axis_index_groups=Z_RI...  11 us
    ppermute x3, starting transfers between devices, body(): lax.ppermute(dealt[k], 'tensor', X_SHIFTS[k])  9.8 us
    all_to_all x1, starting transfers between devices, body(): lax.all_to_all(outgoing, 'group', 0, 0, tiled=True, axis_index_groups=Y_R...  9.34 us
    all_to_all x1, blocking collectives, body(): lax.all_to_all(sums, 'tensor', 0, 0, tiled=True, axis_index_groups=Z_LINES)  8.46 us
    all_to_all x1, waiting for transfers between devices, body(): lax.all_to_all(normed, 'tensor', 0, 0, tiled=True, axis_index_groups=X_CO...  7.51 us
    all_to_all x1, starting transfers between devices, body(): lax.all_to_all(normed, 'tensor', 0, 0, tiled=True, axis_index_groups=X_CO...  4.3 us
  transfers between devices with their start and end apart: 8, of which 2 were waited for; matrix products, arithmetic and copies ran while one was open for 1% of the time, Pallas kernels for 6%

profile of v8, /device:TPU:16, one launch (start us, length us, event | category | flops | bytes accessed | tf_op | source)
XLA Modules:
  0.0 97.4 jit_solution(13746656129752094172)
XLA Ops:
  0.0 0.0 copy-start.4
  0.0 2.7 %pack.1 = (bf16[32,128,128]{2,1,0:T(8,128)(2,1)}, bf16[128,128]{1,0:T(8,128)(2,1)}) custom-call(s32[4,128]{1,0:T(4,128)} %bitcast.21, f32[32,128,128]{2,1,0:T(8,128)} %bitcast.16, bf16[128,128]{1,0:T(8,128)(2,1)} %bitcast.23), custom_call_target="tpu_custom_call" | custom-call | tf_op jit(solution)/shard_map/pack/pallas_call | solution.py:297
  2.7 0.0 copy-start.1
  2.7 9.3 %all-to-all-start = ((bf16[32,128,128]{2,1,0:T(8,128)(2,1)}), bf16[32,128,128]{2,1,0:T(8,128)(2,1)S(1)}, u32[]{:S(2)}, u32[]{:S(2)}) async-start(bf16[32,128,128]{2,1,0:T(8,128)(2,1)} %get-tuple-element.16), calls=%async_computation | async-start | bytes 2097152 | tf_op jit(solution)/shard_map/all_to_all | solution.py:317
  12.1 0.0 copy-done.4
  12.1 0.1 reshape.96
  12.2 0.1 compare_and_fusion
  12.3 0.1 convert_reduce_fusion.1
  12.4 0.2 convert_reduce_fusion
  12.7 0.1 fusion.4
  12.8 0.2 select_reduce_fusion
  13.0 0.1 copy.14
  13.0 0.1 min.12.index_ref
  13.1 13.6 %all-gather = bf16[512,128]{1,0:T(8,128)(2,1)S(1)} all-gather(bf16[128,128]{1,0:T(8,128)(2,1)} %get-tuple-element.15), channel_id=2, replica_groups={{0,2,4,6},{1,3,5,7},{8,10,12,14},{9,11,13,15},{16,18,20,22},{17,19,21,2..., dimensions={0}, use_global_device_ids=true | all-gather | bytes 163840 | tf_op jit(solution)/shard_map/all_gather | solution.py:318
  26.7 0.0 all-to-all-done.rows_ref
  26.7 1.5 %pass_on.1.dep_ref = bf16[20,128,128]{2,1,0:T(8,128)(2,1)} custom-call(s32[20]{0:T(128)S(1)} %min.12.index_ref, bf16[32,128,128]{2,1,0:T(8,128)(2,1)S(1)} %all-to-all-done.rows_ref, bf16[4,128,128]{2,1,0:T(8,128)(2,1)S(1)} %bitcast.19), custom_call_target="tpu_custom_call" | custom-call | tf_op jit(solution)/shard_map/pass_on/pallas_call | solution.py:319
  28.2 0.0 copy-start
  28.2 0.0 copy-start.5
  28.2 0.0 copy-start.6
  28.2 11.0 %all-to-all-start.1 = ((bf16[20,128,128]{2,1,0:T(8,128)(2,1)}), bf16[20,128,128]{2,1,0:T(8,128)(2,1)}, u32[]{:S(2)}, u32[]{:S(2)}) async-start(bf16[20,128,128]{2,1,0:T(8,128)(2,1)} %pass_on.1.dep_ref), calls=%async_computation.1 | async-start | bytes 1310720 | tf_op jit(solution)/shard_map/all_to_all | solution.py:328
  39.2 0.0 copy-done.3
  39.2 0.0 copy-done.1
  39.2 0.0 copy-start.2
  39.3 0.2 lend.1
  39.4 2.1 %collective-permute-start.1 = (bf16[4,4,128,128]{3,2,1,0:T(8,128)(2,1)S(1)}, bf16[4,4,128,128]{3,2,1,0:T(8,128)(2,1)S(1)}, u32[]{:S(2)}, u32[]{:S(2)}) collective-permute-start(bf16[4,4,128,128]{3,2,1,0:T(8,128)(2,1)S(1)} %lend.1), channel_id=1, source_target_pairs={{0,1},{1,0},{2,3},{3,2},{4,5},{5,4},{6,7},{7,6},{8,9},{9,8},{10,11... | collective-permute-start | bytes 1572872 | tf_op jit(solution)/shard_map/ppermute | solution.py:367
  41.5 13.6 %all-gather.1.own_ref = bf16[16,128,128]{2,1,0:T(8,128)(2,1)S(1)} all-gather(bf16[4,128,128]{2,1,0:T(8,128)(2,1)} %after.1), channel_id=3, replica_groups={{0,8,16,24},{1,9,17,25},{2,10,18,26},{3,11,19,27},{4,12,20,28},{5,13,21..., dimensions={0}, use_global_device_ids=true | all-gather | bytes 655360 | tf_op jit(solution)/shard_map/all_gather | solution.py:330
  55.1 1.9 %collective-permute-start = (bf16[16,128,128]{2,1,0:T(8,128)(2,1)S(1)}, bf16[16,128,128]{2,1,0:T(8,128)(2,1)S(1)}, u32[]{:S(2)}, u32[]{:S(2)}) collective-permute-start(bf16[16,128,128]{2,1,0:T(8,128)(2,1)S(1)} %all-gather.1.own_ref), channel_id=1, source_target_pairs={{0,1},{1,0},{2,3},{3,2},{4,5},{5,4},{6,7},{7,6},{8,9},{9,8},{10,11... | collective-permute-start | bytes 1572872 | tf_op jit(solution)/shard_map/ppermute | solution.py:332
  57.6 0.0 collective-permute-done.1.lent_ref
  57.6 1.1 %deal.1 = (bf16[4,256,128]{2,1,0:T(8,128)(2,1)S(1)}, bf16[4,256,128]{2,1,0:T(8,128)(2,1)}, bf16[4,256,128]{2,1,0:T(8,128)(2,1)}, bf16[4,256,128]{2,1,0:T(8,128)(2,1)}) custom-call(bf16[128,4096]{1,0:T(8,128)(2,1)S(1)} %copy-done.1, bf16[4,4,128,128]{3,2,1,0:T(8,128)(2,1)S(1)} %collective-permute-done.1.lent_ref), custom_call_target="tpu_custom_call" | custom-call | tf_op jit(solution)/shard_map/deal/pallas_call | solution.py:368
  58.7 3.3 %collective-permute-start.2 = (bf16[4,256,128]{2,1,0:T(8,128)(2,1)}, bf16[4,256,128]{2,1,0:T(8,128)(2,1)S(1)}, u32[]{:S(2)}, u32[]{:S(2)}) collective-permute-start(bf16[4,256,128]{2,1,0:T(8,128)(2,1)} %get-tuple-element.22), channel_id=1, source_target_pairs={{0,8},{1,9},{2,10},{3,11},{4,12},{5,13},{6,14},{7,15},{8,16},{9,17... | collective-permute-start | bytes 786440 | tf_op jit(solution)/shard_map/ppermute | solution.py:376
  62.0 4.6 %collective-permute-start.3 = (bf16[4,256,128]{2,1,0:T(8,128)(2,1)}, bf16[4,256,128]{2,1,0:T(8,128)(2,1)S(1)}, u32[]{:S(2)}, u32[]{:S(2)}) collective-permute-start(bf16[4,256,128]{2,1,0:T(8,128)(2,1)} %get-tuple-element.23), channel_id=1, source_target_pairs={{0,16},{1,17},{2,18},{3,19},{4,20},{5,21},{6,22},{7,23},{8,24},{9,... | collective-permute-start | bytes 786440 | tf_op jit(solution)/shard_map/ppermute | solution.py:376
  66.6 2.0 %collective-permute-start.4 = (bf16[4,256,128]{2,1,0:T(8,128)(2,1)}, bf16[4,256,128]{2,1,0:T(8,128)(2,1)S(1)}, u32[]{:S(2)}, u32[]{:S(2)}) collective-permute-start(bf16[4,256,128]{2,1,0:T(8,128)(2,1)} %get-tuple-element.24), channel_id=1, source_target_pairs={{0,24},{1,25},{2,26},{3,27},{4,28},{5,29},{6,30},{7,31},{8,0},{9,1... | collective-permute-start | bytes 786440 | tf_op jit(solution)/shard_map/ppermute | solution.py:376
  68.5 0.0 collective-permute-done.other_ref
  68.5 0.0 copy-done
  68.5 0.0 copy-done.5
  68.6 0.0 copy-done.6
  68.6 0.0 copy-done.2
  68.6 2.9 %project.1 = (f32[128,128]{1,0:T(8,128)S(1)}, f32[128,128]{1,0:T(8,128)S(1)}, f32[128,128]{1,0:T(8,128)S(1)}, s32[14]{0:T(128)S(1)}) custom-call(s32[512]{0:T(512)S(1)} %copy-done.4, s32[512]{0:T(512)S(1)} %copy-done.5, f32[1]{0:T(128)S(6)} %copy.19.decay_ref, f32[1,128]{1,0:T(1,128)S(1)} %bitcast.22, bf16[16,128,128]{2,1,0:T(8,128)(2,1)S(1)} %all-gather.1.own_ref, ...), custom_call_target="tpu_custom_call" | custom-call | flops 402653184 | bytes 6291456 | tf_op jit(solution)/shard_map/project/pallas_call | solution.py:333
  71.5 2.4 %all-to-all-done.1.incoming_ref = bf16[20,128,128]{2,1,0:T(8,128)(2,1)} async-done(((bf16[20,128,128]{2,1,0:T(8,128)(2,1)}), bf16[20,128,128]{2,1,0:T(8,128)(2,1)}, u32[]{:S(2)}, u32[]{:S(2)}) %all-to-all-start.1) | async-done | bytes 655392 | tf_op jit(solution)/shard_map/all_to_all | solution.py:328
  73.9 2.2 %finish.1 = bf16[8,128,128]{2,1,0:T(8,128)(2,1)} custom-call(s32[14]{0:T(128)S(1)} %get-tuple-element.17.code_ref, f32[128,128]{1,0:T(8,128)S(1)} %get-tuple-element.18.scaled_ref, f32[128,128]{1,0:T(8,128)S(1)} %get-tuple-element.19.partial_ref, f32[128,128]{1,0:T(8,128)S(1)} %get-tuple-element.20.gains_ref, bf16[20,128,128]{2,1,0:T(8,128)(2,1)} %all-to-all-done.1.incoming_ref), custom_call_target="tpu_custom_call" | custom-call | tf_op jit(solution)/shard_map/finish/pallas_call | solution.py:378
  76.0 4.3 %all-to-all-start.2 = ((bf16[8,128,128]{2,1,0:T(8,128)(2,1)}), bf16[8,128,128]{2,1,0:T(8,128)(2,1)S(1)}, u32[]{:S(2)}, u32[]{:S(2)}) async-start(bf16[8,128,128]{2,1,0:T(8,128)(2,1)} %finish.1), calls=%async_computation.2 | async-start | bytes 524288 | tf_op jit(solution)/shard_map/all_to_all | solution.py:387
  80.3 0.0 collective-permute-done.2.refs_1_
  80.4 0.0 collective-permute-done.3.refs_2_
  80.4 0.0 collective-permute-done.4.refs_3_
  80.4 7.5 %all-to-all-done.2.ring_ref = bf16[8,128,128]{2,1,0:T(8,128)(2,1)S(1)} async-done(((bf16[8,128,128]{2,1,0:T(8,128)(2,1)}), bf16[8,128,128]{2,1,0:T(8,128)(2,1)S(1)}, u32[]{:S(2)}, u32[]{:S(2)}) %all-to-all-start.2) | async-done | bytes 262176 | tf_op jit(solution)/shard_map/all_to_all | solution.py:387
  87.9 0.4 output.1
  88.3 8.5 %all_to_all.20 = bf16[4,128,128]{2,1,0:T(8,128)(2,1)S(1)} all-to-all(bf16[4,128,128]{2,1,0:T(8,128)(2,1)S(1)} %output.1), channel_id=1, replica_groups={{0,2,4,6},{1,3,5,7},{8,10,12,14},{9,11,13,15},{16,18,20,22},{17,19,21,2..., dimensions={0} | all-to-all | bytes 262144 | tf_op jit(solution)/shard_map/all_to_all | solution.py:396
  96.8 0.6 reduce_sum.45
  (8 shorter events, 0.0 us)
Async XLA Ops:
  0.0 12.1 %copy-start.4 = (s32[512]{0:T(512)S(1)}, s32[512]{0:T(512)}, u32[]{:S(2)}) copy-start(s32[512]{0:T(512)} %plan_ref.1) | copy-start | bytes 6148
  2.7 36.5 %copy-start.1 = (bf16[128,4096]{1,0:T(8,128)(2,1)S(1)}, bf16[128,4096]{1,0:T(8,128)(2,1)}, u32[]{:S(2)}) copy-start(bf16[128,4096]{1,0:T(8,128)(2,1)} %weight_ref.3) | copy-start | bytes 3145732
  2.7 24.0 %all-to-all-start = ((bf16[32,128,128]{2,1,0:T(8,128)(2,1)}), bf16[32,128,128]{2,1,0:T(8,128)(2,1)S(1)}, u32[]{:S(2)}, u32[]{:S(2)}) async-start(bf16[32,128,128]{2,1,0:T(8,128)(2,1)} %get-tuple-element.16), calls=%async_computation | async-start | bytes 2097152 | tf_op jit(solution)/shard_map/all_to_all | solution.py:317
  26.7 12.6 %copy-start.3 = (bf16[512,128]{1,0:T(8,128)(2,1)}, bf16[512,128]{1,0:T(8,128)(2,1)S(1)}, u32[]{:S(2)}) copy-start(bf16[512,128]{1,0:T(8,128)(2,1)S(1)} %all-gather) | copy-start | bytes 393220
  28.2 40.4 %copy-start = (f32[32,1,128,128]{3,2,1,0:T(8,128)S(1)}, f32[32,1,128,128]{3,2,1,0:T(8,128)}, u32[]{:S(2)}) copy-start(f32[32,1,128,128]{3,2,1,0:T(8,128)} %param.13) | copy-start | bytes 6291460
  28.2 40.4 %copy-start.5 = (s32[512]{0:T(512)S(1)}, s32[512]{0:T(512)}, u32[]{:S(2)}) copy-start(s32[512]{0:T(512)} %remaining_ref.1) | copy-start | bytes 6148
  28.2 40.4 %copy-start.6 = (f32[128]{0:T(128)S(1)}, f32[128]{0:T(128)}, u32[]{:S(2)}) copy-start(f32[128]{0:T(128)} %param.11) | copy-start | bytes 1540
  28.2 45.7 %all-to-all-start.1 = ((bf16[20,128,128]{2,1,0:T(8,128)(2,1)}), bf16[20,128,128]{2,1,0:T(8,128)(2,1)}, u32[]{:S(2)}, u32[]{:S(2)}) async-start(bf16[20,128,128]{2,1,0:T(8,128)(2,1)} %pass_on.1.dep_ref), calls=%async_computation.1 | async-start | bytes 1310720 | tf_op jit(solution)/shard_map/all_to_all | solution.py:328
  39.2 29.3 %copy-start.2 = (bf16[4096,3,128]{2,0,1:T(8,128)(2,1)S(1)}, bf16[4096,3,128]{2,0,1:T(8,128)(2,1)}, u32[]{:S(2)}) copy-start(bf16[4096,3,128]{2,0,1:T(8,128)(2,1)} %param.9) | copy-start | bytes 9437188
  39.4 18.2 %collective-permute-start.1 = (bf16[4,4,128,128]{3,2,1,0:T(8,128)(2,1)S(1)}, bf16[4,4,128,128]{3,2,1,0:T(8,128)(2,1)S(1)}, u32[]{:S(2)}, u32[]{:S(2)}) collective-permute-start(bf16[4,4,128,128]{3,2,1,0:T(8,128)(2,1)S(1)} %lend.1), channel_id=1, source_target_pairs={{0,1},{1,0},{2,3},{3,2},{4,5},{5,4},{6,7},{7,6},{8,9},{9,8},{10,11... | collective-permute-start | bytes 1572872 | tf_op jit(solution)/shard_map/ppermute | solution.py:367
  55.1 13.5 %collective-permute-start = (bf16[16,128,128]{2,1,0:T(8,128)(2,1)S(1)}, bf16[16,128,128]{2,1,0:T(8,128)(2,1)S(1)}, u32[]{:S(2)}, u32[]{:S(2)}) collective-permute-start(bf16[16,128,128]{2,1,0:T(8,128)(2,1)S(1)} %all-gather.1.own_ref), channel_id=1, source_target_pairs={{0,1},{1,0},{2,3},{3,2},{4,5},{5,4},{6,7},{7,6},{8,9},{9,8},{10,11... | collective-permute-start | bytes 1572872 | tf_op jit(solution)/shard_map/ppermute | solution.py:332
  58.7 21.6 %collective-permute-start.2 = (bf16[4,256,128]{2,1,0:T(8,128)(2,1)}, bf16[4,256,128]{2,1,0:T(8,128)(2,1)S(1)}, u32[]{:S(2)}, u32[]{:S(2)}) collective-permute-start(bf16[4,256,128]{2,1,0:T(8,128)(2,1)} %get-tuple-element.22), channel_id=1, source_target_pairs={{0,8},{1,9},{2,10},{3,11},{4,12},{5,13},{6,14},{7,15},{8,16},{9,17... | collective-permute-start | bytes 786440 | tf_op jit(solution)/shard_map/ppermute | solution.py:376
  62.0 18.4 %collective-permute-start.3 = (bf16[4,256,128]{2,1,0:T(8,128)(2,1)}, bf16[4,256,128]{2,1,0:T(8,128)(2,1)S(1)}, u32[]{:S(2)}, u32[]{:S(2)}) collective-permute-start(bf16[4,256,128]{2,1,0:T(8,128)(2,1)} %get-tuple-element.23), channel_id=1, source_target_pairs={{0,16},{1,17},{2,18},{3,19},{4,20},{5,21},{6,22},{7,23},{8,24},{9,... | collective-permute-start | bytes 786440 | tf_op jit(solution)/shard_map/ppermute | solution.py:376
  66.6 13.8 %collective-permute-start.4 = (bf16[4,256,128]{2,1,0:T(8,128)(2,1)}, bf16[4,256,128]{2,1,0:T(8,128)(2,1)S(1)}, u32[]{:S(2)}, u32[]{:S(2)}) collective-permute-start(bf16[4,256,128]{2,1,0:T(8,128)(2,1)} %get-tuple-element.24), channel_id=1, source_target_pairs={{0,24},{1,25},{2,26},{3,27},{4,28},{5,29},{6,30},{7,31},{8,0},{9,1... | collective-permute-start | bytes 786440 | tf_op jit(solution)/shard_map/ppermute | solution.py:376
  76.0 11.8 %all-to-all-start.2 = ((bf16[8,128,128]{2,1,0:T(8,128)(2,1)}), bf16[8,128,128]{2,1,0:T(8,128)(2,1)S(1)}, u32[]{:S(2)}, u32[]{:S(2)}) async-start(bf16[8,128,128]{2,1,0:T(8,128)(2,1)} %finish.1), calls=%async_computation.2 | async-start | bytes 524288 | tf_op jit(solution)/shard_map/all_to_all | solution.py:387
